TPU v7x, 32 devices: a whole 2x2x4 slice. The times are simulated.
32 devices in a mesh: grp: 2 (over x), idx: 16 (over z, y, core).
Axes of the slice: x: 2, y: 2, z: 4, core: 2. Of those that a mesh axis runs over, the one named last changes fastest.
Arguments:
- amplitudes: bfloat16 [256, 80000], P(('grp', 'idx')), parts along dimension 0, may hold values from -0.109375 to 0.109375
- integrals: bfloat16 [256, 80000], P(('grp', 'idx')), parts along dimension 0, may hold values from -8 to 8
- hole_integrals: bfloat16 [32, 8, 16], P(('grp', 'idx')), parts along dimension 0, may hold values from -24 to 24
- occ_energy: float32 [400], P('grp'), parts along dimension 0, may hold values from -2 to -0.3
- vir_energy: float32 [1600], P('grp'), parts along dimension 0, may hold values from 0.2 to 3
- pair_orbitals: int32 [256, 2], P(('grp', 'idx')), parts along dimension 0, may hold values from 0 to 199
Outputs:
- new_amplitudes: bfloat16 [256, 80000], P(('grp', 'idx')), parts along dimension 0
There are 2 independent parts, one for each index of `grp`. A program takes and returns all parts, laid end to end along the dimension named above; each array names one. Nothing has to cross between parts.
All inputs are finite; a program needn't handle non-finite values.
Results may differ from a plain program's by a relative error of at most 0.0034.
Values may be sent and summed in bfloat16 or wider, within the bound.
No kernel may reach another device: no remote copies, remote signals or barrier semaphores. Data moves between devices by JAX's collectives and lax.ppermute only.
A program may use at most 64 MiB of HBM per device.

v0:
```python
import jax
import jax.numpy as jnp
from jax import lax
from jax.sharding import PartitionSpec as P

IRREPS = 8


def on_device(amplitudes, integrals, hole_integrals, occ_energy, vir_energy, pair_orbitals):
    local_pairs = amplitudes.shape[0]
    moved_amps, moved_ints = (
        lax.all_to_all(amplitudes, "idx", split_axis=1, concat_axis=0, tiled=True),
        lax.all_to_all(integrals, "idx", split_axis=1, concat_axis=0, tiled=True),
    )
    all_pairs = moved_amps.shape[0]
    pair_count = all_pairs // IRREPS
    width = moved_amps.shape[1]
    amp_blocks = moved_amps.reshape(IRREPS, pair_count, width)
    int_blocks = moved_ints.reshape(IRREPS, pair_count, width)
    partial_value = jnp.einsum(
        "sie,ske->isk", amp_blocks, int_blocks, preferred_element_type=jnp.float32
    )
    summed = lax.psum(partial_value, "idx")
    bare_all = lax.all_gather(hole_integrals, "idx", axis=0, tiled=True)
    chi_half = (summed + bare_all.astype(jnp.float32)).astype(jnp.bfloat16)
    ladder = jnp.einsum("isk,ske->sie", chi_half, amp_blocks, preferred_element_type=jnp.float32)
    ladder = ladder.astype(jnp.bfloat16).reshape(all_pairs, width)
    returned = lax.all_to_all(ladder, "idx", split_axis=0, concat_axis=1, tiled=True)
    first_pair = lax.axis_index("idx") * local_pairs
    symmetry = (first_pair + jnp.arange(local_pairs, dtype=jnp.int32)) // pair_count
    sym_ids = jnp.arange(IRREPS, dtype=jnp.int32)
    partner = jnp.bitwise_xor(symmetry[:, None], sym_ids[None, :])
    partner_onehot = (partner[:, :, None] == sym_ids[None, None, :]).astype(jnp.float32)
    vir_blocks = vir_energy.reshape(IRREPS, -1)
    energy_partner = jnp.einsum(
        "pgh,hb->pgb", partner_onehot, vir_blocks, precision=lax.Precision.HIGHEST
    )
    orbital_ids = jnp.arange(occ_energy.shape[0], dtype=jnp.int32)
    occ_onehot = (pair_orbitals[:, :, None] == orbital_ids[None, None, :]).astype(jnp.float32)
    occ_each = jnp.einsum("pjo,o->pj", occ_onehot, occ_energy, precision=lax.Precision.HIGHEST)
    occupied = occ_each[:, 0] + occ_each[:, 1]
    denom = (
        vir_blocks[None, :, :, None] + energy_partner[:, :, None, :] - occupied[:, None, None, None]
    )
    denom = denom.reshape(local_pairs, -1)
    total = integrals.astype(jnp.float32) + returned.astype(jnp.float32)
    return (total / denom).astype(jnp.bfloat16)


def solution(mesh):
    in_specs = (
        P(("grp", "idx"), None),
        P(("grp", "idx"), None),
        P(("grp", "idx"), None, None),
        P("grp"),
        P("grp"),
        P(("grp", "idx"), None),
    )
    out_specs = P(("grp", "idx"), None)
    return jax.shard_map(
        on_device, mesh=mesh, in_specs=in_specs, out_specs=out_specs, check_vma=False
    )
```

profile of v0, /device:TPU:0, one launch (start us, length us, event | category | flops | bytes accessed | tf_op | source)
XLA Modules:
  0.0 196.7 jit_solution(17988393408962210980)
XLA Ops:
  0.0 0.0 copy-start
  0.0 3.2 %reshape.84 = bf16[640000]{0:T(1024)(128)(2,1)S(1)} reshape(bf16[8,80000]{1,0:T(8,128)(2,1)} %param.6) | data formatting | bytes 2560000
  3.2 2.2 %all_to_all.37 = bf16[8,16,5000]{2,1,0:T(8,128)(2,1)S(1)} reshape(bf16[640000]{0:T(1024)(128)(2,1)S(1)} %reshape.84) | data formatting | bytes 2560000 | tf_op jit(solution)/shard_map/all_to_all | solution.py:12
  5.5 1.8 copy.22
  7.3 0.0 copy-start.1
  7.3 7.5 %all-to-all-start.1 = ((bf16[8,16,5000]{2,0,1:T(8,128)(2,1)}), bf16[8,16,5000]{2,0,1:T(8,128)(2,1)S(1)}, u32[]{:S(2)}, u32[]{:S(2)}) async-start(bf16[8,16,5000]{2,0,1:T(8,128)(2,1)} %copy.22), calls=%async_computation.1 | async-start | bytes 2621440 | tf_op jit(solution)/shard_map/all_to_all | solution.py:12
  14.8 0.0 copy-done.1
  14.8 3.0 %reshape.86 = bf16[640000]{0:T(1024)(128)(2,1)} reshape(bf16[8,80000]{1,0:T(8,128)(2,1)S(1)} %copy-done.1) | data formatting | bytes 2560000
  17.8 3.4 %all_to_all.34 = bf16[8,16,5000]{2,1,0:T(8,128)(2,1)S(1)} reshape(bf16[640000]{0:T(1024)(128)(2,1)} %reshape.86) | data formatting | bytes 2560000 | tf_op jit(solution)/shard_map/all_to_all | solution.py:13
  21.2 1.8 copy.21
  23.0 0.0 copy-start.3
  23.0 19.2 %all-to-all-done.1 = bf16[8,16,5000]{2,0,1:T(8,128)(2,1)S(1)} async-done(((bf16[8,16,5000]{2,0,1:T(8,128)(2,1)}), bf16[8,16,5000]{2,0,1:T(8,128)(2,1)S(1)}, u32[]{:S(2)}, u32[]{:S(2)}) %all-to-all-start.1) | async-done | bytes 1280032 | tf_op jit(solution)/shard_map/all_to_all | solution.py:12
  42.2 8.0 %all-to-all-start = ((bf16[8,16,5000]{2,0,1:T(8,128)(2,1)}), bf16[8,16,5000]{2,0,1:T(8,128)(2,1)S(1)}, u32[]{:S(2)}, u32[]{:S(2)}) async-start(bf16[8,16,5000]{2,0,1:T(8,128)(2,1)} %copy.21), calls=%async_computation | async-start | bytes 2621440 | tf_op jit(solution)/shard_map/all_to_all | solution.py:13
  50.2 0.0 copy-done.3
  50.3 37.9 %all_gather.3 = bf16[16,8,16]{2,1,0:T(8,128)(2,1)S(1)} all-gather(bf16[1,8,16]{2,1,0:T(8,128)(2,1)S(1)} %copy-done.3), channel_id=1, replica_groups=mesh['grp'=2,'idx'=16] {'idx'}, dimensions={0}, use_global_device_ids=true | all-gather | bytes 4352 | tf_op jit(solution)/shard_map/all_gather | solution.py:24
  88.1 0.1 copy.23
  88.2 0.0 all-to-all-done
  88.2 0.6 convolution_bitcast_fusion
  88.9 63.3 %psum.7 = f32[16,8,16]{0,2,1:T(8,128)S(1)} all-reduce(f32[16,8,16]{0,2,1:T(8,128)S(1)} %convolution_bitcast_fusion), channel_id=1, replica_groups=mesh['grp'=2,'idx'=16] {'idx'}, use_global_device_ids=true, to_apply=%region_0.0 | all-reduce | flops 2048 | bytes 16384 | tf_op jit(solution)/shard_map/psum | solution.py:23
  152.1 1.6 convolution_convert_fusion
  153.7 0.0 copy-start.2
  153.7 4.7 %all-to-all-start.2 = ((bf16[16,8,5000]{2,1,0:T(8,128)(2,1)}), bf16[16,8,5000]{2,1,0:T(8,128)(2,1)}, u32[]{:S(2)}, u32[]{:S(2)}) async-start(bf16[16,8,5000]{2,1,0:T(8,128)(2,1)} %bitcast.5), calls=%async_computation.2 | async-start | bytes 2621440 | tf_op jit(solution)/shard_map/all_to_all | solution.py:28
  158.4 0.0 copy-done.2
  158.5 0.1 reshape.80
  158.5 0.1 add.57
  158.6 0.1 iota_xor_fusion
  158.7 0.2 fusion
  158.9 0.2 add.63
  159.1 0.0 copy-start.4
  159.1 3.1 %add.64 = f32[8,80000]{1,0:T(8,128)} reshape(f32[8,8,100,100]{3,2,1,0:T(8,128)S(1)} %add.63) | data formatting | bytes 5120000 | tf_op jit(solution)/shard_map/add | solution.py:43
  162.3 0.0 copy-done.4
  162.3 0.1 copy.26
  162.4 0.2 add.58
  162.5 0.4 add.59
  162.9 0.1 iota_compare_fusion.2
  163.0 0.0 copy-done
  163.0 0.1 fusion.2
  163.1 22.7 %all-to-all-done.2 = bf16[16,8,5000]{2,1,0:T(8,128)(2,1)} async-done(((bf16[16,8,5000]{2,1,0:T(8,128)(2,1)}), bf16[16,8,5000]{2,1,0:T(8,128)(2,1)}, u32[]{:S(2)}, u32[]{:S(2)}) %all-to-all-start.2) | async-done | bytes 1280032 | tf_op jit(solution)/shard_map/all_to_all | solution.py:28
  185.8 1.6 convert_bitcast_fusion
  187.4 1.5 copy.25
  188.9 3.2 %reshape.79 = f32[8,80000]{1,0:T(8,128)} reshape(f32[8,16,5000]{2,1,0:T(8,128)S(1)} %copy.25) | data formatting | bytes 5120000 | tf_op jit(solution)/shard_map/convert_element_type | solution.py:46
  192.1 4.6 %divide_convert_fusion = bf16[8,80000]{1,0:T(8,128)(2,1)} fusion(f32[8,80000]{1,0:T(8,128)} %add.64, f32[8,80000]{1,0:T(8,128)} %reshape.79, bf16[8,80000]{1,0:T(8,128)(2,1)} %param.7, f32[8]{0:T(128)S(1)} %add_bitcast_fusion, f32[80000]{0:T(1024)S(1)} %add.59), kind=kLoop, calls=%fused_computation.2 | loop fusion | flops 3840000 | bytes 8000032 | tf_op jit(solution)/shard_map/convert_element_type | solution.py:47
  (2 shorter events, 0.0 us)
Async XLA Ops:
  0.0 163.0 %copy-start = (f32[200]{0:T(256)S(1)}, f32[200]{0:T(256)}, u32[]{:S(2)}) copy-start(f32[200]{0:T(256)} %param.9) | copy-start | bytes 2404
  7.3 7.5 %copy-start.1 = (bf16[8,80000]{1,0:T(8,128)(2,1)S(1)}, bf16[8,80000]{1,0:T(8,128)(2,1)}, u32[]{:S(2)}) copy-start(bf16[8,80000]{1,0:T(8,128)(2,1)} %param.7) | copy-start | bytes 3840004
  7.3 34.9 %all-to-all-start.1 = ((bf16[8,16,5000]{2,0,1:T(8,128)(2,1)}), bf16[8,16,5000]{2,0,1:T(8,128)(2,1)S(1)}, u32[]{:S(2)}, u32[]{:S(2)}) async-start(bf16[8,16,5000]{2,0,1:T(8,128)(2,1)} %copy.22), calls=%async_computation.1 | async-start | bytes 2621440 | tf_op jit(solution)/shard_map/all_to_all | solution.py:12
  23.0 27.2 %copy-start.3 = (bf16[1,8,16]{2,1,0:T(8,128)(2,1)S(1)}, bf16[1,8,16]{2,1,0:T(8,128)(2,1)}, u32[]{:S(2)}) copy-start(bf16[1,8,16]{2,1,0:T(8,128)(2,1)} %param.8) | copy-start | bytes 772
  42.2 46.0 %all-to-all-start = ((bf16[8,16,5000]{2,0,1:T(8,128)(2,1)}), bf16[8,16,5000]{2,0,1:T(8,128)(2,1)S(1)}, u32[]{:S(2)}, u32[]{:S(2)}) async-start(bf16[8,16,5000]{2,0,1:T(8,128)(2,1)} %copy.21), calls=%async_computation | async-start | bytes 2621440 | tf_op jit(solution)/shard_map/all_to_all | solution.py:13
  153.7 4.7 %copy-start.2 = (f32[800]{0:T(1024)S(1)}, f32[800]{0:T(1024)}, u32[]{:S(2)}) copy-start(f32[800]{0:T(1024)} %param.10) | copy-start | bytes 9604
  153.7 32.1 %all-to-all-start.2 = ((bf16[16,8,5000]{2,1,0:T(8,128)(2,1)}), bf16[16,8,5000]{2,1,0:T(8,128)(2,1)}, u32[]{:S(2)}, u32[]{:S(2)}) async-start(bf16[16,8,5000]{2,1,0:T(8,128)(2,1)} %bitcast.5), calls=%async_computation.2 | async-start | bytes 2621440 | tf_op jit(solution)/shard_map/all_to_all | solution.py:28
  159.1 3.2 %copy-start.4 = (s32[8,2]{0,1:T(2,128)S(1)}, s32[8,2]{0,1:T(2,128)}, u32[]{:S(2)}) copy-start(s32[8,2]{0,1:T(2,128)} %param.11) | copy-start | bytes 196
where the time goes:
time: 199 us; the launch traced here: 197 us
  blocking collectives  101 us (51%)
  waiting for transfers between devices  41.9 us (21%)
  local copies, waits for them, and re-layouts  24.4 us (12%)
  starting transfers between devices  20.2 us (10%)
  other arithmetic  6.29 us (3%)
  matrix products  2.58 us (1%)
    psum x1, blocking collectives, on_device(): summed = lax.psum(partial_value, 'idx')  63.3 us
    all_gather x1, blocking collectives, on_device(): bare_all = lax.all_gather(hole_integrals, 'idx', axis=0, tiled=True)  37.9 us
    all_to_all x1, waiting for transfers between devices, on_device(): lax.all_to_all(ladder, 'idx', split_axis=0, concat_axis=1, tiled=True)  22.7 us
    all_to_all x1, waiting for transfers between devices, on_device(): lax.all_to_all(amplitudes, 'idx', split_axis=1, concat_axis=0, tiled=True)  19.2 us
    all_to_all x1, starting transfers between devices, on_device(): lax.all_to_all(integrals, 'idx', split_axis=1, concat_axis=0, tiled=True)  8.01 us
    all_to_all x1, starting transfers between devices, on_device(): lax.all_to_all(amplitudes, 'idx', split_axis=1, concat_axis=0, tiled=True)  7.52 us
    unnamed x13, local copies, waits for them, and re-layouts  6.31 us
    all_to_all x2, local copies, waits for them, and re-layouts, on_device(): lax.all_to_all(integrals, 'idx', split_axis=1, concat_axis=0, tiled=True)  5.23 us
  transfers between devices with their start and end apart: 3, of which 2 were waited for; matrix products, arithmetic and copies ran while one was open for 5% of the time, Pallas kernels for 0%

commit v1 on v0

v1 whole, which is shorter than its diff:
```python
import jax
import jax.numpy as jnp
from jax import lax
from jax.sharding import PartitionSpec as P

IRREPS = 8


def team_exchange(block, team, size):
    return [
        lax.ppermute(block, "idx", [(d, (d // team) * team + (d - step) % team) for d in range(size)])
        for step in range(1, team)
    ]


def reciprocal_denominators(occ_energy, vir_energy, pair_orbitals, symmetry):
    sym_ids = jnp.arange(IRREPS, dtype=jnp.int32)
    vir_blocks = vir_energy.reshape(IRREPS, -1)
    partner = jnp.bitwise_xor(symmetry, sym_ids)
    onehot = (partner[:, None] == sym_ids[None, :]).astype(jnp.float32)
    energy_partner = jnp.einsum("gh,hb->gb", onehot, vir_blocks, precision=lax.Precision.HIGHEST)
    virtual = (vir_blocks[:, :, None] + energy_partner[:, None, :]).reshape(-1)
    orbital_ids = jnp.arange(occ_energy.shape[0], dtype=jnp.int32)
    occ_onehot = pair_orbitals[:, :, None] == orbital_ids[None, None, :]
    occ_each = jnp.sum(jnp.where(occ_onehot, occ_energy[None, None, :], 0.0), axis=-1)
    occupied = occ_each[:, 0] + occ_each[:, 1]
    return 1.0 / (virtual[None, :] - occupied[:, None])


def on_device(amplitudes, integrals, hole_integrals, occ_energy, vir_energy, pair_orbitals, size):
    local_pairs = amplitudes.shape[0]
    pair_count = local_pairs * size // IRREPS
    team = pair_count // local_pairs
    me = lax.axis_index("idx")
    symmetry, rank = me // team, me % team

    amps = [amplitudes] + team_exchange(amplitudes, team, size)
    ints = [integrals] + team_exchange(integrals, team, size)

    bare = jnp.repeat(jnp.swapaxes(hole_integrals, 0, 1), team, axis=0)
    bare = lax.all_to_all(bare, "idx", split_axis=0, concat_axis=0, tiled=True)
    bare = bare.reshape(pair_count, pair_count)
    bare = lax.dynamic_slice_in_dim(bare, rank * local_pairs, local_pairs, axis=0)
    bare = bare.reshape(local_pairs, team, local_pairs).astype(jnp.float32)

    inverse = reciprocal_denominators(occ_energy, vir_energy, pair_orbitals, symmetry)
    ladder = 0.0
    for step in range(team):
        chi = jnp.einsum("ie,ke->ik", amplitudes, ints[step], preferred_element_type=jnp.float32)
        mine = lax.dynamic_index_in_dim(bare, (rank + step) % team, axis=1, keepdims=False)
        chi_half = (mine + chi).astype(jnp.bfloat16)
        ladder += jnp.einsum("ik,ke->ie", chi_half, amps[step], preferred_element_type=jnp.float32)
    total = integrals.astype(jnp.float32) + ladder.astype(jnp.bfloat16).astype(jnp.float32)
    return (total * inverse).astype(jnp.bfloat16)


def solution(mesh):
    size = mesh.shape["idx"]
    in_specs = (
        P(("grp", "idx"), None),
        P(("grp", "idx"), None),
        P(("grp", "idx"), None, None),
        P("grp"),
        P("grp"),
        P(("grp", "idx"), None),
    )
    out_specs = P(("grp", "idx"), None)

    def run(*args):
        return on_device(*args, size)

    return jax.shard_map(run, mesh=mesh, in_specs=in_specs, out_specs=out_specs, check_vma=False)
```

time: 199 us -> 24.2 us (0.12); the launches traced: 197 us -> 24 us
  blocking collectives: 101 us -> 0 us
  waiting for transfers between devices: 41.9 us -> 3.36 us
  local copies, waits for them, and re-layouts: 24.4 us -> 2.61 us
  starting transfers between devices: 20.2 us -> 7.96 us
  matrix products: 2.58 us -> 8.89 us
  other arithmetic: 6.29 us -> 1.06 us
    psum x1 -> x0, blocking collectives: 63.3 us -> none  [on_device(): summed = lax.psum(partial_value, 'idx')]
    all_to_all x3 -> x1, waiting for transfers between devices: 41.9 us -> 3.35 us  [on_device(): bare = lax.all_to_all(bare, 'idx', split_axis=0, concat_axis=0, tiled=True)]
    all_gather x1 -> x0, blocking collectives: 37.9 us -> none  [on_device(): bare_all = lax.all_gather(hole_integrals, 'idx', axis=0, tiled=True)]
    all_to_all x3 -> x1, starting transfers between devices: 20.2 us -> 7.39 us  [on_device(): bare = lax.all_to_all(bare, 'idx', split_axis=0, concat_axis=0, tiled=True)]
    all_to_all x4 -> x0, local copies, waits for them, and re-layouts: 9.26 us -> none  [the longest x2 5.23 us: on_device(): lax.all_to_all(integrals, 'idx', split_axis=1, concat_axis=0, tiled=True)]
    dot_general x4 -> x3, matrix products: 2.58 us -> 8.89 us  [the longest x2 8.71 us: on_device(): jnp.einsum('ik,ke->ie', chi_half, amps[step], preferred_element_type=jnp....]
    unnamed x13 -> x4, local copies, waits for them, and re-layouts: 6.31 us -> 0.01 us
    convert_element_type x2 -> x1, other arithmetic: 6.12 us -> 0.02 us  [on_device(): bare = bare.reshape(local_pairs, team, local_pairs).astype(jnp.float32)]
  transfers between devices with their start and end apart: 3 -> 3, of which waited for: 2 -> 1; matrix products, arithmetic and copies ran while one was open for 5% -> 26% of each run, Pallas kernels for 0% -> 0%
where the time goes in v1:
time: 24.2 us; the launch traced here: 24 us
  matrix products  8.89 us (37%)
  starting transfers between devices  7.96 us (33%)
  waiting for transfers between devices  3.36 us (14%)
  local copies, waits for them, and re-layouts  2.61 us (11%)
  other arithmetic  1.06 us (4%)
    dot_general x2, matrix products, on_device(): jnp.einsum('ik,ke->ie', chi_half, amps[step], preferred_element_type=jnp....  8.71 us
    all_to_all x1, starting transfers between devices, on_device(): bare = lax.all_to_all(bare, 'idx', split_axis=0, concat_axis=0, tiled=True)  7.39 us
    all_to_all x1, waiting for transfers between devices, on_device(): bare = lax.all_to_all(bare, 'idx', split_axis=0, concat_axis=0, tiled=True)  3.35 us
    broadcast_in_dim x2, local copies, waits for them, and re-layouts, on_device(): bare = jnp.repeat(jnp.swapaxes(hole_integrals, 0, 1), team, axis=0)  1.39 us
    add x2, local copies, waits for them, and re-layouts, reciprocal_denominators(): virtual = (vir_blocks[:, :, None] + energy_partner[:, None, :]).reshape(-1)  1.12 us
    reduce_sum x1, other arithmetic, reciprocal_denominators(): jnp.sum(jnp.where(occ_onehot, occ_energy[None, None, :], 0.0), axis=-1)  0.85 us
    ppermute x2, starting transfers between devices, team_exchange(): lax.ppermute(block, 'idx', [(d, d // team * team + (d - step) % team) for...  0.58 us
  transfers between devices with their start and end apart: 3, of which 1 were waited for; matrix products, arithmetic and copies ran while one was open for 26% of the time, Pallas kernels for 0%

profile of v1, /device:TPU:0, one launch (start us, length us, event | category | flops | bytes accessed | tf_op | source)
XLA Modules:
  0.0 24.0 jit_solution(8042396534776845518)
XLA Ops:
  0.0 0.0 copy-start
  0.0 0.8 %broadcast_in_dim.24 = bf16[8,2,16]{2,1,0:T(2,128)(2,1)S(1)} broadcast(bf16[8,16]{1,0:T(8,128)(2,1)} %bitcast.16), dimensions={0,2} | broadcast | bytes 768 | tf_op jit(solution)/shard_map/broadcast_in_dim | solution.py:40
  0.8 0.6 %copy.12 = bf16[16,1,16]{2,1,0:T(2,128)(2,1)} copy(bf16[16,1,16]{2,0,1:T(8,128)(2,1)S(1)} %bitcast.14) | data formatting | bytes 1024 | tf_op jit(solution)/shard_map/broadcast_in_dim | solution.py:40
  1.4 7.4 %all-to-all-start = ((bf16[16,1,16]{2,1,0:T(2,128)(2,1)}), bf16[16,1,16]{2,1,0:T(2,128)(2,1)S(1)}, u32[]{:S(2)}, u32[]{:S(2)}) async-start(bf16[16,1,16]{2,1,0:T(2,128)(2,1)} %copy.12), calls=%async_computation | async-start | bytes 16384 | tf_op jit(solution)/shard_map/all_to_all | solution.py:41
  8.8 0.4 %collective-permute-start.1 = (bf16[8,80000]{1,0:T(8,128)(2,1)}, bf16[8,80000]{1,0:T(8,128)(2,1)}, u32[]{:S(2)}, u32[]{:S(2)}) collective-permute-start(bf16[8,80000]{1,0:T(8,128)(2,1)} %param.6), channel_id=1, source_target_pairs={{0,1},{1,0},{2,3},{3,2},{4,5},{5,4},{6,7},{7,6},{8,9},{9,8},{10,11... | collective-permute-start | bytes 3840008 | tf_op jit(solution)/shard_map/ppermute | solution.py:11
  9.2 0.2 collective-permute-start
  9.4 0.8 %add.73 = f32[8,100]{1,0:T(8,128)S(1)} reshape(f32[800]{0:T(1024)} %param.10) | data formatting | bytes 6400 | tf_op jit(solution)/shard_map/add | solution.py:22
  10.1 0.9 %select_reduce_fusion = f32[8,2]{0,1:T(2,128)S(1)} fusion(f32[200]{0:T(256)} %param.9, s32[8,2]{0,1:T(2,128)} %param.11), kind=kLoop, calls=%fused_computation.12 | loop fusion | flops 9584 | bytes 928 | tf_op jit(solution)/shard_map/reduce_sum | solution.py:25
  11.0 0.2 fusion.8
  11.2 0.2 broadcast_add_fusion
  11.4 0.4 %add.77 = f32[80000]{0:T(1024)S(1)} reshape(f32[8,100,100]{2,1,0:T(8,128)S(1)} %broadcast_add_fusion) | data formatting | bytes 640000 | tf_op jit(solution)/shard_map/add | solution.py:22
  11.8 3.4 %all-to-all-done = bf16[16,1,16]{2,1,0:T(2,128)(2,1)S(1)} async-done(((bf16[16,1,16]{2,1,0:T(2,128)(2,1)}), bf16[16,1,16]{2,1,0:T(2,128)(2,1)S(1)}, u32[]{:S(2)}, u32[]{:S(2)}) %all-to-all-start) | async-done | bytes 544 | tf_op jit(solution)/shard_map/all_to_all | solution.py:41
  15.1 0.1 reshape.35
  15.2 0.0 copy-done
  15.3 0.0 copy-start.1
  15.3 3.8 %fusion.7 = f32[8,80000]{1,0:T(8,128)} fusion(bf16[8,80000]{1,0:T(8,128)(2,1)S(1)} %copy-done, f32[8,8]{1,0:T(8,128)S(1)} %bitcast.13, bf16[8,80000]{1,0:T(8,128)(2,1)} %param.7), kind=kOutput, calls=%fused_computation.10 | convolution fusion | flops 20480128 | bytes 5120256 | tf_op jit(solution)/shard_map/ik,ke->ie/dot_general | solution.py:52
  19.1 0.0 collective-permute-done.1
  19.1 0.0 collective-permute-done
  19.1 0.0 copy-done.1
  19.1 4.9 %fusion.4 = bf16[8,80000]{1,0:T(8,128)(2,1)} fusion(f32[8,80000]{1,0:T(8,128)} %fusion.7, bf16[8,80000]{1,0:T(8,128)(2,1)} %collective-permute-done.1, bf16[8,80000]{1,0:T(8,128)(2,1)S(1)} %copy-done.1, f32[8]{0:T(128)S(1)} %add_bitcast_fusion, f32[80000]{0:T(1024)S(1)} %add.77, f32[8,8]{1,0:T(8,128)S(1)} %bitcast.15, bf16[8,80000]{1,0:T(8,128)(2,1)S(1)} %copy-done, ...), kind=kOutput, calls=%fused_computation.5 | convolution fusion | flops 26240128 | bytes 9280288 | tf_op jit(solution)/shard_map/ik,ke->ie/dot_general | solution.py:52
  (4 shorter events, 0.0 us)
Async XLA Ops:
  0.0 15.2 %copy-start = (bf16[8,80000]{1,0:T(8,128)(2,1)S(1)}, bf16[8,80000]{1,0:T(8,128)(2,1)}, u32[]{:S(2)}) copy-start(bf16[8,80000]{1,0:T(8,128)(2,1)} %param.6) | copy-start | bytes 3840004
  1.4 13.7 %all-to-all-start = ((bf16[16,1,16]{2,1,0:T(2,128)(2,1)}), bf16[16,1,16]{2,1,0:T(2,128)(2,1)S(1)}, u32[]{:S(2)}, u32[]{:S(2)}) async-start(bf16[16,1,16]{2,1,0:T(2,128)(2,1)} %copy.12), calls=%async_computation | async-start | bytes 16384 | tf_op jit(solution)/shard_map/all_to_all | solution.py:41
  8.8 10.3 %collective-permute-start.1 = (bf16[8,80000]{1,0:T(8,128)(2,1)}, bf16[8,80000]{1,0:T(8,128)(2,1)}, u32[]{:S(2)}, u32[]{:S(2)}) collective-permute-start(bf16[8,80000]{1,0:T(8,128)(2,1)} %param.6), channel_id=1, source_target_pairs={{0,1},{1,0},{2,3},{3,2},{4,5},{5,4},{6,7},{7,6},{8,9},{9,8},{10,11... | collective-permute-start | bytes 3840008 | tf_op jit(solution)/shard_map/ppermute | solution.py:11
  9.2 9.9 %collective-permute-start = (bf16[8,80000]{1,0:T(8,128)(2,1)}, bf16[8,80000]{1,0:T(8,128)(2,1)}, u32[]{:S(2)}, u32[]{:S(2)}) collective-permute-start(bf16[8,80000]{1,0:T(8,128)(2,1)} %param.7), channel_id=1, source_target_pairs={{0,1},{1,0},{2,3},{3,2},{4,5},{5,4},{6,7},{7,6},{8,9},{9,8},{10,11... | collective-permute-start | bytes 3840008 | tf_op jit(solution)/shard_map/ppermute | solution.py:11
  15.3 3.9 %copy-start.1 = (bf16[8,80000]{1,0:T(8,128)(2,1)S(1)}, bf16[8,80000]{1,0:T(8,128)(2,1)}, u32[]{:S(2)}) copy-start(bf16[8,80000]{1,0:T(8,128)(2,1)} %param.7) | copy-start | bytes 3840004

commit v2 on v1

v2 whole, which is shorter than its diff:
```python
import functools

import jax
import jax.numpy as jnp
import numpy as np
from jax import lax
from jax.experimental import pallas as pl
from jax.experimental.pallas import tpu as pltpu
from jax.sharding import PartitionSpec as P

IRREPS = 8
CHUNKS = 5
IN_VMEM = pl.BlockSpec(memory_space=pltpu.VMEM)
PARAMS = pltpu.CompilerParams(vmem_limit_bytes=24 * 1024 * 1024)


def chunk_slices(width):
    tiles = width // 128
    edges = [tiles * c // CHUNKS * 128 for c in range(CHUNKS)] + [width]
    return [pl.ds(start, stop - start) for start, stop in zip(edges, edges[1:])]


def chi_kernel(team, amps_ref, *refs):
    ints, chi_ref = refs[:team], refs[team]
    total = jnp.zeros(chi_ref.shape, jnp.float32)
    for cut in chunk_slices(amps_ref.shape[1]):
        columns = jnp.concatenate([ref[:, cut] for ref in ints], axis=0)
        total += lax.dot_general(
            amps_ref[:, cut], columns, (((1,), (1,)), ((), ())), preferred_element_type=jnp.float32
        )
    chi_ref[...] = total


def update_kernel(team, slabs, rows_ref, order_ref, chi_ref, virtual_ref, occupied_ref, ints_ref, *refs):
    bare, amps = refs[:slabs], refs[slabs : slabs + team]
    out_ref, buffer, sems = refs[slabs + team :]
    stack = jnp.concatenate([ref[...] for ref in bare], axis=0)
    pairs, count = chi_ref.shape
    pick = lax.broadcasted_iota(jnp.int32, (pairs, stack.shape[0]), 1) == rows_ref[...]
    mine = jnp.dot(pick.astype(jnp.bfloat16), stack, preferred_element_type=jnp.float32)
    turn = lax.broadcasted_iota(jnp.int32, (count, count), 0) == order_ref[...]
    mine = jnp.dot(mine.astype(jnp.bfloat16), turn.astype(jnp.bfloat16), preferred_element_type=jnp.float32)
    chi_half = (mine + chi_ref[...]).astype(jnp.bfloat16)
    copies = []
    for index, cut in enumerate(chunk_slices(ints_ref.shape[1])):
        block = jnp.concatenate([ref[:, cut] for ref in amps], axis=0)
        ladder = jnp.dot(chi_half, block, preferred_element_type=jnp.float32).astype(jnp.bfloat16)
        total = ints_ref[:, cut].astype(jnp.float32) + ladder.astype(jnp.float32)
        denominator = virtual_ref[:, cut] - occupied_ref[...]
        buffer[:, cut] = (total / denominator).astype(jnp.bfloat16)
        copy = pltpu.make_async_copy(buffer.at[:, cut], out_ref.at[:, cut], sems.at[index])
        copy.start()
        copies.append(copy)
    for copy in copies:
        copy.wait()


def team_exchange(block, team, size):
    return [
        lax.ppermute(block, "idx", [(d, (d // team) * team + (d - step) % team) for d in range(size)])
        for step in range(1, team)
    ]


def exchange_rows_16(hole):
    near, far, both = 6, 4, 2

    def home(d):
        return (d >> 3) == (d & 1)

    hops = (
        [(d, d ^ (near if home(d) else far ^ 9)) for d in range(16)],
        [(d, d ^ (both if home(d) else both ^ 9)) for d in range(16)],
        [(d, d ^ 8) for d in range(16)],
    )
    own = jnp.concatenate([hole, lax.ppermute(hole, "idx", [(d, d ^ 1) for d in range(16)])], axis=0)
    first = lax.ppermute(own, "idx", hops[0])
    second = lax.ppermute(own, "idx", hops[1])
    third = lax.ppermute(jnp.concatenate([own, first], axis=0), "idx", hops[2])

    def held(d):
        return [d, d ^ 1]

    source = [dict((dst, src) for src, dst in hop) for hop in hops]
    table = np.zeros((16, 8), np.int32)
    for d in range(16):
        one, two, three = (hop[d] for hop in source)
        slots = held(d) + held(one) + held(two) + held(three) + held(source[0][three])
        table[d] = [slots.index((d & 1) * 8 + row) for row in range(8)]
    return [own, first, second, third], table


def exchange_rows(hole, team, size):
    rows, _, count = hole.shape
    sent = jnp.repeat(jnp.swapaxes(hole, 0, 1), team, axis=0)
    received = lax.all_to_all(sent, "idx", split_axis=0, concat_axis=0, tiled=True)
    table = np.arange(count, dtype=np.int32).reshape(team, -1)[np.arange(size) % team]
    return [received.reshape(size * rows, 1, count)], table


def virtual_sums(vir_energy, symmetry):
    sym_ids = jnp.arange(IRREPS, dtype=jnp.int32)
    blocks = vir_energy.reshape(IRREPS, -1)
    onehot = (jnp.bitwise_xor(symmetry, sym_ids)[:, None] == sym_ids[None, :]).astype(jnp.float32)
    partner = jnp.einsum("gh,hb->gb", onehot, blocks, precision=lax.Precision.HIGHEST)
    return (blocks[:, :, None] + partner[:, None, :]).reshape(1, -1)


def occupied_sums(occ_energy, pair_orbitals):
    orbital_ids = jnp.arange(occ_energy.shape[0], dtype=jnp.int32)
    onehot = pair_orbitals[:, :, None] == orbital_ids[None, None, :]
    each = jnp.sum(jnp.where(onehot, occ_energy[None, None, :], 0.0), axis=-1)
    return each[:, 0:1] + each[:, 1:2]


def on_device(amplitudes, integrals, hole_integrals, occ_energy, vir_energy, pair_orbitals, size):
    local_pairs, width = amplitudes.shape
    pair_count = hole_integrals.shape[2]
    team = pair_count // local_pairs
    me = lax.axis_index("idx")
    symmetry, rank = me // team, me % team

    if size == 16 and team == 2:
        slabs, table = exchange_rows_16(hole_integrals)
    else:
        slabs, table = exchange_rows(hole_integrals, team, size)
    amps = [amplitudes] + team_exchange(amplitudes, team, size)
    ints = [integrals] + team_exchange(integrals, team, size)

    wide = slabs[0].shape[1]
    slabs = [slab.reshape(-1, pair_count) for slab in slabs]
    rows = lax.dynamic_slice_in_dim(jnp.asarray(table), me, 1, axis=0).reshape(local_pairs, 1)
    if wide > 1:
        rows = rows * wide + symmetry
    order = (jnp.arange(pair_count, dtype=jnp.int32) + rank * local_pairs) % pair_count

    chi = pl.pallas_call(
        functools.partial(chi_kernel, team),
        out_shape=jax.ShapeDtypeStruct((local_pairs, pair_count), jnp.float32),
        in_specs=[IN_VMEM] * (1 + team),
        out_specs=IN_VMEM,
        compiler_params=PARAMS,
        cost_estimate=pl.CostEstimate(
            flops=2 * local_pairs * pair_count * width, bytes_accessed=2 * local_pairs * width * 2, transcendentals=0
        ),
    )(amplitudes, *ints)
    return pl.pallas_call(
        functools.partial(update_kernel, team, len(slabs)),
        out_shape=jax.ShapeDtypeStruct((local_pairs, width), jnp.bfloat16),
        in_specs=[IN_VMEM] * (6 + len(slabs) + team),
        out_specs=pl.BlockSpec(memory_space=pl.ANY),
        scratch_shapes=[
            pltpu.VMEM((local_pairs, width), jnp.bfloat16),
            pltpu.SemaphoreType.DMA((CHUNKS,)),
        ],
        compiler_params=PARAMS,
        cost_estimate=pl.CostEstimate(
            flops=2 * local_pairs * pair_count * width, bytes_accessed=4 * local_pairs * width * 2, transcendentals=0
        ),
    )(
        rows,
        order.reshape(1, pair_count),
        chi,
        virtual_sums(vir_energy, symmetry),
        occupied_sums(occ_energy, pair_orbitals),
        integrals,
        *slabs,
        *amps,
    )


def solution(mesh):
    size = mesh.shape["idx"]
    in_specs = (
        P(("grp", "idx"), None),
        P(("grp", "idx"), None),
        P(("grp", "idx"), None, None),
        P("grp"),
        P("grp"),
        P(("grp", "idx"), None),
    )
    out_specs = P(("grp", "idx"), None)

    def run(*args):
        return on_device(*args, size)

    return jax.shard_map(run, mesh=mesh, in_specs=in_specs, out_specs=out_specs, check_vma=False)
```

time: 24.2 us -> 19.7 us (0.81)
  matrix products: 8.89 us -> 0.18 us
  Pallas kernels: 0 us -> 4.36 us
  waiting for transfers between devices: 3.36 us -> 0.04 us
  starting transfers between devices: 7.96 us -> 9.36 us
  local copies, waits for them, and re-layouts: 2.61 us -> 3.62 us
  other arithmetic: 1.06 us -> 1.76 us
    ppermute x0 -> x4, starting transfers between devices: none -> 8.85 us  [the longest x1 4.23 us: exchange_rows_16(): third = lax.ppermute(jnp.concatenate([own, first], axis=0), 'idx', hops[2])]
    dot_general x3 -> x1, matrix products: 8.89 us -> 0.18 us  [virtual_sums(): jnp.einsum('gh,hb->gb', onehot, blocks, precision=lax.Precision.HIGHEST)]
    all_to_all x1 -> x0, starting transfers between devices: 7.39 us -> none  [on_device(): bare = lax.all_to_all(bare, 'idx', split_axis=0, concat_axis=0, tiled=True)]
    pallas_call x0 -> x2, Pallas kernels: none -> 4.36 us  [the longest x1 3.28 us: on_device(): pl.pallas_call(functools.partial(update_kernel, team, len(slabs)), out_sh...]
    all_to_all x1 -> x0, waiting for transfers between devices: 3.35 us -> none  [on_device(): bare = lax.all_to_all(bare, 'idx', split_axis=0, concat_axis=0, tiled=True)]
    unnamed x4 -> x9, local copies, waits for them, and re-layouts: 0.01 us -> 2.16 us
    broadcast_in_dim x2 -> x0, local copies, waits for them, and re-layouts: 1.39 us -> none  [on_device(): bare = jnp.repeat(jnp.swapaxes(hole_integrals, 0, 1), team, axis=0)]
    add x1 -> x3, other arithmetic: 0.18 us -> 0.88 us  [the longest x1 0.69 us: on_device(): rows = rows * wide + symmetry]
  transfers between devices with their start and end apart: 3 -> 6, of which waited for: 1 -> 0; matrix products, arithmetic and copies ran while one was open for 26% -> 22% of each run, Pallas kernels for 0% -> 6%
where the time goes in v2:
time: 19.7 us; the launch traced here: 19.4 us
  starting transfers between devices  9.36 us (48%)
  Pallas kernels  4.36 us (22%)
  local copies, waits for them, and re-layouts  3.62 us (18%)
  other arithmetic  1.76 us (9%)
    ppermute x1, starting transfers between devices, exchange_rows_16(): third = lax.ppermute(jnp.concatenate([own, first], axis=0), 'idx', hops[2])  4.23 us
    ppermute x1, starting transfers between devices, exchange_rows_16(): first = lax.ppermute(own, 'idx', hops[0])  3.66 us
    pallas_call x1, Pallas kernels, on_device(): pl.pallas_call(functools.partial(update_kernel, team, len(slabs)), out_sh...  3.28 us
    unnamed x9, local copies, waits for them, and re-layouts  2.16 us
    add x2, local copies, waits for them, and re-layouts, virtual_sums(): return (blocks[:, :, None] + partner[:, None, :]).reshape(1, -1)  1.37 us
    pallas_call x1, Pallas kernels, on_device(): pl.pallas_call(functools.partial(chi_kernel, team), out_shape=jax.ShapeDt...  1.09 us
    reduce_sum x1, other arithmetic, occupied_sums(): each = jnp.sum(jnp.where(onehot, occ_energy[None, None, :], 0.0), axis=-1)  0.85 us
    add x1, other arithmetic, on_device(): rows = rows * wide + symmetry  0.69 us
  transfers between devices with their start and end apart: 6, of which 0 were waited for; matrix products, arithmetic and copies ran while one was open for 22% of the time, Pallas kernels for 6%

profile of v2, /device:TPU:0, one launch (start us, length us, event | category | flops | bytes accessed | tf_op | source)
XLA Modules:
  0.0 19.4 jit_solution(16433106060971542425)
XLA Ops:
  0.0 0.0 copy-start.2
  0.0 0.0 copy-start
  0.0 0.5 %collective-permute-start.1 = (bf16[1,8,16]{2,1,0:T(8,128)(2,1)}, bf16[1,8,16]{2,1,0:T(8,128)(2,1)S(1)}, u32[]{:S(2)}, u32[]{:S(2)}) collective-permute-start(bf16[1,8,16]{2,1,0:T(8,128)(2,1)} %param.9), channel_id=1, source_target_pairs={{0,1},{1,0},{2,3},{3,2},{4,5},{5,4},{6,7},{7,6},{8,9},{9,8},{10,11... | collective-permute-start | bytes 776 | tf_op jit(solution)/shard_map/ppermute | solution.py:76
  0.5 0.1 collective-permute-start
  0.5 0.4 %collective-permute-start.5 = (bf16[8,80000]{1,0:T(8,128)(2,1)}, bf16[8,80000]{1,0:T(8,128)(2,1)}, u32[]{:S(2)}, u32[]{:S(2)}) collective-permute-start(bf16[8,80000]{1,0:T(8,128)(2,1)} %refs_4_.1), channel_id=1, source_target_pairs={{0,1},{1,0},{2,3},{3,2},{4,5},{5,4},{6,7},{7,6},{8,9},{9,8},{10,11... | collective-permute-start | bytes 3840008 | tf_op jit(solution)/shard_map/ppermute | solution.py:60
  1.0 0.7 %constant_dynamic-update-slice_fusion.1 = bf16[2,8,16]{2,1,0:T(8,128)(2,1)S(1)} fusion(bf16[1,8,16]{2,1,0:T(8,128)(2,1)} %param.9), kind=kLoop, calls=%fused_computation.5 | loop fusion | bytes 2304
  1.7 0.8 %add.80 = f32[8,100]{1,0:T(8,128)S(1)} reshape(f32[800]{0:T(1024)} %param.11) | data formatting | bytes 6400 | tf_op jit(solution)/shard_map/add | solution.py:106
  2.4 0.9 %select_reduce_fusion = f32[8,2]{0,1:T(2,128)S(1)} fusion(f32[200]{0:T(256)} %param.10, s32[8,2]{0,1:T(2,128)} %param.12), kind=kLoop, calls=%fused_computation.1 | loop fusion | flops 9584 | bytes 928 | tf_op jit(solution)/shard_map/reduce_sum | solution.py:112
  3.3 0.2 fusion
  3.5 0.2 broadcast_add_fusion
  3.7 0.0 collective-permute-done.1
  3.7 3.7 %collective-permute-start.2 = (bf16[2,8,16]{2,1,0:T(8,128)(2,1)S(1)}, bf16[2,8,16]{2,1,0:T(8,128)(2,1)S(1)}, u32[]{:S(2)}, u32[]{:S(2)}) collective-permute-start(bf16[2,8,16]{2,1,0:T(8,128)(2,1)S(1)} %constant_dynamic-update-slice_fusion), channel_id=1, source_target_pairs={{0,6},{1,12},{2,4},{3,14},{4,2},{5,8},{6,0},{7,10},{8,5},{9,15},{1... | collective-permute-start | bytes 1544 | tf_op jit(solution)/shard_map/ppermute | solution.py:77
  7.4 0.7 %add_bitcast_fusion = s32[8,1]{0,1:T(1,128)S(1)} fusion(s32[16,8]{1,0:T(8,128)} %constant.50.clone, s32[]{:T(128)S(6)} %select_n.31, s32[]{:T(128)S(6)} %select_n.32), kind=kLoop, calls=%fused_computation.14 | loop fusion | flops 16 | bytes 72 | tf_op jit(solution)/shard_map/add | solution.py:134
  8.0 0.6 %add.85.virtual_ref = f32[1,80000]{1,0:T(1,128)S(1)} reshape(f32[8,100,100]{2,1,0:T(8,128)S(1)} %broadcast_add_fusion) | data formatting | bytes 640000 | tf_op jit(solution)/shard_map/add | solution.py:106
  8.7 0.1 copy.14.rows_ref
  8.7 0.1 copy.15
  8.8 0.1 copy.16
  8.9 0.5 %collective-permute-start.3 = (bf16[2,8,16]{2,1,0:T(8,128)(2,1)S(1)}, bf16[2,8,16]{2,1,0:T(8,128)(2,1)S(1)}, u32[]{:S(2)}, u32[]{:S(2)}) collective-permute-start(bf16[2,8,16]{2,1,0:T(8,128)(2,1)S(1)} %constant_dynamic-update-slice_fusion), channel_id=1, source_target_pairs={{0,2},{1,10},{2,0},{3,8},{4,6},{5,14},{6,4},{7,12},{8,3},{9,11},{1... | collective-permute-start | bytes 1544 | tf_op jit(solution)/shard_map/ppermute | solution.py:78
  9.4 0.0 collective-permute-done.2
  9.4 0.0 copy-done.2
  9.4 4.2 %collective-permute-start.4 = (bf16[4,8,16]{2,1,0:T(8,128)(2,1)S(1)}, bf16[4,8,16]{2,1,0:T(8,128)(2,1)S(1)}, u32[]{:S(2)}, u32[]{:S(2)}) collective-permute-start(bf16[4,8,16]{2,1,0:T(8,128)(2,1)S(1)} %pad_maximum_fusion), channel_id=1, source_target_pairs={{0,8},{1,9},{2,10},{3,11},{4,12},{5,13},{6,14},{7,15},{8,0},{9,1},... | collective-permute-start | bytes 3080 | tf_op jit(solution)/shard_map/ppermute | solution.py:79
  13.7 0.0 collective-permute-done.refs_1_
  13.7 0.0 copy-done
  13.7 0.0 copy-start.1
  13.7 1.3 %copy-done.1 = bf16[8,80000]{1,0:T(8,128)(2,1)S(1)} copy-done((bf16[8,80000]{1,0:T(8,128)(2,1)S(1)}, bf16[8,80000]{1,0:T(8,128)(2,1)}, u32[]{:S(2)}) %copy-start.1) | copy-done | bytes 1280024
  15.0 1.1 %shard_map.73.chi_ref = f32[8,16]{1,0:T(8,128)S(1)} custom-call(bf16[8,80000]{1,0:T(8,128)(2,1)S(1)} %copy-done, bf16[8,80000]{1,0:T(8,128)(2,1)S(1)} %copy-done.1, bf16[8,80000]{1,0:T(8,128)(2,1)S(1)} %collective-permute-done.refs_1_), custom_call_target="tpu_custom_call" | custom-call | flops 20480000 | bytes 2560000 | tf_op jit(solution)/shard_map/pallas_call | solution.py:137
  16.1 0.0 collective-permute-done.3
  16.1 0.0 collective-permute-done.4
  16.1 0.0 collective-permute-done.5.refs_5_
  16.1 3.3 %shard_map.74 = bf16[8,80000]{1,0:T(8,128)(2,1)} custom-call(s32[8,1]{1,0:T(8,128)S(1)} %copy.14.rows_ref, s32[1,16]{1,0:T(1,128)S(1)} %and_select_fusion.order_ref, f32[8,16]{1,0:T(8,128)S(1)} %shard_map.73.chi_ref, f32[1,80000]{1,0:T(1,128)S(1)} %add.85.virtual_ref, f32[8,1]{1,0:T(8,128)S(1)} %add.86.occupied_ref, bf16[8,80000]{1,0:T(8,128)(2,1)S(1)} %copy-done.1, ...), custom_call_target="tpu_custom_call" | custom-call | flops 20480000 | bytes 5120000 | tf_op jit(solution)/shard_map/pallas_call | solution.py:147
  (6 shorter events, 0.0 us)
Async XLA Ops:
  0.0 9.4 %copy-start.2 = (bf16[1,8,16]{2,1,0:T(8,128)(2,1)S(1)}, bf16[1,8,16]{2,1,0:T(8,128)(2,1)}, u32[]{:S(2)}) copy-start(bf16[1,8,16]{2,1,0:T(8,128)(2,1)} %param.9) | copy-start | bytes 772
  0.0 13.7 %copy-start = (bf16[8,80000]{1,0:T(8,128)(2,1)S(1)}, bf16[8,80000]{1,0:T(8,128)(2,1)}, u32[]{:S(2)}) copy-start(bf16[8,80000]{1,0:T(8,128)(2,1)} %refs_4_.1) | copy-start | bytes 3840004
  0.0 3.7 %collective-permute-start.1 = (bf16[1,8,16]{2,1,0:T(8,128)(2,1)}, bf16[1,8,16]{2,1,0:T(8,128)(2,1)S(1)}, u32[]{:S(2)}, u32[]{:S(2)}) collective-permute-start(bf16[1,8,16]{2,1,0:T(8,128)(2,1)} %param.9), channel_id=1, source_target_pairs={{0,1},{1,0},{2,3},{3,2},{4,5},{5,4},{6,7},{7,6},{8,9},{9,8},{10,11... | collective-permute-start | bytes 776 | tf_op jit(solution)/shard_map/ppermute | solution.py:76
  0.5 13.2 %collective-permute-start = (bf16[8,80000]{1,0:T(8,128)(2,1)}, bf16[8,80000]{1,0:T(8,128)(2,1)S(1)}, u32[]{:S(2)}, u32[]{:S(2)}) collective-permute-start(bf16[8,80000]{1,0:T(8,128)(2,1)} %ints_ref.1), channel_id=1, source_target_pairs={{0,1},{1,0},{2,3},{3,2},{4,5},{5,4},{6,7},{7,6},{8,9},{9,8},{10,11... | collective-permute-start | bytes 3840008 | tf_op jit(solution)/shard_map/ppermute | solution.py:60
  0.5 15.6 %collective-permute-start.5 = (bf16[8,80000]{1,0:T(8,128)(2,1)}, bf16[8,80000]{1,0:T(8,128)(2,1)}, u32[]{:S(2)}, u32[]{:S(2)}) collective-permute-start(bf16[8,80000]{1,0:T(8,128)(2,1)} %refs_4_.1), channel_id=1, source_target_pairs={{0,1},{1,0},{2,3},{3,2},{4,5},{5,4},{6,7},{7,6},{8,9},{9,8},{10,11... | collective-permute-start | bytes 3840008 | tf_op jit(solution)/shard_map/ppermute | solution.py:60
  3.7 5.7 %collective-permute-start.2 = (bf16[2,8,16]{2,1,0:T(8,128)(2,1)S(1)}, bf16[2,8,16]{2,1,0:T(8,128)(2,1)S(1)}, u32[]{:S(2)}, u32[]{:S(2)}) collective-permute-start(bf16[2,8,16]{2,1,0:T(8,128)(2,1)S(1)} %constant_dynamic-update-slice_fusion), channel_id=1, source_target_pairs={{0,6},{1,12},{2,4},{3,14},{4,2},{5,8},{6,0},{7,10},{8,5},{9,15},{1... | collective-permute-start | bytes 1544 | tf_op jit(solution)/shard_map/ppermute | solution.py:77
  8.9 7.2 %collective-permute-start.3 = (bf16[2,8,16]{2,1,0:T(8,128)(2,1)S(1)}, bf16[2,8,16]{2,1,0:T(8,128)(2,1)S(1)}, u32[]{:S(2)}, u32[]{:S(2)}) collective-permute-start(bf16[2,8,16]{2,1,0:T(8,128)(2,1)S(1)} %constant_dynamic-update-slice_fusion), channel_id=1, source_target_pairs={{0,2},{1,10},{2,0},{3,8},{4,6},{5,14},{6,4},{7,12},{8,3},{9,11},{1... | collective-permute-start | bytes 1544 | tf_op jit(solution)/shard_map/ppermute | solution.py:78
  9.4 6.7 %collective-permute-start.4 = (bf16[4,8,16]{2,1,0:T(8,128)(2,1)S(1)}, bf16[4,8,16]{2,1,0:T(8,128)(2,1)S(1)}, u32[]{:S(2)}, u32[]{:S(2)}) collective-permute-start(bf16[4,8,16]{2,1,0:T(8,128)(2,1)S(1)} %pad_maximum_fusion), channel_id=1, source_target_pairs={{0,8},{1,9},{2,10},{3,11},{4,12},{5,13},{6,14},{7,15},{8,0},{9,1},... | collective-permute-start | bytes 3080 | tf_op jit(solution)/shard_map/ppermute | solution.py:79
  13.7 1.3 %copy-start.1 = (bf16[8,80000]{1,0:T(8,128)(2,1)S(1)}, bf16[8,80000]{1,0:T(8,128)(2,1)}, u32[]{:S(2)}) copy-start(bf16[8,80000]{1,0:T(8,128)(2,1)} %ints_ref.1) | copy-start | bytes 3840004

commit v3 on v1

v3 whole, which is shorter than its diff:
```python
import functools
import math

import jax
import jax.numpy as jnp
from jax import lax
from jax.experimental import pallas as pl
from jax.experimental.pallas import tpu as pltpu
from jax.sharding import PartitionSpec as P

IRREPS = 8
CHUNKS = 5
IN_VMEM = pl.BlockSpec(memory_space=pltpu.VMEM)


def cuts(width, period):
    count = width // period
    edges = [count * c // CHUNKS for c in range(CHUNKS + 1)]
    return [(edge, stop) for edge, stop in zip(edges, edges[1:]) if stop > edge]


def one_hot_sum(values, columns):
    lanes = lax.broadcasted_iota(jnp.int32, (columns.shape[0], values.shape[1]), 1)
    return jnp.sum(jnp.where(lanes == columns, values, 0.0), axis=1, keepdims=True)


def occupied_sums(occ, orbitals):
    pairs = orbitals.shape[1]
    diagonal = lax.broadcasted_iota(jnp.int32, (pairs, pairs), 0) == lax.broadcasted_iota(
        jnp.int32, (pairs, pairs), 1
    )
    each = [
        one_hot_sum(occ, jnp.sum(jnp.where(diagonal, orbitals[j : j + 1, :], 0), axis=1, keepdims=True))
        for j in range(2)
    ]
    return jnp.broadcast_to(each[0] + each[1], (pairs, 128))


def virtual_sums(vir, symmetry, rows, period):
    block = vir.shape[1] // IRREPS
    step = period // block
    padded = jnp.concatenate([vir, jnp.zeros((1, 128), jnp.float32)], axis=1)
    held = -(-rows // 8) * 8
    row = lax.broadcasted_iota(jnp.int32, (held, 128), 0)
    lane = lax.broadcasted_iota(jnp.int32, (held, 128), 1)

    def irrep_of(orbital):
        return sum((orbital >= block * q).astype(jnp.int32) for q in range(1, IRREPS))

    def partner(orbital):
        other = jnp.bitwise_xor(irrep_of(orbital), symmetry)
        energies = jnp.zeros((held, 128), jnp.float32)
        for q in range(IRREPS):
            energies = jnp.where(other == q, padded[:, block * q : block * q + 128], energies)
        return energies

    firsts = [padded[:, step * r : step * r + 128] for r in range(rows)]
    first = jnp.concatenate(firsts + [jnp.zeros((held - rows, 128), jnp.float32)], axis=0)
    low, high = partner(row * step), partner(row * step + step - 1)
    turn = (irrep_of(row * step) + 1) * block
    sums = []
    for tile in range(period // 128):
        start = tile * 128 // block
        element = lane + tile * 128
        a = start + sum((element >= block * (start + q)).astype(jnp.int32) for q in range(1, 2 + 127 // block))
        b = element - a * block
        second = jnp.where(
            row * step + a >= turn, jnp.take_along_axis(high, b, axis=1), jnp.take_along_axis(low, b, axis=1)
        )
        sums.append(jnp.take_along_axis(first, a, axis=1) + second)
    return jnp.concatenate(sums, axis=1)


def chi_kernel(team, rows, vir_ref, occ_ref, orbitals_ref, amps_ref, *refs):
    ints, (chi_ref, virtual_ref, occupied_ref) = refs[:team], refs[team:]
    symmetry = lax.axis_index("idx") // team
    period = virtual_ref.shape[1]
    total = jnp.zeros(chi_ref.shape, jnp.float32)
    for start, stop in cuts(amps_ref.shape[1], period):
        cut = pl.ds(start * period, (stop - start) * period)
        columns = jnp.concatenate([ref[:, cut] for ref in ints], axis=0)
        total += lax.dot_general(
            amps_ref[:, cut], columns, (((1,), (1,)), ((), ())), preferred_element_type=jnp.float32
        )
    chi_ref[...] = total
    virtual_ref[...] = virtual_sums(vir_ref[...], symmetry, rows, period)
    occupied_ref[...] = occupied_sums(occ_ref[...], orbitals_ref[...])


def update_kernel(team, slabs, owners, chi_ref, virtual_ref, occupied_ref, ints_ref, *refs):
    bare, amps = refs[:slabs], refs[slabs : slabs + team]
    out_ref, buffer, sems = refs[slabs + team :]
    me = lax.axis_index("idx")
    symmetry, rank = me // team, me % team
    pairs, count = chi_ref.shape
    stack = jnp.concatenate([ref[...] for ref in bare], axis=0)
    held = owners(me)
    lane = lax.broadcasted_iota(jnp.int32, (pairs, stack.shape[0]), 1)
    if held is None:
        owner = lane
    else:
        wide = stack.shape[0] // len(held)
        owner = jnp.full(lane.shape, -1, jnp.int32)
        for slot, row in enumerate(held):
            owner = jnp.where(lane == slot * wide + symmetry, row, owner)
    pick = owner == rank * pairs + lax.broadcasted_iota(jnp.int32, lane.shape, 0)
    mine = jnp.dot(pick.astype(jnp.bfloat16), stack, preferred_element_type=jnp.float32)
    column = lax.broadcasted_iota(jnp.int32, (count, count), 1) + rank * pairs
    turn = lax.broadcasted_iota(jnp.int32, (count, count), 0) == jnp.where(column >= count, column - count, column)
    mine = jnp.dot(mine.astype(jnp.bfloat16), turn.astype(jnp.bfloat16), preferred_element_type=jnp.float32)
    chi_half = (mine + chi_ref[...]).astype(jnp.bfloat16)
    occupied = occupied_ref[:, 0:1]
    period = virtual_ref.shape[1]
    copies = []
    for index, (start, stop) in enumerate(cuts(ints_ref.shape[1], period)):
        for row in range(start, stop):
            cut = pl.ds(row * period, period)
            block = jnp.concatenate([ref[:, cut] for ref in amps], axis=0)
            ladder = jnp.dot(chi_half, block, preferred_element_type=jnp.float32).astype(jnp.bfloat16)
            total = ints_ref[:, cut].astype(jnp.float32) + ladder.astype(jnp.float32)
            buffer[:, cut] = (total / (virtual_ref[row : row + 1, :] - occupied)).astype(jnp.bfloat16)
        cut = pl.ds(start * period, (stop - start) * period)
        copy = pltpu.make_async_copy(buffer.at[:, cut], out_ref.at[:, cut], sems.at[index])
        copy.start()
        copies.append(copy)
    for copy in copies:
        copy.wait()


def team_exchange(block, team, size):
    return [
        lax.ppermute(block, "idx", [(d, (d // team) * team + (d - step) % team) for d in range(size)])
        for step in range(1, team)
    ]


def exchange_rows_16(hole):
    near, far, both = 6, 4, 2

    def by_home(d, home, away):
        at_home = (d >> 3) == (d & 1)
        if isinstance(d, int):
            return d ^ (home if at_home else away)
        return d ^ jnp.where(at_home, home, away)

    def hop_one(d):
        return by_home(d, near, far ^ 9)

    def hop_two(d):
        return by_home(d, both, both ^ 9)

    def hop_three(d):
        return d ^ 8

    def permute(block, hop):
        return lax.ppermute(block, "idx", [(d, hop(d)) for d in range(16)])

    def owners(me):
        third = hop_three(me)
        pairs = (me, hop_one(me), hop_two(me), third, hop_one(third))
        return [row for d in pairs for row in (d, d ^ 1)]

    own = jnp.concatenate([hole, permute(hole, lambda d: d ^ 1)], axis=0)
    first, second = permute(own, hop_one), permute(own, hop_two)
    forward = jnp.concatenate([own, first], axis=0)
    return [own, first, second, permute(forward, hop_three)], owners, forward


def exchange_rows(hole, team):
    sent = jnp.repeat(jnp.swapaxes(hole, 0, 1), team, axis=0)
    received = lax.all_to_all(sent, "idx", split_axis=0, concat_axis=0, tiled=True)
    return [received], lambda me: None, received


def after(block, other):
    return lax.optimization_barrier((block, other))[0]


def on_device(amplitudes, integrals, hole_integrals, occ_energy, vir_energy, pair_orbitals, size):
    local_pairs, width = amplitudes.shape
    pair_count = hole_integrals.shape[2]
    team = pair_count // local_pairs
    block = vir_energy.shape[0] // IRREPS
    period = math.lcm(block, 128)
    rows = width // period

    if size == 16 and team == 2:
        slabs, owners, last_sent = exchange_rows_16(hole_integrals)
    else:
        slabs, owners, last_sent = exchange_rows(hole_integrals, team)
    amps = [amplitudes] + team_exchange(amplitudes, team, size)
    ints = [integrals] + [after(other, last_sent) for other in team_exchange(integrals, team, size)]
    slabs = [slab.reshape(-1, pair_count) for slab in slabs]

    def near(array):
        return pltpu.with_memory_space_constraint(array, pltpu.VMEM) if team == 2 else array

    params = pltpu.CompilerParams(vmem_limit_bytes=(16 if team == 2 else 40) * 1024 * 1024)
    cost = functools.partial(pl.CostEstimate, flops=2 * local_pairs * pair_count * width, transcendentals=0)
    chi, virtual, occupied = pl.pallas_call(
        functools.partial(chi_kernel, team, rows),
        out_shape=[
            jax.ShapeDtypeStruct((local_pairs, pair_count), jnp.float32),
            jax.ShapeDtypeStruct((-(-rows // 8) * 8, period), jnp.float32),
            jax.ShapeDtypeStruct((local_pairs, 128), jnp.float32),
        ],
        in_specs=[IN_VMEM] * (4 + team),
        out_specs=[IN_VMEM] * 3,
        compiler_params=params,
        cost_estimate=cost(bytes_accessed=2 * local_pairs * width * 2),
    )(
        near(vir_energy.reshape(1, -1)),
        near(occ_energy.reshape(1, -1)),
        near(pair_orbitals.T),
        near(amplitudes),
        *[near(other) for other in ints],
    )
    return pl.pallas_call(
        functools.partial(update_kernel, team, len(slabs), owners),
        out_shape=jax.ShapeDtypeStruct((local_pairs, width), jnp.bfloat16),
        in_specs=[IN_VMEM] * (4 + len(slabs) + team),
        out_specs=pl.BlockSpec(memory_space=pl.ANY),
        scratch_shapes=[
            pltpu.VMEM((local_pairs, width), jnp.bfloat16),
            pltpu.SemaphoreType.DMA((CHUNKS,)),
        ],
        compiler_params=params,
        cost_estimate=cost(bytes_accessed=4 * local_pairs * width * 2),
    )(chi, virtual, occupied, near(integrals), *slabs, *[near(other) for other in amps])


def solution(mesh):
    size = mesh.shape["idx"]
    in_specs = (
        P(("grp", "idx"), None),
        P(("grp", "idx"), None),
        P(("grp", "idx"), None, None),
        P("grp"),
        P("grp"),
        P(("grp", "idx"), None),
    )
    out_specs = P(("grp", "idx"), None)

    def run(*args):
        return on_device(*args, size)

    return jax.shard_map(run, mesh=mesh, in_specs=in_specs, out_specs=out_specs, check_vma=False)
```

time: 24.2 us -> 22.4 us (0.926)
  matrix products: 8.89 us -> 0 us
  Pallas kernels: 0 us -> 3.28 us
  local copies, waits for them, and re-layouts: 2.61 us -> 5.75 us
  starting transfers between devices: 7.96 us -> 9.15 us
  other arithmetic: 1.06 us -> 0 us
  waiting for transfers between devices: 3.36 us -> 3.88 us
    dot_general x3 -> x0, matrix products: 8.89 us -> none  [the longest x2 8.71 us: on_device(): jnp.einsum('ik,ke->ie', chi_half, amps[step], preferred_element_type=jnp....]
    ppermute x0 -> x4, starting transfers between devices: none -> 8.64 us  [permute(): return lax.ppermute(block, 'idx', [(d, hop(d)) for d in range(16)])]
    all_to_all x1 -> x0, starting transfers between devices: 7.39 us -> none  [on_device(): bare = lax.all_to_all(bare, 'idx', split_axis=0, concat_axis=0, tiled=True)]
    unnamed x4 -> x13, local copies, waits for them, and re-layouts: 0.01 us -> 5.05 us
    ppermute x0 -> x4, waiting for transfers between devices: none -> 3.87 us  [permute(): return lax.ppermute(block, 'idx', [(d, hop(d)) for d in range(16)])]
    all_to_all x1 -> x0, waiting for transfers between devices: 3.35 us -> none  [on_device(): bare = lax.all_to_all(bare, 'idx', split_axis=0, concat_axis=0, tiled=True)]
    pallas_call x0 -> x2, Pallas kernels: none -> 3.28 us  [the longest x1 2.03 us: on_device(): pl.pallas_call(functools.partial(update_kernel, team, len(slabs), owners)...]
    broadcast_in_dim x2 -> x0, local copies, waits for them, and re-layouts: 1.39 us -> none  [on_device(): bare = jnp.repeat(jnp.swapaxes(hole_integrals, 0, 1), team, axis=0)]
  transfers between devices with their start and end apart: 3 -> 6, of which waited for: 1 -> 2; matrix products, arithmetic and copies ran while one was open for 26% -> 6% of each run, Pallas kernels for 0% -> 6%
where the time goes in v3:
time: 22.4 us; the launch traced here: 22.1 us
  starting transfers between devices  9.15 us (41%)
  local copies, waits for them, and re-layouts  5.75 us (26%)
  waiting for transfers between devices  3.88 us (17%)
  Pallas kernels  3.28 us (15%)
    ppermute x4, starting transfers between devices, permute(): return lax.ppermute(block, 'idx', [(d, hop(d)) for d in range(16)])  8.64 us
    unnamed x13, local copies, waits for them, and re-layouts  5.05 us
    ppermute x4, waiting for transfers between devices, permute(): return lax.ppermute(block, 'idx', [(d, hop(d)) for d in range(16)])  3.87 us
    pallas_call x1, Pallas kernels, on_device(): pl.pallas_call(functools.partial(update_kernel, team, len(slabs), owners)...  2.03 us
    pallas_call x1, Pallas kernels, on_device(): pl.pallas_call(functools.partial(chi_kernel, team, rows), out_shape=[jax....  1.25 us
    reshape x1, local copies, waits for them, and re-layouts, on_device(): vir_energy.reshape(1, -1)  0.69 us
    ppermute x2, starting transfers between devices, team_exchange(): lax.ppermute(block, 'idx', [(d, d // team * team + (d - step) % team) for...  0.51 us
  transfers between devices with their start and end apart: 6, of which 2 were waited for; matrix products, arithmetic and copies ran while one was open for 6% of the time, Pallas kernels for 6%

profile of v3, /device:TPU:0, one launch (start us, length us, event | category | flops | bytes accessed | tf_op | source)
XLA Modules:
  0.0 22.1 jit_solution(12592075684611589215)
XLA Ops:
  0.0 0.5 %collective-permute-start = (bf16[8,80000]{1,0:T(8,128)(2,1)}, bf16[8,80000]{1,0:T(8,128)(2,1)S(1)}, u32[]{:S(2)}, u32[]{:S(2)}) collective-permute-start(bf16[8,80000]{1,0:T(8,128)(2,1)} %ints_ref.1), channel_id=1, source_target_pairs={{0,1},{1,0},{2,3},{3,2},{4,5},{5,4},{6,7},{7,6},{8,9},{9,8},{10,11... | collective-permute-start | bytes 3840008 | tf_op jit(solution)/shard_map/ppermute | solution.py:132
  0.5 0.1 collective-permute-start.5
  0.5 0.5 %collective-permute-start.1 = (bf16[1,8,16]{2,1,0:T(8,128)(2,1)}, bf16[1,8,16]{2,1,0:T(8,128)(2,1)S(1)}, u32[]{:S(2)}, u32[]{:S(2)}) collective-permute-start(bf16[1,8,16]{2,1,0:T(8,128)(2,1)} %param.8), channel_id=1, source_target_pairs={{0,1},{1,0},{2,3},{3,2},{4,5},{5,4},{6,7},{7,6},{8,9},{9,8},{10,11... | collective-permute-start | bytes 776 | tf_op jit(solution)/shard_map/ppermute | solution.py:156
  1.0 0.7 %constant_dynamic-update-slice_fusion.1 = (bf16[2,8,16]{2,1,0:T(8,128)(2,1)S(1)}, bf16[4,8,16]{2,1,0:T(8,128)(2,1)S(1)}) fusion(bf16[1,8,16]{2,1,0:T(8,128)(2,1)} %param.8), kind=kLoop, calls=%fused_computation.1 | loop fusion | bytes 4352
  1.6 3.5 %collective-permute-done.1 = bf16[1,8,16]{2,1,0:T(8,128)(2,1)S(1)} collective-permute-done((bf16[1,8,16]{2,1,0:T(8,128)(2,1)}, bf16[1,8,16]{2,1,0:T(8,128)(2,1)S(1)}, u32[]{:S(2)}, u32[]{:S(2)}) %collective-permute-start.1) | collective-permute-done | bytes 288 | tf_op jit(solution)/shard_map/ppermute | solution.py:156
  5.1 3.9 %collective-permute-start.2 = (bf16[2,8,16]{2,1,0:T(8,128)(2,1)S(1)}, bf16[2,8,16]{2,1,0:T(8,128)(2,1)S(1)}, u32[]{:S(2)}, u32[]{:S(2)}) collective-permute-start(bf16[2,8,16]{2,1,0:T(8,128)(2,1)S(1)} %get-tuple-element.13), channel_id=1, source_target_pairs={{0,6},{1,12},{2,4},{3,14},{4,2},{5,8},{6,0},{7,10},{8,5},{9,15},{1... | collective-permute-start | bytes 1544 | tf_op jit(solution)/shard_map/ppermute | solution.py:156
  9.0 0.7 %reshape.18.vir_ref = f32[1,800]{1,0:T(1,128)S(1)} reshape(f32[800]{0:T(1024)} %param.10) | data formatting | bytes 6400 | tf_op jit(solution)/shard_map/reshape | solution.py:212
  9.7 0.5 %collective-permute-start.3 = (bf16[2,8,16]{2,1,0:T(8,128)(2,1)S(1)}, bf16[2,8,16]{2,1,0:T(8,128)(2,1)S(1)}, u32[]{:S(2)}, u32[]{:S(2)}) collective-permute-start(bf16[2,8,16]{2,1,0:T(8,128)(2,1)S(1)} %get-tuple-element.13), channel_id=1, source_target_pairs={{0,2},{1,10},{2,0},{3,8},{4,6},{5,14},{6,4},{7,12},{8,3},{9,11},{1... | collective-permute-start | bytes 1544 | tf_op jit(solution)/shard_map/ppermute | solution.py:156
  10.2 0.4 %collective-permute-done.2 = bf16[2,8,16]{2,1,0:T(8,128)(2,1)S(1)} collective-permute-done((bf16[2,8,16]{2,1,0:T(8,128)(2,1)S(1)}, bf16[2,8,16]{2,1,0:T(8,128)(2,1)S(1)}, u32[]{:S(2)}, u32[]{:S(2)}) %collective-permute-start.2) | collective-permute-done | bytes 544 | tf_op jit(solution)/shard_map/ppermute | solution.py:156
  10.6 3.8 %collective-permute-start.4 = (bf16[4,8,16]{2,1,0:T(8,128)(2,1)S(1)}, bf16[4,8,16]{2,1,0:T(8,128)(2,1)S(1)}, u32[]{:S(2)}, u32[]{:S(2)}) collective-permute-start(bf16[4,8,16]{2,1,0:T(8,128)(2,1)S(1)} %constant_dynamic-update-slice_fusion.2), channel_id=1, source_target_pairs={{0,8},{1,9},{2,10},{3,11},{4,12},{5,13},{6,14},{7,15},{8,0},{9,1},... | collective-permute-start | bytes 3080 | tf_op jit(solution)/shard_map/ppermute | solution.py:156
  14.4 0.0 collective-permute-done.refs_1_
  14.4 0.0 copy-start
  14.4 1.3 %copy-done = bf16[8,80000]{1,0:T(8,128)(2,1)S(1)} copy-done((bf16[8,80000]{1,0:T(8,128)(2,1)S(1)}, bf16[8,80000]{1,0:T(8,128)(2,1)}, u32[]{:S(2)}) %copy-start) | copy-done | bytes 1280024
  15.7 0.0 copy-start.2
  15.7 1.3 %copy-done.2 = bf16[8,80000]{1,0:T(8,128)(2,1)S(1)} copy-done((bf16[8,80000]{1,0:T(8,128)(2,1)S(1)}, bf16[8,80000]{1,0:T(8,128)(2,1)}, u32[]{:S(2)}) %copy-start.2) | copy-done | bytes 1280024
  17.0 0.0 copy-start.4
  17.0 0.7 %copy-done.4 = f32[200]{0:T(256)S(1)} copy-done((f32[200]{0:T(256)S(1)}, f32[200]{0:T(256)}, u32[]{:S(2)}) %copy-start.4) | copy-done | bytes 824
  17.7 0.0 copy-start.5
  17.7 0.7 %copy-done.5 = s32[8,2]{0,1:T(2,128)S(1)} copy-done((s32[8,2]{0,1:T(2,128)S(1)}, s32[8,2]{0,1:T(2,128)}, u32[]{:S(2)}) %copy-start.5) | copy-done | bytes 88
  18.4 0.0 copy-start.1
  18.4 0.0 copy-start.3
  18.4 1.3 %shard_map.64 = (f32[8,16]{1,0:T(8,128)S(1)}, f32[32,3200]{1,0:T(8,128)S(1)}, f32[8,128]{1,0:T(8,128)S(1)}) custom-call(f32[1,800]{1,0:T(1,128)S(1)} %reshape.18.vir_ref, f32[1,200]{1,0:T(1,128)S(1)} %bitcast.10, s32[2,8]{1,0:T(2,128)S(1)} %bitcast.11, bf16[8,80000]{1,0:T(8,128)(2,1)S(1)} %copy-done, bf16[8,80000]{1,0:T(8,128)(2,1)S(1)} %copy-done.2, ...), custom_call_target="tpu_custom_call" | custom-call | flops 20480000 | bytes 2560000 | tf_op jit(solution)/shard_map/pallas_call | solution.py:200
  19.6 0.0 collective-permute-done.3
  19.6 0.0 collective-permute-done.4
  19.7 0.0 collective-permute-done.5.refs_5_
  19.7 0.0 copy-done.1
  19.7 0.4 %copy-done.3 = bf16[8,80000]{1,0:T(8,128)(2,1)S(1)} copy-done((bf16[8,80000]{1,0:T(8,128)(2,1)S(1)}, bf16[8,80000]{1,0:T(8,128)(2,1)}, u32[]{:S(2)}) %copy-start.3) | copy-done | bytes 1280024
  20.1 2.0 %shard_map.65 = bf16[8,80000]{1,0:T(8,128)(2,1)} custom-call(f32[8,16]{1,0:T(8,128)S(1)} %get-tuple-element.10.chi_ref, f32[32,3200]{1,0:T(8,128)S(1)} %get-tuple-element.11.virtual_ref, f32[8,128]{1,0:T(8,128)S(1)} %get-tuple-element.12.occupied_ref, bf16[8,80000]{1,0:T(8,128)(2,1)S(1)} %copy-done.3, bf16[16,16]{1,0:T(8,128)(2,1)S(1)} %bitcast.7, ...), custom_call_target="tpu_custom_call" | custom-call | flops 20480000 | bytes 5120000 | tf_op jit(solution)/shard_map/pallas_call | solution.py:218
  (2 shorter events, 0.0 us)
Async XLA Ops:
  0.0 14.4 %collective-permute-start = (bf16[8,80000]{1,0:T(8,128)(2,1)}, bf16[8,80000]{1,0:T(8,128)(2,1)S(1)}, u32[]{:S(2)}, u32[]{:S(2)}) collective-permute-start(bf16[8,80000]{1,0:T(8,128)(2,1)} %ints_ref.1), channel_id=1, source_target_pairs={{0,1},{1,0},{2,3},{3,2},{4,5},{5,4},{6,7},{7,6},{8,9},{9,8},{10,11... | collective-permute-start | bytes 3840008 | tf_op jit(solution)/shard_map/ppermute | solution.py:132
  0.5 19.2 %collective-permute-start.5 = (bf16[8,80000]{1,0:T(8,128)(2,1)}, bf16[8,80000]{1,0:T(8,128)(2,1)S(1)}, u32[]{:S(2)}, u32[]{:S(2)}) collective-permute-start(bf16[8,80000]{1,0:T(8,128)(2,1)} %refs_4_.1), channel_id=1, source_target_pairs={{0,1},{1,0},{2,3},{3,2},{4,5},{5,4},{6,7},{7,6},{8,9},{9,8},{10,11... | collective-permute-start | bytes 3840008 | tf_op jit(solution)/shard_map/ppermute | solution.py:132
  0.5 4.6 %collective-permute-start.1 = (bf16[1,8,16]{2,1,0:T(8,128)(2,1)}, bf16[1,8,16]{2,1,0:T(8,128)(2,1)S(1)}, u32[]{:S(2)}, u32[]{:S(2)}) collective-permute-start(bf16[1,8,16]{2,1,0:T(8,128)(2,1)} %param.8), channel_id=1, source_target_pairs={{0,1},{1,0},{2,3},{3,2},{4,5},{5,4},{6,7},{7,6},{8,9},{9,8},{10,11... | collective-permute-start | bytes 776 | tf_op jit(solution)/shard_map/ppermute | solution.py:156
  5.1 5.5 %collective-permute-start.2 = (bf16[2,8,16]{2,1,0:T(8,128)(2,1)S(1)}, bf16[2,8,16]{2,1,0:T(8,128)(2,1)S(1)}, u32[]{:S(2)}, u32[]{:S(2)}) collective-permute-start(bf16[2,8,16]{2,1,0:T(8,128)(2,1)S(1)} %get-tuple-element.13), channel_id=1, source_target_pairs={{0,6},{1,12},{2,4},{3,14},{4,2},{5,8},{6,0},{7,10},{8,5},{9,15},{1... | collective-permute-start | bytes 1544 | tf_op jit(solution)/shard_map/ppermute | solution.py:156
  9.7 9.9 %collective-permute-start.3 = (bf16[2,8,16]{2,1,0:T(8,128)(2,1)S(1)}, bf16[2,8,16]{2,1,0:T(8,128)(2,1)S(1)}, u32[]{:S(2)}, u32[]{:S(2)}) collective-permute-start(bf16[2,8,16]{2,1,0:T(8,128)(2,1)S(1)} %get-tuple-element.13), channel_id=1, source_target_pairs={{0,2},{1,10},{2,0},{3,8},{4,6},{5,14},{6,4},{7,12},{8,3},{9,11},{1... | collective-permute-start | bytes 1544 | tf_op jit(solution)/shard_map/ppermute | solution.py:156
  10.6 9.0 %collective-permute-start.4 = (bf16[4,8,16]{2,1,0:T(8,128)(2,1)S(1)}, bf16[4,8,16]{2,1,0:T(8,128)(2,1)S(1)}, u32[]{:S(2)}, u32[]{:S(2)}) collective-permute-start(bf16[4,8,16]{2,1,0:T(8,128)(2,1)S(1)} %constant_dynamic-update-slice_fusion.2), channel_id=1, source_target_pairs={{0,8},{1,9},{2,10},{3,11},{4,12},{5,13},{6,14},{7,15},{8,0},{9,1},... | collective-permute-start | bytes 3080 | tf_op jit(solution)/shard_map/ppermute | solution.py:156
  14.4 1.3 %copy-start = (bf16[8,80000]{1,0:T(8,128)(2,1)S(1)}, bf16[8,80000]{1,0:T(8,128)(2,1)}, u32[]{:S(2)}) copy-start(bf16[8,80000]{1,0:T(8,128)(2,1)} %refs_4_.1) | copy-start | bytes 3840004
  15.7 1.3 %copy-start.2 = (bf16[8,80000]{1,0:T(8,128)(2,1)S(1)}, bf16[8,80000]{1,0:T(8,128)(2,1)}, u32[]{:S(2)}) copy-start(bf16[8,80000]{1,0:T(8,128)(2,1)} %ints_ref.1) | copy-start | bytes 3840004
  17.0 0.7 %copy-start.4 = (f32[200]{0:T(256)S(1)}, f32[200]{0:T(256)}, u32[]{:S(2)}) copy-start(f32[200]{0:T(256)} %param.9) | copy-start | bytes 2404
  17.7 0.7 %copy-start.5 = (s32[8,2]{0,1:T(2,128)S(1)}, s32[8,2]{0,1:T(2,128)}, u32[]{:S(2)}) copy-start(s32[8,2]{0,1:T(2,128)} %param.11) | copy-start | bytes 196
  18.4 1.3 %copy-start.1 = (bf16[8,80000]{1,0:T(8,128)(2,1)S(1)}, bf16[8,80000]{1,0:T(8,128)(2,1)}, u32[]{:S(2)}) copy-start(bf16[8,80000]{1,0:T(8,128)(2,1)} %refs_4_.1) | copy-start | bytes 3840004
  18.4 1.7 %copy-start.3 = (bf16[8,80000]{1,0:T(8,128)(2,1)S(1)}, bf16[8,80000]{1,0:T(8,128)(2,1)}, u32[]{:S(2)}) copy-start(bf16[8,80000]{1,0:T(8,128)(2,1)} %ints_ref.1) | copy-start | bytes 3840004

commit v4 on v3

--- a/solution.py
+++ b/solution.py
@@ -10,7 +10,9 @@
 
 IRREPS = 8
 CHUNKS = 5
+GROUPS = 5
 IN_VMEM = pl.BlockSpec(memory_space=pltpu.VMEM)
+IN_HBM = pl.BlockSpec(memory_space=pltpu.HBM)
 
 
 def cuts(width, period):
@@ -71,20 +73,45 @@
     return jnp.concatenate(sums, axis=1)
 
 
-def chi_kernel(team, rows, vir_ref, occ_ref, orbitals_ref, amps_ref, *refs):
-    ints, (chi_ref, virtual_ref, occupied_ref) = refs[:team], refs[team:]
+def chi_kernel(team, rows, vir_hbm, occ_hbm, orbitals_hbm, amps_hbm, ints_hbm, *refs):
+    others = refs[: team - 1]
+    chi_ref, virtual_ref, occupied_ref, amps_ref, ints_ref = refs[team - 1 : team + 4]
+    vir_ref, occ_ref, orbitals_ref, sems = refs[team + 4 :]
+    moves = (
+        (vir_hbm, vir_ref),
+        (occ_hbm, occ_ref),
+        (orbitals_hbm, orbitals_ref),
+        (amps_hbm, amps_ref),
+        (ints_hbm, ints_ref),
+    )
+    copies = [pltpu.make_async_copy(*move, sems.at[slot]) for slot, move in enumerate(moves)]
+    for copy in copies:
+        copy.start()
+    for copy in copies[:3]:
+        copy.wait()
     symmetry = lax.axis_index("idx") // team
-    period = virtual_ref.shape[1]
-    total = jnp.zeros(chi_ref.shape, jnp.float32)
-    for start, stop in cuts(amps_ref.shape[1], period):
-        cut = pl.ds(start * period, (stop - start) * period)
-        columns = jnp.concatenate([ref[:, cut] for ref in ints], axis=0)
-        total += lax.dot_general(
-            amps_ref[:, cut], columns, (((1,), (1,)), ((), ())), preferred_element_type=jnp.float32
+    virtual_ref[...] = virtual_sums(vir_ref[...].reshape(1, -1), symmetry, rows, virtual_ref.shape[1])
+    occupied_ref[...] = occupied_sums(occ_ref[...].reshape(1, -1), orbitals_ref[...])
+    for copy in copies[3:]:
+        copy.wait()
+
+    ints = (ints_ref, *others)
+    pairs, width = amps_ref.shape
+    part = width // GROUPS // 128 * 128
+    rest = width - part * GROUPS
+
+    def dot(spans):
+        return lax.dot_general(
+            jnp.concatenate([amps_ref[:, span] for span in spans], axis=0),
+            jnp.concatenate([ref[:, span] for span in spans for ref in ints], axis=0),
+            (((1,), (1,)), ((), ())),
+            preferred_element_type=jnp.float32,
         )
-    chi_ref[...] = total
-    virtual_ref[...] = virtual_sums(vir_ref[...], symmetry, rows, period)
-    occupied_ref[...] = occupied_sums(occ_ref[...], orbitals_ref[...])
+
+    whole = dot([pl.ds(g * part, part) for g in range(GROUPS)])
+    count = chi_ref.shape[1]
+    total = sum(whole[g * pairs : (g + 1) * pairs, g * count : (g + 1) * count] for g in range(GROUPS))
+    chi_ref[...] = total + dot([pl.ds(part * GROUPS, rest)]) if rest else total
 
 
 def update_kernel(team, slabs, owners, chi_ref, virtual_ref, occupied_ref, ints_ref, *refs):
@@ -163,13 +190,13 @@
     own = jnp.concatenate([hole, permute(hole, lambda d: d ^ 1)], axis=0)
     first, second = permute(own, hop_one), permute(own, hop_two)
     forward = jnp.concatenate([own, first], axis=0)
-    return [own, first, second, permute(forward, hop_three)], owners, forward
+    return [own, first, second, permute(forward, hop_three)], owners, own, forward
 
 
 def exchange_rows(hole, team):
     sent = jnp.repeat(jnp.swapaxes(hole, 0, 1), team, axis=0)
     received = lax.all_to_all(sent, "idx", split_axis=0, concat_axis=0, tiled=True)
-    return [received], lambda me: None, received
+    return [received], lambda me: None, hole, received
 
 
 def after(block, other):
@@ -184,49 +211,58 @@
     period = math.lcm(block, 128)
     rows = width // period
 
-    if size == 16 and team == 2:
-        slabs, owners, last_sent = exchange_rows_16(hole_integrals)
-    else:
-        slabs, owners, last_sent = exchange_rows(hole_integrals, team)
-    amps = [amplitudes] + team_exchange(amplitudes, team, size)
-    ints = [integrals] + [after(other, last_sent) for other in team_exchange(integrals, team, size)]
-    slabs = [slab.reshape(-1, pair_count) for slab in slabs]
+    def in_hbm(array):
+        return pltpu.with_memory_space_constraint(array, pltpu.HBM)
 
     def near(array):
         return pltpu.with_memory_space_constraint(array, pltpu.VMEM) if team == 2 else array
 
     params = pltpu.CompilerParams(vmem_limit_bytes=(16 if team == 2 else 40) * 1024 * 1024)
     cost = functools.partial(pl.CostEstimate, flops=2 * local_pairs * pair_count * width, transcendentals=0)
-    chi, virtual, occupied = pl.pallas_call(
+
+    if size == 16 and team == 2:
+        slabs, owners, first_sent, last_sent = exchange_rows_16(hole_integrals)
+    else:
+        slabs, owners, first_sent, last_sent = exchange_rows(hole_integrals, team)
+    other_ints = [after(far, last_sent) for far in team_exchange(after(integrals, first_sent), team, size)]
+    other_amps = team_exchange(after(amplitudes, first_sent), team, size)
+    slabs = [slab.reshape(-1, pair_count) for slab in slabs]
+
+    chi, virtual, occupied, own_amps, own_ints = pl.pallas_call(
         functools.partial(chi_kernel, team, rows),
         out_shape=[
             jax.ShapeDtypeStruct((local_pairs, pair_count), jnp.float32),
             jax.ShapeDtypeStruct((-(-rows // 8) * 8, period), jnp.float32),
             jax.ShapeDtypeStruct((local_pairs, 128), jnp.float32),
+            pltpu.VMEM(amplitudes.shape, amplitudes.dtype),
+            pltpu.VMEM(integrals.shape, integrals.dtype),
         ],
-        in_specs=[IN_VMEM] * (4 + team),
-        out_specs=[IN_VMEM] * 3,
+        in_specs=[IN_HBM] * 5 + [IN_VMEM] * (team - 1),
+        out_specs=[IN_VMEM] * 5,
+        scratch_shapes=[
+            pltpu.VMEM(vir_energy.shape, jnp.float32),
+            pltpu.VMEM(occ_energy.shape, jnp.float32),
+            pltpu.VMEM((2, local_pairs), jnp.int32),
+            pltpu.SemaphoreType.DMA((5,)),
+        ],
         compiler_params=params,
-        cost_estimate=cost(bytes_accessed=2 * local_pairs * width * 2),
+        cost_estimate=cost(bytes_accessed=2 * amplitudes.nbytes),
     )(
-        near(vir_energy.reshape(1, -1)),
-        near(occ_energy.reshape(1, -1)),
-        near(pair_orbitals.T),
-        near(amplitudes),
-        *[near(other) for other in ints],
+        *[in_hbm(array) for array in (vir_energy, occ_energy, pair_orbitals.T, amplitudes, integrals)],
+        *[near(far) for far in other_ints],
     )
     return pl.pallas_call(
         functools.partial(update_kernel, team, len(slabs), owners),
         out_shape=jax.ShapeDtypeStruct((local_pairs, width), jnp.bfloat16),
         in_specs=[IN_VMEM] * (4 + len(slabs) + team),
-        out_specs=pl.BlockSpec(memory_space=pl.ANY),
+        out_specs=IN_HBM,
         scratch_shapes=[
             pltpu.VMEM((local_pairs, width), jnp.bfloat16),
             pltpu.SemaphoreType.DMA((CHUNKS,)),
         ],
         compiler_params=params,
         cost_estimate=cost(bytes_accessed=4 * local_pairs * width * 2),
-    )(chi, virtual, occupied, near(integrals), *slabs, *[near(other) for other in amps])
+    )(chi, virtual, occupied, own_ints, *slabs, own_amps, *[near(far) for far in other_amps])
 
 
 def solution(mesh):

time: 22.4 us -> 15.6 us (0.70)
  local copies, waits for them, and re-layouts: 5.75 us -> 0.7 us
  waiting for transfers between devices: 3.88 us -> 1.44 us
  Pallas kernels: 3.28 us -> 4.84 us
  starting transfers between devices: 9.15 us -> 8.42 us
    unnamed x13 -> x2, local copies, waits for them, and re-layouts: 5.05 us -> 0.69 us
    ppermute x4, waiting for transfers between devices: 3.87 us -> 1.43 us  [permute(): return lax.ppermute(block, 'idx', [(d, hop(d)) for d in range(16)])]
    pallas_call x1, Pallas kernels: 1.25 us -> 2.8 us  [on_device(): pl.pallas_call(functools.partial(chi_kernel, team, rows), out_shape=[jax....]
    ppermute x4, starting transfers between devices: 8.64 us -> 7.91 us  [permute(): return lax.ppermute(block, 'idx', [(d, hop(d)) for d in range(16)])]
    reshape x1 -> x0, local copies, waits for them, and re-layouts: 0.69 us -> none  [on_device(): vir_energy.reshape(1, -1)]
  transfers between devices with their start and end apart: 6 -> 6, of which waited for: 2 -> 2; matrix products, arithmetic and copies ran while one was open for 6% -> 4% of each run, Pallas kernels for 6% -> 18%
where the time goes in v4:
time: 15.6 us; the launch traced here: 15.4 us
  starting transfers between devices  8.42 us (54%)
  Pallas kernels  4.84 us (31%)
  waiting for transfers between devices  1.44 us (9%)
  local copies, waits for them, and re-layouts  0.7 us (4%)
    ppermute x4, starting transfers between devices, permute(): return lax.ppermute(block, 'idx', [(d, hop(d)) for d in range(16)])  7.91 us
    pallas_call x1, Pallas kernels, on_device(): pl.pallas_call(functools.partial(chi_kernel, team, rows), out_shape=[jax....  2.8 us
    pallas_call x1, Pallas kernels, on_device(): pl.pallas_call(functools.partial(update_kernel, team, len(slabs), owners)...  2.04 us
    ppermute x4, waiting for transfers between devices, permute(): return lax.ppermute(block, 'idx', [(d, hop(d)) for d in range(16)])  1.43 us
    unnamed x2, local copies, waits for them, and re-layouts  0.69 us
    ppermute x2, starting transfers between devices, team_exchange(): lax.ppermute(block, 'idx', [(d, d // team * team + (d - step) % team) for...  0.51 us
  transfers between devices with their start and end apart: 6, of which 2 were waited for; matrix products, arithmetic and copies ran while one was open for 4% of the time, Pallas kernels for 18%

profile of v4, /device:TPU:0, one launch (start us, length us, event | category | flops | bytes accessed | tf_op | source)
XLA Modules:
  0.0 15.4 jit_solution(2533826344785177210)
XLA Ops:
  0.0 0.5 %collective-permute-start = (bf16[1,8,16]{2,1,0:T(8,128)(2,1)}, bf16[1,8,16]{2,1,0:T(8,128)(2,1)S(1)}, u32[]{:S(2)}, u32[]{:S(2)}) collective-permute-start(bf16[1,8,16]{2,1,0:T(8,128)(2,1)} %param.8), channel_id=1, source_target_pairs={{0,1},{1,0},{2,3},{3,2},{4,5},{5,4},{6,7},{7,6},{8,9},{9,8},{10,11... | collective-permute-start | bytes 776 | tf_op jit(solution)/shard_map/ppermute | solution.py:183
  0.5 0.7 %constant_dynamic-update-slice_fusion.4 = (bf16[4,8,16]{2,1,0:T(8,128)(2,1)S(1)}, bf16[2,8,16]{2,1,0:T(8,128)(2,1)S(1)}) fusion(bf16[1,8,16]{2,1,0:T(8,128)(2,1)} %param.8), kind=kLoop, calls=%fused_computation.4 | loop fusion | bytes 4352
  1.1 0.3 %collective-permute-done = bf16[1,8,16]{2,1,0:T(8,128)(2,1)S(1)} collective-permute-done((bf16[1,8,16]{2,1,0:T(8,128)(2,1)}, bf16[1,8,16]{2,1,0:T(8,128)(2,1)S(1)}, u32[]{:S(2)}, u32[]{:S(2)}) %collective-permute-start) | collective-permute-done | bytes 288 | tf_op jit(solution)/shard_map/ppermute | solution.py:183
  1.5 0.3 %collective-permute-start.1 = (bf16[8,80000]{1,0:T(8,128)(2,1)}, bf16[8,80000]{1,0:T(8,128)(2,1)S(1)}, u32[]{:S(2)}, u32[]{:S(2)}) collective-permute-start(bf16[8,80000]{1,0:T(8,128)(2,1)} %ints_hbm.1), channel_id=1, source_target_pairs={{0,1},{1,0},{2,3},{3,2},{4,5},{5,4},{6,7},{7,6},{8,9},{9,8},{10,11... | collective-permute-start | bytes 3840008 | tf_op jit(solution)/shard_map/ppermute | solution.py:159
  1.8 0.2 %collective-permute-start.5 = (bf16[8,80000]{1,0:T(8,128)(2,1)}, bf16[8,80000]{1,0:T(8,128)(2,1)S(1)}, u32[]{:S(2)}, u32[]{:S(2)}) collective-permute-start(bf16[8,80000]{1,0:T(8,128)(2,1)} %amps_hbm.1), channel_id=1, source_target_pairs={{0,1},{1,0},{2,3},{3,2},{4,5},{5,4},{6,7},{7,6},{8,9},{9,8},{10,11... | collective-permute-start | bytes 3840008 | tf_op jit(solution)/shard_map/ppermute | solution.py:159
  2.0 3.9 %collective-permute-start.2 = (bf16[2,8,16]{2,1,0:T(8,128)(2,1)S(1)}, bf16[2,8,16]{2,1,0:T(8,128)(2,1)S(1)}, u32[]{:S(2)}, u32[]{:S(2)}) collective-permute-start(bf16[2,8,16]{2,1,0:T(8,128)(2,1)S(1)} %get-tuple-element.22), channel_id=1, source_target_pairs={{0,6},{1,12},{2,4},{3,14},{4,2},{5,8},{6,0},{7,10},{8,5},{9,15},{1... | collective-permute-start | bytes 1544 | tf_op jit(solution)/shard_map/ppermute | solution.py:183
  5.9 0.5 %collective-permute-start.3 = (bf16[2,8,16]{2,1,0:T(8,128)(2,1)S(1)}, bf16[2,8,16]{2,1,0:T(8,128)(2,1)S(1)}, u32[]{:S(2)}, u32[]{:S(2)}) collective-permute-start(bf16[2,8,16]{2,1,0:T(8,128)(2,1)S(1)} %get-tuple-element.22), channel_id=1, source_target_pairs={{0,2},{1,10},{2,0},{3,8},{4,6},{5,14},{6,4},{7,12},{8,3},{9,11},{1... | collective-permute-start | bytes 1544 | tf_op jit(solution)/shard_map/ppermute | solution.py:183
  6.4 1.1 %collective-permute-done.2 = bf16[2,8,16]{2,1,0:T(8,128)(2,1)S(1)} collective-permute-done((bf16[2,8,16]{2,1,0:T(8,128)(2,1)S(1)}, bf16[2,8,16]{2,1,0:T(8,128)(2,1)S(1)}, u32[]{:S(2)}, u32[]{:S(2)}) %collective-permute-start.2) | collective-permute-done | bytes 544 | tf_op jit(solution)/shard_map/ppermute | solution.py:183
  7.5 3.1 %collective-permute-start.4 = (bf16[4,8,16]{2,1,0:T(8,128)(2,1)S(1)}, bf16[4,8,16]{2,1,0:T(8,128)(2,1)S(1)}, u32[]{:S(2)}, u32[]{:S(2)}) collective-permute-start(bf16[4,8,16]{2,1,0:T(8,128)(2,1)S(1)} %constant_dynamic-update-slice_fusion.2), channel_id=1, source_target_pairs={{0,8},{1,9},{2,10},{3,11},{4,12},{5,13},{6,14},{7,15},{8,0},{9,1},... | collective-permute-start | bytes 3080 | tf_op jit(solution)/shard_map/ppermute | solution.py:183
  10.6 0.0 collective-permute-done.1.refs_0_
  10.6 2.8 %shard_map.64 = (f32[8,16]{1,0:T(8,128)S(1)}, f32[32,3200]{1,0:T(8,128)S(1)}, f32[8,128]{1,0:T(8,128)S(1)}, bf16[8,80000]{1,0:T(8,128)(2,1)S(1)}, bf16[8,80000]{1,0:T(8,128)(2,1)S(1)}) custom-call(f32[800]{0:T(1024)} %vir_hbm.1, f32[200]{0:T(256)} %occ_hbm.1, s32[2,8]{1,0:T(2,128)} %bitcast.9, bf16[8,80000]{1,0:T(8,128)(2,1)} %amps_hbm.1, ...), custom_call_target="tpu_custom_call" | custom-call | flops 20480000 | bytes 2560000 | tf_op jit(solution)/shard_map/pallas_call | solution.py:231
  13.4 0.0 collective-permute-done.3
  13.4 0.0 collective-permute-done.4
  13.4 0.0 collective-permute-done.5.refs_5_
  13.4 2.0 %shard_map.65 = bf16[8,80000]{1,0:T(8,128)(2,1)} custom-call(f32[8,16]{1,0:T(8,128)S(1)} %get-tuple-element.15.chi_ref, f32[32,3200]{1,0:T(8,128)S(1)} %get-tuple-element.16.virtual_ref, f32[8,128]{1,0:T(8,128)S(1)} %get-tuple-element.17.occupied_ref, bf16[8,80000]{1,0:T(8,128)(2,1)S(1)} %get-tuple-element.18.ints_ref, bf16[16,16]{1,0:T(8,128)(2,1)S(1)} %bitcast.6, ...), custom_call_target="tpu_custom_call" | custom-call | flops 20480000 | bytes 5120000 | tf_op jit(solution)/shard_map/pallas_call | solution.py:254
  (2 shorter events, 0.0 us)
Async XLA Ops:
  0.0 1.5 %collective-permute-start = (bf16[1,8,16]{2,1,0:T(8,128)(2,1)}, bf16[1,8,16]{2,1,0:T(8,128)(2,1)S(1)}, u32[]{:S(2)}, u32[]{:S(2)}) collective-permute-start(bf16[1,8,16]{2,1,0:T(8,128)(2,1)} %param.8), channel_id=1, source_target_pairs={{0,1},{1,0},{2,3},{3,2},{4,5},{5,4},{6,7},{7,6},{8,9},{9,8},{10,11... | collective-permute-start | bytes 776 | tf_op jit(solution)/shard_map/ppermute | solution.py:183
  1.5 9.1 %collective-permute-start.1 = (bf16[8,80000]{1,0:T(8,128)(2,1)}, bf16[8,80000]{1,0:T(8,128)(2,1)S(1)}, u32[]{:S(2)}, u32[]{:S(2)}) collective-permute-start(bf16[8,80000]{1,0:T(8,128)(2,1)} %ints_hbm.1), channel_id=1, source_target_pairs={{0,1},{1,0},{2,3},{3,2},{4,5},{5,4},{6,7},{7,6},{8,9},{9,8},{10,11... | collective-permute-start | bytes 3840008 | tf_op jit(solution)/shard_map/ppermute | solution.py:159
  1.8 11.6 %collective-permute-start.5 = (bf16[8,80000]{1,0:T(8,128)(2,1)}, bf16[8,80000]{1,0:T(8,128)(2,1)S(1)}, u32[]{:S(2)}, u32[]{:S(2)}) collective-permute-start(bf16[8,80000]{1,0:T(8,128)(2,1)} %amps_hbm.1), channel_id=1, source_target_pairs={{0,1},{1,0},{2,3},{3,2},{4,5},{5,4},{6,7},{7,6},{8,9},{9,8},{10,11... | collective-permute-start | bytes 3840008 | tf_op jit(solution)/shard_map/ppermute | solution.py:159
  2.0 5.4 %collective-permute-start.2 = (bf16[2,8,16]{2,1,0:T(8,128)(2,1)S(1)}, bf16[2,8,16]{2,1,0:T(8,128)(2,1)S(1)}, u32[]{:S(2)}, u32[]{:S(2)}) collective-permute-start(bf16[2,8,16]{2,1,0:T(8,128)(2,1)S(1)} %get-tuple-element.22), channel_id=1, source_target_pairs={{0,6},{1,12},{2,4},{3,14},{4,2},{5,8},{6,0},{7,10},{8,5},{9,15},{1... | collective-permute-start | bytes 1544 | tf_op jit(solution)/shard_map/ppermute | solution.py:183
  5.9 7.5 %collective-permute-start.3 = (bf16[2,8,16]{2,1,0:T(8,128)(2,1)S(1)}, bf16[2,8,16]{2,1,0:T(8,128)(2,1)S(1)}, u32[]{:S(2)}, u32[]{:S(2)}) collective-permute-start(bf16[2,8,16]{2,1,0:T(8,128)(2,1)S(1)} %get-tuple-element.22), channel_id=1, source_target_pairs={{0,2},{1,10},{2,0},{3,8},{4,6},{5,14},{6,4},{7,12},{8,3},{9,11},{1... | collective-permute-start | bytes 1544 | tf_op jit(solution)/shard_map/ppermute | solution.py:183
  7.5 5.9 %collective-permute-start.4 = (bf16[4,8,16]{2,1,0:T(8,128)(2,1)S(1)}, bf16[4,8,16]{2,1,0:T(8,128)(2,1)S(1)}, u32[]{:S(2)}, u32[]{:S(2)}) collective-permute-start(bf16[4,8,16]{2,1,0:T(8,128)(2,1)S(1)} %constant_dynamic-update-slice_fusion.2), channel_id=1, source_target_pairs={{0,8},{1,9},{2,10},{3,11},{4,12},{5,13},{6,14},{7,15},{8,0},{9,1},... | collective-permute-start | bytes 3080 | tf_op jit(solution)/shard_map/ppermute | solution.py:183

commit v5 on v4

v5 whole, which is shorter than its diff:
```python
import functools
import itertools
import math

import jax
import jax.numpy as jnp
from jax import lax
from jax.experimental import pallas as pl
from jax.experimental.pallas import tpu as pltpu
from jax.sharding import PartitionSpec as P

IRREPS = 8
GROUPS = 5
IN_VMEM = pl.BlockSpec(memory_space=pltpu.VMEM)
IN_HBM = pl.BlockSpec(memory_space=pltpu.HBM)


def one_hot_sum(values, columns):
    lanes = lax.broadcasted_iota(jnp.int32, (columns.shape[0], values.shape[1]), 1)
    return jnp.sum(jnp.where(lanes == columns, values, 0.0), axis=1, keepdims=True)


def occupied_sums(occ, orbitals):
    pairs = orbitals.shape[1]
    diagonal = lax.broadcasted_iota(jnp.int32, (pairs, pairs), 0) == lax.broadcasted_iota(
        jnp.int32, (pairs, pairs), 1
    )
    each = [
        one_hot_sum(occ, jnp.sum(jnp.where(diagonal, orbitals[j : j + 1, :], 0), axis=1, keepdims=True))
        for j in range(2)
    ]
    return jnp.broadcast_to(each[0] + each[1], (pairs, 128))


def irrep_tiles(block):
    return [g * block * block // 128 for g in range(IRREPS)] + [-(-IRREPS * block * block // 128)]


def virtual_sums(vir, symmetry, tiles):
    block = vir.shape[1] // IRREPS
    padded = jnp.concatenate([vir, jnp.zeros((1, 128), jnp.float32)], axis=1)
    energies = [padded[:, block * g : block * g + 128] for g in range(IRREPS)]
    first = jnp.concatenate(energies, axis=0)
    row = lax.broadcasted_iota(jnp.int32, (IRREPS, 128), 0)
    lane = lax.broadcasted_iota(jnp.int32, (IRREPS, 128), 1)
    other = jnp.bitwise_xor(row, symmetry)
    second = jnp.zeros((IRREPS, 128), jnp.float32)
    for g in range(IRREPS):
        second = jnp.where(other == g, energies[g], second)
    lead = (row * (block * block)) % 128
    sums = []
    for tile in range(tiles):
        element = jnp.clip(lane + tile * 128 - lead, 0, block * block - 1)
        least = max(0, tile * 128 - 127) // block
        a = least + sum((element >= block * (least + q)).astype(jnp.int32) for q in range(1, 3 + 254 // block))
        b = element - a * block
        sums.append(jnp.take_along_axis(first, a, axis=1) + jnp.take_along_axis(second, b, axis=1))
    starts = irrep_tiles(block)
    ends = jnp.zeros((IRREPS, 128), jnp.float32)
    for g in range(1, IRREPS):
        ends = jnp.where(row == g, sums[starts[g] - starts[g - 1]][g - 1 : g, :], ends)
    sums[0] = jnp.where(lane < lead, ends, sums[0])
    return jnp.concatenate(sums, axis=1)


def load_kernel(team, vir_hbm, occ_hbm, orbitals_hbm, hole_hbm, amps_hbm, ints_hbm, *refs):
    virtual_ref, occupied_ref, hole_ref, tiles_ref, vir_ref, occ_ref, orbitals_ref, sems = refs
    moves = (
        (vir_hbm, vir_ref),
        (occ_hbm, occ_ref),
        (orbitals_hbm, orbitals_ref),
        (hole_hbm, hole_ref),
        (amps_hbm, tiles_ref.at[0]),
        (ints_hbm, tiles_ref.at[1]),
    )
    copies = [pltpu.make_async_copy(*move, sems.at[slot]) for slot, move in enumerate(moves)]
    for copy in copies:
        copy.start()
    for copy in copies[:3]:
        copy.wait()
    symmetry = lax.axis_index("idx") // team
    virtual_ref[...] = virtual_sums(vir_ref[...].reshape(1, -1), symmetry, virtual_ref.shape[1] // 128)
    occupied_ref[...] = occupied_sums(occ_ref[...].reshape(1, -1), orbitals_ref[...])
    for copy in copies[3:]:
        copy.wait()


def folded_dot(left, rights):
    pairs, width = left.shape
    part = width // GROUPS // 128 * 128
    rest = width - part * GROUPS
    count = sum(ref.shape[0] for ref in rights)

    def dot(spans):
        return lax.dot_general(
            jnp.concatenate([left[:, span] for span in spans], axis=0),
            jnp.concatenate([ref[:, span] for span in spans for ref in rights], axis=0),
            (((1,), (1,)), ((), ())),
            preferred_element_type=jnp.float32,
        )

    whole = dot([pl.ds(g * part, part) for g in range(GROUPS)])
    total = sum(whole[g * pairs : (g + 1) * pairs, g * count : (g + 1) * count] for g in range(GROUPS))
    return total + dot([pl.ds(part * GROUPS, rest)]) if rest else total


def chi_kernel(*refs):
    tiles, chi_ref = refs[:-1], refs[-1]
    chi_ref[...] = folded_dot(tiles[0].at[0], [ref.at[1] for ref in tiles])


def update_kernel(team, slabs, owners, chi_ref, virtual_ref, occupied_ref, *refs):
    bare, tiles = refs[:slabs], refs[slabs : slabs + team]
    ints_ref, amps = tiles[0].at[1], [ref.at[0] for ref in tiles]
    out_ref, buffer, sems = refs[slabs + team :]
    me = lax.axis_index("idx")
    symmetry, rank = me // team, me % team
    pairs, count = chi_ref.shape
    stack = jnp.concatenate([ref[...] for ref in bare], axis=0)
    held = owners(me)
    lane = lax.broadcasted_iota(jnp.int32, (pairs, stack.shape[0]), 1)
    if held is None:
        owner = lane
    else:
        wide = stack.shape[0] // len(held)
        owner = jnp.full(lane.shape, -1, jnp.int32)
        for slot, row in enumerate(held):
            owner = jnp.where(lane == slot * wide + symmetry, row, owner)
    pick = owner == rank * pairs + lax.broadcasted_iota(jnp.int32, lane.shape, 0)
    mine = jnp.dot(pick.astype(jnp.bfloat16), stack, preferred_element_type=jnp.float32)
    column = lax.broadcasted_iota(jnp.int32, (count, count), 1) + rank * pairs
    turn = lax.broadcasted_iota(jnp.int32, (count, count), 0) == jnp.where(column >= count, column - count, column)
    mine = jnp.dot(mine.astype(jnp.bfloat16), turn.astype(jnp.bfloat16), preferred_element_type=jnp.float32)
    chi_half = (mine + chi_ref[...]).astype(jnp.bfloat16)
    occupied = occupied_ref[:, 0:1]
    width = ints_ref.shape[1]
    copies = []
    for g, (start, end) in enumerate(itertools.pairwise(irrep_tiles(math.isqrt(width // IRREPS)))):
        cut = pl.ds(start * 128, (end - start) * 128)
        block = jnp.concatenate([ref[:, cut] for ref in amps], axis=0)
        ladder = jnp.dot(chi_half, block, preferred_element_type=jnp.float32).astype(jnp.bfloat16)
        total = ints_ref[:, cut].astype(jnp.float32) + ladder.astype(jnp.float32)
        denominator = virtual_ref[g : g + 1, : (end - start) * 128] - occupied
        buffer[:, cut] = (total / denominator).astype(jnp.bfloat16)
        copy = pltpu.make_async_copy(buffer.at[:, cut], out_ref.at[:, cut], sems.at[g])
        copy.start()
        copies.append(copy)
    for copy in copies:
        copy.wait()


def team_exchange(block, team, size):
    return [
        lax.ppermute(block, "idx", [(d, (d // team) * team + (d - step) % team) for d in range(size)])
        for step in range(1, team)
    ]


def exchange_rows_16(hole, near_hole):
    near, far, both = 6, 4, 2

    def by_home(d, home, away):
        at_home = (d >> 3) == (d & 1)
        if isinstance(d, int):
            return d ^ (home if at_home else away)
        return d ^ jnp.where(at_home, home, away)

    def hop_one(d):
        return by_home(d, near, far ^ 9)

    def hop_two(d):
        return by_home(d, both, both ^ 9)

    def hop_three(d):
        return d ^ 8

    def permute(block, hop):
        return lax.ppermute(block, "idx", [(d, hop(d)) for d in range(16)])

    def owners(me):
        third = hop_three(me)
        pairs = (me, hop_one(me), hop_two(me), third, hop_one(third))
        return [row for d in pairs for row in (d, d ^ 1)]

    own = jnp.concatenate([near_hole, permute(hole, lambda d: d ^ 1)], axis=0)
    first, second = permute(own, hop_one), permute(own, hop_two)
    forward = jnp.concatenate([own, first], axis=0)
    return [own, first, second, permute(forward, hop_three)], owners, own, forward


def exchange_rows(hole, team):
    sent = jnp.repeat(jnp.swapaxes(hole, 0, 1), team, axis=0)
    received = lax.all_to_all(sent, "idx", split_axis=0, concat_axis=0, tiled=True)
    return [received], lambda me: None, hole, received


def after(block, other):
    return lax.optimization_barrier((block, other))[0]


def on_device(amplitudes, integrals, hole_integrals, occ_energy, vir_energy, pair_orbitals, size):
    local_pairs, width = amplitudes.shape
    pair_count = hole_integrals.shape[2]
    team = pair_count // local_pairs
    block = vir_energy.shape[0] // IRREPS
    tiles = max(end - start for start, end in itertools.pairwise(irrep_tiles(block))) + 1

    def in_hbm(array):
        return pltpu.with_memory_space_constraint(array, pltpu.HBM)

    def near(array):
        return pltpu.with_memory_space_constraint(array, pltpu.VMEM) if team == 2 else array

    params = pltpu.CompilerParams(vmem_limit_bytes=(16 if team == 2 else 40) * 1024 * 1024)
    cost = functools.partial(pl.CostEstimate, flops=2 * local_pairs * pair_count * width, transcendentals=0)

    virtual, occupied, near_hole, own = pl.pallas_call(
        functools.partial(load_kernel, team),
        out_shape=[
            jax.ShapeDtypeStruct((IRREPS, tiles * 128), jnp.float32),
            jax.ShapeDtypeStruct((local_pairs, 128), jnp.float32),
            pltpu.VMEM(hole_integrals.shape, hole_integrals.dtype),
            pltpu.VMEM((2, *amplitudes.shape), amplitudes.dtype),
        ],
        in_specs=[IN_HBM] * 6,
        out_specs=[IN_VMEM] * 4,
        scratch_shapes=[
            pltpu.VMEM(vir_energy.shape, jnp.float32),
            pltpu.VMEM(occ_energy.shape, jnp.float32),
            pltpu.VMEM((2, local_pairs), jnp.int32),
            pltpu.SemaphoreType.DMA((6,)),
        ],
        compiler_params=params,
        cost_estimate=pl.CostEstimate(flops=0, bytes_accessed=2 * amplitudes.nbytes, transcendentals=0),
    )(
        *[in_hbm(array) for array in (vir_energy, occ_energy, pair_orbitals.T)],
        *[in_hbm(array) for array in (hole_integrals, amplitudes, integrals)],
    )

    if size == 16 and team == 2:
        slabs, owners, first_sent, last_sent = exchange_rows_16(hole_integrals, near_hole)
    else:
        slabs, owners, first_sent, last_sent = exchange_rows(hole_integrals, team)
    others = [after(far, last_sent) for far in team_exchange(after(own, first_sent), team, size)]
    held = [near(tile) for tile in (own, *others)]
    slabs = [slab.reshape(-1, pair_count) for slab in slabs]

    chi = pl.pallas_call(
        chi_kernel,
        out_shape=jax.ShapeDtypeStruct((local_pairs, pair_count), jnp.float32),
        in_specs=[IN_VMEM] * team,
        out_specs=IN_VMEM,
        compiler_params=params,
        cost_estimate=cost(bytes_accessed=2 * amplitudes.nbytes),
    )(*held)
    return pl.pallas_call(
        functools.partial(update_kernel, team, len(slabs), owners),
        out_shape=jax.ShapeDtypeStruct((local_pairs, width), jnp.bfloat16),
        in_specs=[IN_VMEM] * (3 + len(slabs) + team),
        out_specs=IN_HBM,
        scratch_shapes=[
            pltpu.VMEM((local_pairs, width), jnp.bfloat16),
            pltpu.SemaphoreType.DMA((IRREPS,)),
        ],
        compiler_params=params,
        cost_estimate=cost(bytes_accessed=4 * local_pairs * width * 2),
    )(chi, virtual, occupied, *slabs, *held)


def solution(mesh):
    size = mesh.shape["idx"]
    in_specs = (
        P(("grp", "idx"), None),
        P(("grp", "idx"), None),
        P(("grp", "idx"), None, None),
        P("grp"),
        P("grp"),
        P(("grp", "idx"), None),
    )
    out_specs = P(("grp", "idx"), None)

    def run(*args):
        return on_device(*args, size)

    return jax.shard_map(run, mesh=mesh, in_specs=in_specs, out_specs=out_specs, check_vma=False)
```

time: 15.6 us -> 15 us (0.962)
  local copies, waits for them, and re-layouts: 0.7 us -> 0.02 us
  waiting for transfers between devices: 1.44 us -> 1.75 us
  starting transfers between devices: 8.42 us -> 8.15 us
    unnamed x2, local copies, waits for them, and re-layouts: 0.69 us -> 0.01 us
    ppermute x2 -> x1, starting transfers between devices: 0.51 us -> 0.12 us  [team_exchange(): lax.ppermute(block, 'idx', [(d, d // team * team + (d - step) % team) for...]
    ppermute x4, waiting for transfers between devices: 1.43 us -> 1.74 us  [permute(): return lax.ppermute(block, 'idx', [(d, hop(d)) for d in range(16)])]
    pallas_call x1 -> x2, Pallas kernels: 2.8 us -> 2.79 us  [the longest x1 1.81 us: on_device(): pl.pallas_call(functools.partial(load_kernel, team), out_shape=[jax.Shape...]
  transfers between devices with their start and end apart: 6 -> 5, of which waited for: 2 -> 2; matrix products, arithmetic and copies ran while one was open for 4% -> 0% of each run, Pallas kernels for 18% -> 19%
where the time goes in v5:
time: 15 us; the launch traced here: 14.8 us
  starting transfers between devices  8.15 us (54%)
  Pallas kernels  4.83 us (32%)
  waiting for transfers between devices  1.75 us (12%)
    ppermute x4, starting transfers between devices, permute(): return lax.ppermute(block, 'idx', [(d, hop(d)) for d in range(16)])  8.03 us
    pallas_call x1, Pallas kernels, on_device(): pl.pallas_call(functools.partial(update_kernel, team, len(slabs), owners)...  2.04 us
    pallas_call x1, Pallas kernels, on_device(): pl.pallas_call(functools.partial(load_kernel, team), out_shape=[jax.Shape...  1.81 us
    ppermute x4, waiting for transfers between devices, permute(): return lax.ppermute(block, 'idx', [(d, hop(d)) for d in range(16)])  1.74 us
    pallas_call x1, Pallas kernels, on_device(): pl.pallas_call(chi_kernel, out_shape=jax.ShapeDtypeStruct((local_pairs, p...  0.99 us
  transfers between devices with their start and end apart: 5, of which 2 were waited for; matrix products, arithmetic and copies ran while one was open for 0% of the time, Pallas kernels for 19%

profile of v5, /device:TPU:0, one launch (start us, length us, event | category | flops | bytes accessed | tf_op | source)
XLA Modules:
  0.0 14.8 jit_solution(16914391421667250113)
XLA Ops:
  0.0 0.5 %collective-permute-start = (bf16[1,8,16]{2,1,0:T(8,128)(2,1)}, bf16[1,8,16]{2,1,0:T(8,128)(2,1)S(1)}, u32[]{:S(2)}, u32[]{:S(2)}) collective-permute-start(bf16[1,8,16]{2,1,0:T(8,128)(2,1)} %hole_hbm.1), channel_id=1, source_target_pairs={{0,1},{1,0},{2,3},{3,2},{4,5},{5,4},{6,7},{7,6},{8,9},{9,8},{10,11... | collective-permute-start | bytes 776 | tf_op jit(solution)/shard_map/ppermute | solution.py:178
  0.5 1.8 %shard_map.64 = (f32[8,10240]{1,0:T(8,128)S(1)}, f32[8,128]{1,0:T(8,128)S(1)}, bf16[1,8,16]{2,1,0:T(8,128)(2,1)S(1)}, bf16[2,8,80000]{2,1,0:T(8,128)(2,1)S(1)}) custom-call(f32[800]{0:T(1024)} %vir_hbm.1, f32[200]{0:T(256)} %occ_hbm.1, s32[2,8]{1,0:T(2,128)} %bitcast.9, bf16[1,8,16]{2,1,0:T(8,128)(2,1)} %hole_hbm.1, bf16[8,80000]{1,0:T(8,128)(2,1)} %amps_hbm.1, ...), custom_call_target="tpu_custom_call" | custom-call | bytes 2560000 | tf_op jit(solution)/shard_map/pallas_call | solution.py:217
  2.3 0.0 collective-permute-done
  2.3 0.1 collective-permute-start.1
  2.4 4.0 %collective-permute-start.2 = (bf16[2,8,16]{2,1,0:T(8,128)(2,1)S(1)}, bf16[2,8,16]{2,1,0:T(8,128)(2,1)S(1)}, u32[]{:S(2)}, u32[]{:S(2)}) collective-permute-start(bf16[2,8,16]{2,1,0:T(8,128)(2,1)S(1)} %get-tuple-element.18), channel_id=1, source_target_pairs={{0,6},{1,12},{2,4},{3,14},{4,2},{5,8},{6,0},{7,10},{8,5},{9,15},{1... | collective-permute-start | bytes 1544 | tf_op jit(solution)/shard_map/ppermute | solution.py:178
  6.4 0.5 %collective-permute-start.3 = (bf16[2,8,16]{2,1,0:T(8,128)(2,1)S(1)}, bf16[2,8,16]{2,1,0:T(8,128)(2,1)S(1)}, u32[]{:S(2)}, u32[]{:S(2)}) collective-permute-start(bf16[2,8,16]{2,1,0:T(8,128)(2,1)S(1)} %get-tuple-element.18), channel_id=1, source_target_pairs={{0,2},{1,10},{2,0},{3,8},{4,6},{5,14},{6,4},{7,12},{8,3},{9,11},{1... | collective-permute-start | bytes 1544 | tf_op jit(solution)/shard_map/ppermute | solution.py:178
  6.9 1.1 %collective-permute-done.2 = bf16[2,8,16]{2,1,0:T(8,128)(2,1)S(1)} collective-permute-done((bf16[2,8,16]{2,1,0:T(8,128)(2,1)S(1)}, bf16[2,8,16]{2,1,0:T(8,128)(2,1)S(1)}, u32[]{:S(2)}, u32[]{:S(2)}) %collective-permute-start.2) | collective-permute-done | bytes 544 | tf_op jit(solution)/shard_map/ppermute | solution.py:178
  8.0 3.1 %collective-permute-start.4 = (bf16[4,8,16]{2,1,0:T(8,128)(2,1)S(1)}, bf16[4,8,16]{2,1,0:T(8,128)(2,1)S(1)}, u32[]{:S(2)}, u32[]{:S(2)}) collective-permute-start(bf16[4,8,16]{2,1,0:T(8,128)(2,1)S(1)} %constant_dynamic-update-slice_fusion.2), channel_id=1, source_target_pairs={{0,8},{1,9},{2,10},{3,11},{4,12},{5,13},{6,14},{7,15},{8,0},{9,1},... | collective-permute-start | bytes 3080 | tf_op jit(solution)/shard_map/ppermute | solution.py:178
  11.1 0.0 collective-permute-done.1.refs_1_.refs_5_
  11.1 1.0 %shard_map.65.chi_ref = f32[8,16]{1,0:T(8,128)S(1)} custom-call(bf16[2,8,80000]{2,1,0:T(8,128)(2,1)S(1)} %get-tuple-element.13.refs_0_.refs_4_, bf16[2,8,80000]{2,1,0:T(8,128)(2,1)S(1)} %collective-permute-done.1.refs_1_.refs_5_), custom_call_target="tpu_custom_call" | custom-call | flops 20480000 | bytes 2560000 | tf_op jit(solution)/shard_map/pallas_call | solution.py:248
  12.1 0.0 collective-permute-done.3
  12.1 0.7 %collective-permute-done.4 = bf16[4,8,16]{2,1,0:T(8,128)(2,1)S(1)} collective-permute-done((bf16[4,8,16]{2,1,0:T(8,128)(2,1)S(1)}, bf16[4,8,16]{2,1,0:T(8,128)(2,1)S(1)}, u32[]{:S(2)}, u32[]{:S(2)}) %collective-permute-start.4) | collective-permute-done | bytes 1056 | tf_op jit(solution)/shard_map/ppermute | solution.py:178
  12.7 2.0 %shard_map.66 = bf16[8,80000]{1,0:T(8,128)(2,1)} custom-call(f32[8,16]{1,0:T(8,128)S(1)} %shard_map.65.chi_ref, f32[8,10240]{1,0:T(8,128)S(1)} %get-tuple-element.15.virtual_ref, f32[8,128]{1,0:T(8,128)S(1)} %get-tuple-element.16.occupied_ref, bf16[16,16]{1,0:T(8,128)(2,1)S(1)} %bitcast.6, bf16[16,16]{1,0:T(8,128)(2,1)S(1)} %bitcast.5, ...), custom_call_target="tpu_custom_call" | custom-call | flops 20480000 | bytes 5120000 | tf_op jit(solution)/shard_map/pallas_call | solution.py:256
  (3 shorter events, 0.0 us)
Async XLA Ops:
  0.0 2.3 %collective-permute-start = (bf16[1,8,16]{2,1,0:T(8,128)(2,1)}, bf16[1,8,16]{2,1,0:T(8,128)(2,1)S(1)}, u32[]{:S(2)}, u32[]{:S(2)}) collective-permute-start(bf16[1,8,16]{2,1,0:T(8,128)(2,1)} %hole_hbm.1), channel_id=1, source_target_pairs={{0,1},{1,0},{2,3},{3,2},{4,5},{5,4},{6,7},{7,6},{8,9},{9,8},{10,11... | collective-permute-start | bytes 776 | tf_op jit(solution)/shard_map/ppermute | solution.py:178
  2.3 8.8 %collective-permute-start.1 = (bf16[2,8,80000]{2,1,0:T(8,128)(2,1)S(1)}, bf16[2,8,80000]{2,1,0:T(8,128)(2,1)S(1)}, u32[]{:S(2)}, u32[]{:S(2)}) collective-permute-start(bf16[2,8,80000]{2,1,0:T(8,128)(2,1)S(1)} %get-tuple-element.13.refs_0_.refs_4_), channel_id=1, source_target_pairs={{0,1},{1,0},{2,3},{3,2},{4,5},{5,4},{6,7},{7,6},{8,9},{9,8},{10,11... | collective-permute-start | bytes 7680008 | tf_op jit(solution)/shard_map/ppermute | solution.py:154
  2.4 5.6 %collective-permute-start.2 = (bf16[2,8,16]{2,1,0:T(8,128)(2,1)S(1)}, bf16[2,8,16]{2,1,0:T(8,128)(2,1)S(1)}, u32[]{:S(2)}, u32[]{:S(2)}) collective-permute-start(bf16[2,8,16]{2,1,0:T(8,128)(2,1)S(1)} %get-tuple-element.18), channel_id=1, source_target_pairs={{0,6},{1,12},{2,4},{3,14},{4,2},{5,8},{6,0},{7,10},{8,5},{9,15},{1... | collective-permute-start | bytes 1544 | tf_op jit(solution)/shard_map/ppermute | solution.py:178
  6.4 5.7 %collective-permute-start.3 = (bf16[2,8,16]{2,1,0:T(8,128)(2,1)S(1)}, bf16[2,8,16]{2,1,0:T(8,128)(2,1)S(1)}, u32[]{:S(2)}, u32[]{:S(2)}) collective-permute-start(bf16[2,8,16]{2,1,0:T(8,128)(2,1)S(1)} %get-tuple-element.18), channel_id=1, source_target_pairs={{0,2},{1,10},{2,0},{3,8},{4,6},{5,14},{6,4},{7,12},{8,3},{9,11},{1... | collective-permute-start | bytes 1544 | tf_op jit(solution)/shard_map/ppermute | solution.py:178
  8.0 4.7 %collective-permute-start.4 = (bf16[4,8,16]{2,1,0:T(8,128)(2,1)S(1)}, bf16[4,8,16]{2,1,0:T(8,128)(2,1)S(1)}, u32[]{:S(2)}, u32[]{:S(2)}) collective-permute-start(bf16[4,8,16]{2,1,0:T(8,128)(2,1)S(1)} %constant_dynamic-update-slice_fusion.2), channel_id=1, source_target_pairs={{0,8},{1,9},{2,10},{3,11},{4,12},{5,13},{6,14},{7,15},{8,0},{9,1},... | collective-permute-start | bytes 3080 | tf_op jit(solution)/shard_map/ppermute | solution.py:178

commit v6 on v5

--- a/solution.py
+++ b/solution.py
@@ -104,9 +104,34 @@
     return total + dot([pl.ds(part * GROUPS, rest)]) if rest else total
 
 
-def chi_kernel(*refs):
-    tiles, chi_ref = refs[:-1], refs[-1]
-    chi_ref[...] = folded_dot(tiles[0].at[0], [ref.at[1] for ref in tiles])
+def bare_rows(team, pairs, stack, held, me):
+    symmetry, rank = me // team, me % team
+    lane = lax.broadcasted_iota(jnp.int32, (pairs, stack.shape[0]), 1)
+    owner = lane
+    if held is not None:
+        wide = stack.shape[0] // len(held)
+        owner = jnp.full(lane.shape, -1, jnp.int32)
+        for slot, row in enumerate(held):
+            owner = jnp.where(lane == slot * wide + symmetry, row, owner)
+    pick = owner == rank * pairs + lax.broadcasted_iota(jnp.int32, lane.shape, 0)
+    rows = jnp.dot(pick.astype(jnp.bfloat16), stack, preferred_element_type=jnp.float32)
+    if held is None:
+        return rows
+    turned = rows
+    for other in range(1, team):
+        cut = other * pairs
+        turned = jnp.where(rank == other, jnp.concatenate([rows[:, cut:], rows[:, :cut]], axis=1), turned)
+    return turned
+
+
+def chi_kernel(team, slabs, owners, *refs):
+    bare, tiles, chi_ref = refs[:slabs], refs[slabs:-1], refs[-1]
+    chi = folded_dot(tiles[0].at[0], [ref.at[1] for ref in tiles])
+    if bare:
+        me = lax.axis_index("idx")
+        stack = jnp.concatenate([ref[...] for ref in bare], axis=0)
+        chi += bare_rows(team, chi_ref.shape[0], stack, owners(me)[0], me)
+    chi_ref[...] = chi
 
 
 def update_kernel(team, slabs, owners, chi_ref, virtual_ref, occupied_ref, *refs):
@@ -114,23 +139,8 @@
     ints_ref, amps = tiles[0].at[1], [ref.at[0] for ref in tiles]
     out_ref, buffer, sems = refs[slabs + team :]
     me = lax.axis_index("idx")
-    symmetry, rank = me // team, me % team
-    pairs, count = chi_ref.shape
     stack = jnp.concatenate([ref[...] for ref in bare], axis=0)
-    held = owners(me)
-    lane = lax.broadcasted_iota(jnp.int32, (pairs, stack.shape[0]), 1)
-    if held is None:
-        owner = lane
-    else:
-        wide = stack.shape[0] // len(held)
-        owner = jnp.full(lane.shape, -1, jnp.int32)
-        for slot, row in enumerate(held):
-            owner = jnp.where(lane == slot * wide + symmetry, row, owner)
-    pick = owner == rank * pairs + lax.broadcasted_iota(jnp.int32, lane.shape, 0)
-    mine = jnp.dot(pick.astype(jnp.bfloat16), stack, preferred_element_type=jnp.float32)
-    column = lax.broadcasted_iota(jnp.int32, (count, count), 1) + rank * pairs
-    turn = lax.broadcasted_iota(jnp.int32, (count, count), 0) == jnp.where(column >= count, column - count, column)
-    mine = jnp.dot(mine.astype(jnp.bfloat16), turn.astype(jnp.bfloat16), preferred_element_type=jnp.float32)
+    mine = bare_rows(team, chi_ref.shape[0], stack, owners(me)[1], me)
     chi_half = (mine + chi_ref[...]).astype(jnp.bfloat16)
     occupied = occupied_ref[:, 0:1]
     width = ints_ref.shape[1]
@@ -157,8 +167,6 @@
 
 
 def exchange_rows_16(hole, near_hole):
-    near, far, both = 6, 4, 2
-
     def by_home(d, home, away):
         at_home = (d >> 3) == (d & 1)
         if isinstance(d, int):
@@ -166,32 +174,37 @@
         return d ^ jnp.where(at_home, home, away)
 
     def hop_one(d):
-        return by_home(d, near, far ^ 9)
+        return by_home(d, 6, 13)
 
     def hop_two(d):
-        return by_home(d, both, both ^ 9)
+        return by_home(d, 4, 11)
 
     def hop_three(d):
-        return d ^ 8
+        return by_home(d, 8, 3)
+
+    def from_three(d):
+        return by_home(d, 3, 8)
 
     def permute(block, hop):
         return lax.ppermute(block, "idx", [(d, hop(d)) for d in range(16)])
 
     def owners(me):
-        third = hop_three(me)
-        pairs = (me, hop_one(me), hop_two(me), third, hop_one(third))
-        return [row for d in pairs for row in (d, d ^ 1)]
+        third = from_three(me)
+        early, last = (me, hop_one(me)), (hop_two(me), third, hop_one(third))
+        return [[row for d in pairs for row in (d, d ^ 1)] for pairs in (early, last)]
 
     own = jnp.concatenate([near_hole, permute(hole, lambda d: d ^ 1)], axis=0)
     first, second = permute(own, hop_one), permute(own, hop_two)
     forward = jnp.concatenate([own, first], axis=0)
-    return [own, first, second, permute(forward, hop_three)], owners, own, forward
+    return [own, first], [second, permute(forward, hop_three)], owners, own, forward
 
 
 def exchange_rows(hole, team):
-    sent = jnp.repeat(jnp.swapaxes(hole, 0, 1), team, axis=0)
+    share = hole.shape[2] // team
+    sent = jnp.stack([jnp.roll(hole, -rank * share, axis=2) for rank in range(team)], axis=2)
+    sent = jnp.moveaxis(sent, 0, 2).reshape(IRREPS * team, *hole.shape[::2])
     received = lax.all_to_all(sent, "idx", split_axis=0, concat_axis=0, tiled=True)
-    return [received], lambda me: None, hole, received
+    return [], [received], lambda me: (None, None), hole, received
 
 
 def after(block, other):
@@ -238,25 +251,25 @@
     )
 
     if size == 16 and team == 2:
-        slabs, owners, first_sent, last_sent = exchange_rows_16(hole_integrals, near_hole)
+        early, late, owners, first_sent, last_sent = exchange_rows_16(hole_integrals, near_hole)
     else:
-        slabs, owners, first_sent, last_sent = exchange_rows(hole_integrals, team)
+        early, late, owners, first_sent, last_sent = exchange_rows(hole_integrals, team)
     others = [after(far, last_sent) for far in team_exchange(after(own, first_sent), team, size)]
     held = [near(tile) for tile in (own, *others)]
-    slabs = [slab.reshape(-1, pair_count) for slab in slabs]
+    early, late = [[slab.reshape(-1, pair_count) for slab in slabs] for slabs in (early, late)]
 
     chi = pl.pallas_call(
-        chi_kernel,
+        functools.partial(chi_kernel, team, len(early), owners),
         out_shape=jax.ShapeDtypeStruct((local_pairs, pair_count), jnp.float32),
-        in_specs=[IN_VMEM] * team,
+        in_specs=[IN_VMEM] * (len(early) + team),
         out_specs=IN_VMEM,
         compiler_params=params,
         cost_estimate=cost(bytes_accessed=2 * amplitudes.nbytes),
-    )(*held)
+    )(*early, *held)
     return pl.pallas_call(
-        functools.partial(update_kernel, team, len(slabs), owners),
+        functools.partial(update_kernel, team, len(late), owners),
         out_shape=jax.ShapeDtypeStruct((local_pairs, width), jnp.bfloat16),
-        in_specs=[IN_VMEM] * (3 + len(slabs) + team),
+        in_specs=[IN_VMEM] * (3 + len(late) + team),
         out_specs=IN_HBM,
         scratch_shapes=[
             pltpu.VMEM((local_pairs, width), jnp.bfloat16),
@@ -264,7 +277,7 @@
         ],
         compiler_params=params,
         cost_estimate=cost(bytes_accessed=4 * local_pairs * width * 2),
-    )(chi, virtual, occupied, *slabs, *held)
+    )(chi, virtual, occupied, *late, *held)
 
 
 def solution(mesh):

time: 15 us -> 14.6 us (0.973)
  waiting for transfers between devices: 1.75 us -> 1.53 us
    ppermute x4, waiting for transfers between devices: 1.74 us -> 1.53 us  [permute(): return lax.ppermute(block, 'idx', [(d, hop(d)) for d in range(16)])]
where the time goes in v6:
time: 14.6 us; the launch traced here: 14.4 us
  starting transfers between devices  8.09 us (55%)
  Pallas kernels  4.75 us (33%)
  waiting for transfers between devices  1.53 us (10%)
    ppermute x4, starting transfers between devices, permute(): return lax.ppermute(block, 'idx', [(d, hop(d)) for d in range(16)])  7.97 us
    pallas_call x1, Pallas kernels, on_device(): pl.pallas_call(functools.partial(update_kernel, team, len(late), owners),...  1.98 us
    pallas_call x1, Pallas kernels, on_device(): pl.pallas_call(functools.partial(load_kernel, team), out_shape=[jax.Shape...  1.81 us
    ppermute x4, waiting for transfers between devices, permute(): return lax.ppermute(block, 'idx', [(d, hop(d)) for d in range(16)])  1.53 us
    pallas_call x1, Pallas kernels, on_device(): pl.pallas_call(functools.partial(chi_kernel, team, len(early), owners), o...  0.97 us
  transfers between devices with their start and end apart: 5, of which 2 were waited for; matrix products, arithmetic and copies ran while one was open for 0% of the time, Pallas kernels for 19%

profile of v6, /device:TPU:0, one launch (start us, length us, event | category | flops | bytes accessed | tf_op | source)
XLA Modules:
  0.0 14.4 jit_solution(10243125921168438128)
XLA Ops:
  0.0 0.5 %collective-permute-start = (bf16[1,8,16]{2,1,0:T(8,128)(2,1)}, bf16[1,8,16]{2,1,0:T(8,128)(2,1)S(1)}, u32[]{:S(2)}, u32[]{:S(2)}) collective-permute-start(bf16[1,8,16]{2,1,0:T(8,128)(2,1)} %hole_hbm.1), channel_id=1, source_target_pairs={{0,1},{1,0},{2,3},{3,2},{4,5},{5,4},{6,7},{7,6},{8,9},{9,8},{10,11... | collective-permute-start | bytes 776 | tf_op jit(solution)/shard_map/ppermute | solution.py:189
  0.5 1.8 %shard_map.64 = (f32[8,10240]{1,0:T(8,128)S(1)}, f32[8,128]{1,0:T(8,128)S(1)}, bf16[1,8,16]{2,1,0:T(8,128)(2,1)S(1)}, bf16[2,8,80000]{2,1,0:T(8,128)(2,1)S(1)}) custom-call(f32[800]{0:T(1024)} %vir_hbm.1, f32[200]{0:T(256)} %occ_hbm.1, s32[2,8]{1,0:T(2,128)} %bitcast.9, bf16[1,8,16]{2,1,0:T(8,128)(2,1)} %hole_hbm.1, bf16[8,80000]{1,0:T(8,128)(2,1)} %amps_hbm.1, ...), custom_call_target="tpu_custom_call" | custom-call | bytes 2560000 | tf_op jit(solution)/shard_map/pallas_call | solution.py:230
  2.3 0.0 collective-permute-done
  2.3 0.1 collective-permute-start.2
  2.4 4.0 %collective-permute-start.1 = (bf16[2,8,16]{2,1,0:T(8,128)(2,1)S(1)}, bf16[2,8,16]{2,1,0:T(8,128)(2,1)S(1)}, u32[]{:S(2)}, u32[]{:S(2)}) collective-permute-start(bf16[2,8,16]{2,1,0:T(8,128)(2,1)S(1)} %get-tuple-element.18), channel_id=1, source_target_pairs={{0,6},{1,12},{2,4},{3,14},{4,2},{5,8},{6,0},{7,10},{8,5},{9,15},{1... | collective-permute-start | bytes 1544 | tf_op jit(solution)/shard_map/ppermute | solution.py:189
  6.4 0.4 %collective-permute-start.3 = (bf16[2,8,16]{2,1,0:T(8,128)(2,1)S(1)}, bf16[2,8,16]{2,1,0:T(8,128)(2,1)S(1)}, u32[]{:S(2)}, u32[]{:S(2)}) collective-permute-start(bf16[2,8,16]{2,1,0:T(8,128)(2,1)S(1)} %get-tuple-element.18), channel_id=1, source_target_pairs={{0,4},{1,10},{2,6},{3,8},{4,0},{5,14},{6,2},{7,12},{8,3},{9,13},{1... | collective-permute-start | bytes 1544 | tf_op jit(solution)/shard_map/ppermute | solution.py:189
  6.9 1.1 %collective-permute-done.1 = bf16[2,8,16]{2,1,0:T(8,128)(2,1)S(1)} collective-permute-done((bf16[2,8,16]{2,1,0:T(8,128)(2,1)S(1)}, bf16[2,8,16]{2,1,0:T(8,128)(2,1)S(1)}, u32[]{:S(2)}, u32[]{:S(2)}) %collective-permute-start.1) | collective-permute-done | bytes 544 | tf_op jit(solution)/shard_map/ppermute | solution.py:189
  8.0 3.1 %collective-permute-start.4 = (bf16[4,8,16]{2,1,0:T(8,128)(2,1)S(1)}, bf16[4,8,16]{2,1,0:T(8,128)(2,1)S(1)}, u32[]{:S(2)}, u32[]{:S(2)}) collective-permute-start(bf16[4,8,16]{2,1,0:T(8,128)(2,1)S(1)} %constant_dynamic-update-slice_fusion.2), channel_id=1, source_target_pairs={{0,8},{1,2},{2,10},{3,0},{4,12},{5,6},{6,14},{7,4},{8,11},{9,1},{1... | collective-permute-start | bytes 3080 | tf_op jit(solution)/shard_map/ppermute | solution.py:189
  11.1 0.0 collective-permute-done.2.refs_3_
  11.1 1.0 %shard_map.65.chi_ref = f32[8,16]{1,0:T(8,128)S(1)} custom-call(bf16[16,16]{1,0:T(8,128)(2,1)S(1)} %bitcast.6, bf16[16,16]{1,0:T(8,128)(2,1)S(1)} %bitcast.5, bf16[2,8,80000]{2,1,0:T(8,128)(2,1)S(1)} %get-tuple-element.13.refs_2_, bf16[2,8,80000]{2,1,0:T(8,128)(2,1)S(1)} %collective-permute-done.2.refs_3_), custom_call_target="tpu_custom_call" | custom-call | flops 20480000 | bytes 2560000 | tf_op jit(solution)/shard_map/pallas_call | solution.py:261
  12.1 0.0 collective-permute-done.3
  12.1 0.4 %collective-permute-done.4 = bf16[4,8,16]{2,1,0:T(8,128)(2,1)S(1)} collective-permute-done((bf16[4,8,16]{2,1,0:T(8,128)(2,1)S(1)}, bf16[4,8,16]{2,1,0:T(8,128)(2,1)S(1)}, u32[]{:S(2)}, u32[]{:S(2)}) %collective-permute-start.4) | collective-permute-done | bytes 1056 | tf_op jit(solution)/shard_map/ppermute | solution.py:189
  12.5 2.0 %shard_map.66 = bf16[8,80000]{1,0:T(8,128)(2,1)} custom-call(f32[8,16]{1,0:T(8,128)S(1)} %shard_map.65.chi_ref, f32[8,10240]{1,0:T(8,128)S(1)} %get-tuple-element.15.virtual_ref, f32[8,128]{1,0:T(8,128)S(1)} %get-tuple-element.16.occupied_ref, bf16[16,16]{1,0:T(8,128)(2,1)S(1)} %bitcast.8, bf16[32,16]{1,0:T(8,128)(2,1)S(1)} %bitcast.7, ...), custom_call_target="tpu_custom_call" | custom-call | flops 20480000 | bytes 5120000 | tf_op jit(solution)/shard_map/pallas_call | solution.py:269
  (3 shorter events, 0.0 us)
Async XLA Ops:
  0.0 2.3 %collective-permute-start = (bf16[1,8,16]{2,1,0:T(8,128)(2,1)}, bf16[1,8,16]{2,1,0:T(8,128)(2,1)S(1)}, u32[]{:S(2)}, u32[]{:S(2)}) collective-permute-start(bf16[1,8,16]{2,1,0:T(8,128)(2,1)} %hole_hbm.1), channel_id=1, source_target_pairs={{0,1},{1,0},{2,3},{3,2},{4,5},{5,4},{6,7},{7,6},{8,9},{9,8},{10,11... | collective-permute-start | bytes 776 | tf_op jit(solution)/shard_map/ppermute | solution.py:189
  2.3 8.8 %collective-permute-start.2 = (bf16[2,8,80000]{2,1,0:T(8,128)(2,1)S(1)}, bf16[2,8,80000]{2,1,0:T(8,128)(2,1)S(1)}, u32[]{:S(2)}, u32[]{:S(2)}) collective-permute-start(bf16[2,8,80000]{2,1,0:T(8,128)(2,1)S(1)} %get-tuple-element.13.refs_2_), channel_id=1, source_target_pairs={{0,1},{1,0},{2,3},{3,2},{4,5},{5,4},{6,7},{7,6},{8,9},{9,8},{10,11... | collective-permute-start | bytes 7680008 | tf_op jit(solution)/shard_map/ppermute | solution.py:164
  2.4 5.6 %collective-permute-start.1 = (bf16[2,8,16]{2,1,0:T(8,128)(2,1)S(1)}, bf16[2,8,16]{2,1,0:T(8,128)(2,1)S(1)}, u32[]{:S(2)}, u32[]{:S(2)}) collective-permute-start(bf16[2,8,16]{2,1,0:T(8,128)(2,1)S(1)} %get-tuple-element.18), channel_id=1, source_target_pairs={{0,6},{1,12},{2,4},{3,14},{4,2},{5,8},{6,0},{7,10},{8,5},{9,15},{1... | collective-permute-start | bytes 1544 | tf_op jit(solution)/shard_map/ppermute | solution.py:189
  6.4 5.7 %collective-permute-start.3 = (bf16[2,8,16]{2,1,0:T(8,128)(2,1)S(1)}, bf16[2,8,16]{2,1,0:T(8,128)(2,1)S(1)}, u32[]{:S(2)}, u32[]{:S(2)}) collective-permute-start(bf16[2,8,16]{2,1,0:T(8,128)(2,1)S(1)} %get-tuple-element.18), channel_id=1, source_target_pairs={{0,4},{1,10},{2,6},{3,8},{4,0},{5,14},{6,2},{7,12},{8,3},{9,13},{1... | collective-permute-start | bytes 1544 | tf_op jit(solution)/shard_map/ppermute | solution.py:189
  8.0 4.5 %collective-permute-start.4 = (bf16[4,8,16]{2,1,0:T(8,128)(2,1)S(1)}, bf16[4,8,16]{2,1,0:T(8,128)(2,1)S(1)}, u32[]{:S(2)}, u32[]{:S(2)}) collective-permute-start(bf16[4,8,16]{2,1,0:T(8,128)(2,1)S(1)} %constant_dynamic-update-slice_fusion.2), channel_id=1, source_target_pairs={{0,8},{1,2},{2,10},{3,0},{4,12},{5,6},{6,14},{7,4},{8,11},{9,1},{1... | collective-permute-start | bytes 3080 | tf_op jit(solution)/shard_map/ppermute | solution.py:189

commit v7 on v6

--- a/solution.py
+++ b/solution.py
@@ -63,25 +63,29 @@
     return jnp.concatenate(sums, axis=1)
 
 
-def load_kernel(team, vir_hbm, occ_hbm, orbitals_hbm, hole_hbm, amps_hbm, ints_hbm, *refs):
-    virtual_ref, occupied_ref, hole_ref, tiles_ref, vir_ref, occ_ref, orbitals_ref, sems = refs
-    moves = (
-        (vir_hbm, vir_ref),
-        (occ_hbm, occ_ref),
-        (orbitals_hbm, orbitals_ref),
-        (hole_hbm, hole_ref),
-        (amps_hbm, tiles_ref.at[0]),
-        (ints_hbm, tiles_ref.at[1]),
-    )
-    copies = [pltpu.make_async_copy(*move, sems.at[slot]) for slot, move in enumerate(moves)]
+def tile_copies(amps_hbm, ints_hbm, tiles_ref, sems):
+    return [
+        pltpu.make_async_copy(source, tiles_ref.at[which], sems.at[which])
+        for which, source in enumerate((amps_hbm, ints_hbm))
+    ]
+
+
+def load_kernel(here, *refs):
+    small, (amps_hbm, ints_hbm), targets = refs[:4], refs[4:6], refs[6:10]
+    tiles_ref, sems, tile_sems = refs[10:]
+    copies = [pltpu.make_async_copy(*move, sems.at[slot]) for slot, move in enumerate(zip(small, targets))]
     for copy in copies:
         copy.start()
-    for copy in copies[:3]:
-        copy.wait()
-    symmetry = lax.axis_index("idx") // team
-    virtual_ref[...] = virtual_sums(vir_ref[...].reshape(1, -1), symmetry, virtual_ref.shape[1] // 128)
-    occupied_ref[...] = occupied_sums(occ_ref[...].reshape(1, -1), orbitals_ref[...])
-    for copy in copies[3:]:
+
+    @pl.when(lax.axis_index("idx") < here)
+    def _():
+        tiles = tile_copies(amps_hbm, ints_hbm, tiles_ref, tile_sems)
+        for copy in tiles:
+            copy.start()
+        for copy in tiles:
+            copy.wait()
+
+    for copy in copies:
         copy.wait()
 
 
@@ -124,19 +128,31 @@
     return turned
 
 
-def chi_kernel(team, slabs, owners, *refs):
-    bare, tiles, chi_ref = refs[:slabs], refs[slabs:-1], refs[-1]
-    chi = folded_dot(tiles[0].at[0], [ref.at[1] for ref in tiles])
+def chi_kernel(team, here, slabs, owners, amps_hbm, ints_hbm, held_ref, vir_ref, occ_ref, orbitals_ref, *refs):
+    bare, ints = refs[:slabs], refs[slabs : slabs + team - 1]
+    chi_ref, tiles_ref, virtual_ref, occupied_ref, sems = refs[slabs + team - 1 :]
+    me = lax.axis_index("idx")
+
+    @pl.when(me >= here)
+    def _():
+        copies = tile_copies(amps_hbm, ints_hbm, tiles_ref, sems)
+        for copy in copies:
+            copy.start()
+        for copy in copies:
+            copy.wait()
+
+    virtual_ref[...] = virtual_sums(vir_ref[...].reshape(1, -1), me // team, virtual_ref.shape[1] // 128)
+    occupied_ref[...] = occupied_sums(occ_ref[...].reshape(1, -1), orbitals_ref[...])
+    chi = folded_dot(tiles_ref.at[0], [tiles_ref.at[1], *ints])
     if bare:
-        me = lax.axis_index("idx")
         stack = jnp.concatenate([ref[...] for ref in bare], axis=0)
         chi += bare_rows(team, chi_ref.shape[0], stack, owners(me)[0], me)
     chi_ref[...] = chi
 
 
 def update_kernel(team, slabs, owners, chi_ref, virtual_ref, occupied_ref, *refs):
-    bare, tiles = refs[:slabs], refs[slabs : slabs + team]
-    ints_ref, amps = tiles[0].at[1], [ref.at[0] for ref in tiles]
+    bare, tiles_ref = refs[:slabs], refs[slabs]
+    ints_ref, amps = tiles_ref.at[1], [tiles_ref.at[0], *refs[slabs + 1 : slabs + team]]
     out_ref, buffer, sems = refs[slabs + team :]
     me = lax.axis_index("idx")
     stack = jnp.concatenate([ref[...] for ref in bare], axis=0)
@@ -227,45 +243,46 @@
     params = pltpu.CompilerParams(vmem_limit_bytes=(16 if team == 2 else 40) * 1024 * 1024)
     cost = functools.partial(pl.CostEstimate, flops=2 * local_pairs * pair_count * width, transcendentals=0)
 
-    virtual, occupied, near_hole, own = pl.pallas_call(
-        functools.partial(load_kernel, team),
+    paired = size == 16 and team == 2
+    here = size // 2 if paired else size
+
+    small = (vir_energy, occ_energy, pair_orbitals.T, hole_integrals)
+    *energies, near_hole, own = pl.pallas_call(
+        functools.partial(load_kernel, here),
         out_shape=[
-            jax.ShapeDtypeStruct((IRREPS, tiles * 128), jnp.float32),
-            jax.ShapeDtypeStruct((local_pairs, 128), jnp.float32),
-            pltpu.VMEM(hole_integrals.shape, hole_integrals.dtype),
+            *[pltpu.VMEM(array.shape, array.dtype) for array in small],
             pltpu.VMEM((2, *amplitudes.shape), amplitudes.dtype),
         ],
         in_specs=[IN_HBM] * 6,
-        out_specs=[IN_VMEM] * 4,
-        scratch_shapes=[
-            pltpu.VMEM(vir_energy.shape, jnp.float32),
-            pltpu.VMEM(occ_energy.shape, jnp.float32),
-            pltpu.VMEM((2, local_pairs), jnp.int32),
-            pltpu.SemaphoreType.DMA((6,)),
-        ],
-        compiler_params=params,
-        cost_estimate=pl.CostEstimate(flops=0, bytes_accessed=2 * amplitudes.nbytes, transcendentals=0),
-    )(
-        *[in_hbm(array) for array in (vir_energy, occ_energy, pair_orbitals.T)],
-        *[in_hbm(array) for array in (hole_integrals, amplitudes, integrals)],
-    )
-
-    if size == 16 and team == 2:
+        out_specs=[IN_VMEM] * 5,
+        scratch_shapes=[pltpu.SemaphoreType.DMA((4,)), pltpu.SemaphoreType.DMA((2,))],
+        compiler_params=pltpu.CompilerParams(vmem_limit_bytes=61 * 1024 * 1024),
+        cost_estimate=pl.CostEstimate(flops=0, bytes_accessed=0, transcendentals=0),
+    )(*[in_hbm(array) for array in (*small, amplitudes, integrals)])
+
+    if paired:
         early, late, owners, first_sent, last_sent = exchange_rows_16(hole_integrals, near_hole)
     else:
         early, late, owners, first_sent, last_sent = exchange_rows(hole_integrals, team)
-    others = [after(far, last_sent) for far in team_exchange(after(own, first_sent), team, size)]
-    held = [near(tile) for tile in (own, *others)]
+    far_ints = [after(far, last_sent) for far in team_exchange(after(integrals, first_sent), team, size)]
+    far_amps = team_exchange(after(amplitudes, first_sent), team, size)
     early, late = [[slab.reshape(-1, pair_count) for slab in slabs] for slabs in (early, late)]
 
-    chi = pl.pallas_call(
-        functools.partial(chi_kernel, team, len(early), owners),
-        out_shape=jax.ShapeDtypeStruct((local_pairs, pair_count), jnp.float32),
-        in_specs=[IN_VMEM] * (len(early) + team),
-        out_specs=IN_VMEM,
+    chi, own, virtual, occupied = pl.pallas_call(
+        functools.partial(chi_kernel, team, here, len(early), owners),
+        out_shape=[
+            jax.ShapeDtypeStruct((local_pairs, pair_count), jnp.float32),
+            pltpu.VMEM(own.shape, own.dtype),
+            jax.ShapeDtypeStruct((IRREPS, tiles * 128), jnp.float32),
+            jax.ShapeDtypeStruct((local_pairs, 128), jnp.float32),
+        ],
+        in_specs=[IN_HBM] * 2 + [IN_VMEM] * (3 + len(early) + team),
+        out_specs=[IN_VMEM] * 4,
+        scratch_shapes=[pltpu.SemaphoreType.DMA((2,))],
+        input_output_aliases={2: 1},
         compiler_params=params,
         cost_estimate=cost(bytes_accessed=2 * amplitudes.nbytes),
-    )(*early, *held)
+    )(in_hbm(amplitudes), in_hbm(integrals), near(own), *energies, *early, *[near(far) for far in far_ints])
     return pl.pallas_call(
         functools.partial(update_kernel, team, len(late), owners),
         out_shape=jax.ShapeDtypeStruct((local_pairs, width), jnp.bfloat16),
@@ -277,7 +294,7 @@
         ],
         compiler_params=params,
         cost_estimate=cost(bytes_accessed=4 * local_pairs * width * 2),
-    )(chi, virtual, occupied, *late, *held)
+    )(chi, virtual, occupied, *late, near(own), *[near(far) for far in far_amps])
 
 
 def solution(mesh):

time: 14.6 us -> 14 us (0.959)
  starting transfers between devices: 8.09 us -> 7.55 us
  waiting for transfers between devices: 1.53 us -> 1.22 us
  Pallas kernels: 4.75 us -> 5.06 us
    ppermute x4, starting transfers between devices: 7.97 us -> 6.98 us  [permute(): return lax.ppermute(block, 'idx', [(d, hop(d)) for d in range(16)])]
    ppermute x1 -> x2, starting transfers between devices: 0.12 us -> 0.58 us  [team_exchange(): lax.ppermute(block, 'idx', [(d, d // team * team + (d - step) % team) for...]
    ppermute x4, waiting for transfers between devices: 1.53 us -> 1.21 us  [permute(): return lax.ppermute(block, 'idx', [(d, hop(d)) for d in range(16)])]
    pallas_call x2, Pallas kernels: 2.77 us -> 3.08 us  [the longest x1 1.81 us: on_device(): pl.pallas_call(functools.partial(load_kernel, here), out_shape=[*[pltpu.V...]
  transfers between devices with their start and end apart: 5 -> 6, of which waited for: 2 -> 2; matrix products, arithmetic and copies ran while one was open for 0% -> 0% of each run, Pallas kernels for 19% -> 22%
where the time goes in v7:
time: 14 us; the launch traced here: 13.9 us
  starting transfers between devices  7.55 us (54%)
  Pallas kernels  5.06 us (36%)
  waiting for transfers between devices  1.22 us (9%)
    ppermute x4, starting transfers between devices, permute(): return lax.ppermute(block, 'idx', [(d, hop(d)) for d in range(16)])  6.98 us
    pallas_call x1, Pallas kernels, on_device(): pl.pallas_call(functools.partial(update_kernel, team, len(late), owners),...  1.97 us
    pallas_call x1, Pallas kernels, on_device(): pl.pallas_call(functools.partial(load_kernel, here), out_shape=[*[pltpu.V...  1.81 us
    pallas_call x1, Pallas kernels, on_device(): pl.pallas_call(functools.partial(chi_kernel, team, here, len(early), owne...  1.27 us
    ppermute x4, waiting for transfers between devices, permute(): return lax.ppermute(block, 'idx', [(d, hop(d)) for d in range(16)])  1.21 us
    ppermute x2, starting transfers between devices, team_exchange(): lax.ppermute(block, 'idx', [(d, d // team * team + (d - step) % team) for...  0.58 us
  transfers between devices with their start and end apart: 6, of which 2 were waited for; matrix products, arithmetic and copies ran while one was open for 0% of the time, Pallas kernels for 22%

profile of v7, /device:TPU:0, one launch (start us, length us, event | category | flops | bytes accessed | tf_op | source)
XLA Modules:
  0.0 13.9 jit_solution(10755387485953000099)
XLA Ops:
  0.0 0.5 %collective-permute-start = (bf16[1,8,16]{2,1,0:T(8,128)(2,1)}, bf16[1,8,16]{2,1,0:T(8,128)(2,1)S(1)}, u32[]{:S(2)}, u32[]{:S(2)}) collective-permute-start(bf16[1,8,16]{2,1,0:T(8,128)(2,1)} %refs_3_.1), channel_id=1, source_target_pairs={{0,1},{1,0},{2,3},{3,2},{4,5},{5,4},{6,7},{7,6},{8,9},{9,8},{10,11... | collective-permute-start | bytes 776 | tf_op jit(solution)/shard_map/ppermute | solution.py:205
  0.5 1.8 %shard_map.64 = (f32[800]{0:T(1024)S(1)}, f32[200]{0:T(256)S(1)}, s32[2,8]{1,0:T(2,128)S(1)}, bf16[1,8,16]{2,1,0:T(8,128)(2,1)S(1)}, bf16[2,8,80000]{2,1,0:T(8,128)(2,1)S(1)}) custom-call(f32[800]{0:T(1024)} %refs_0_.1, f32[200]{0:T(256)} %refs_1_.1, s32[2,8]{1,0:T(2,128)} %bitcast.9, bf16[1,8,16]{2,1,0:T(8,128)(2,1)} %refs_3_.1, bf16[8,80000]{1,0:T(8,128)(2,1)} %amps_hbm.1, ...), custom_call_target="tpu_custom_call" | custom-call | tf_op jit(solution)/shard_map/pallas_call | solution.py:250
  2.3 0.0 collective-permute-done
  2.3 0.1 collective-permute-start.2
  2.4 0.5 %collective-permute-start.5 = (bf16[8,80000]{1,0:T(8,128)(2,1)}, bf16[8,80000]{1,0:T(8,128)(2,1)S(1)}, u32[]{:S(2)}, u32[]{:S(2)}) collective-permute-start(bf16[8,80000]{1,0:T(8,128)(2,1)} %amps_hbm.1), channel_id=1, source_target_pairs={{0,1},{1,0},{2,3},{3,2},{4,5},{5,4},{6,7},{7,6},{8,9},{9,8},{10,11... | collective-permute-start | bytes 3840008 | tf_op jit(solution)/shard_map/ppermute | solution.py:180
  2.9 3.6 %collective-permute-start.1 = (bf16[2,8,16]{2,1,0:T(8,128)(2,1)S(1)}, bf16[2,8,16]{2,1,0:T(8,128)(2,1)S(1)}, u32[]{:S(2)}, u32[]{:S(2)}) collective-permute-start(bf16[2,8,16]{2,1,0:T(8,128)(2,1)S(1)} %get-tuple-element.30), channel_id=1, source_target_pairs={{0,6},{1,12},{2,4},{3,14},{4,2},{5,8},{6,0},{7,10},{8,5},{9,15},{1... | collective-permute-start | bytes 1544 | tf_op jit(solution)/shard_map/ppermute | solution.py:205
  6.5 0.4 %collective-permute-start.3 = (bf16[2,8,16]{2,1,0:T(8,128)(2,1)S(1)}, bf16[2,8,16]{2,1,0:T(8,128)(2,1)S(1)}, u32[]{:S(2)}, u32[]{:S(2)}) collective-permute-start(bf16[2,8,16]{2,1,0:T(8,128)(2,1)S(1)} %get-tuple-element.30), channel_id=1, source_target_pairs={{0,4},{1,10},{2,6},{3,8},{4,0},{5,14},{6,2},{7,12},{8,3},{9,13},{1... | collective-permute-start | bytes 1544 | tf_op jit(solution)/shard_map/ppermute | solution.py:205
  6.9 1.1 %collective-permute-done.1 = bf16[2,8,16]{2,1,0:T(8,128)(2,1)S(1)} collective-permute-done((bf16[2,8,16]{2,1,0:T(8,128)(2,1)S(1)}, bf16[2,8,16]{2,1,0:T(8,128)(2,1)S(1)}, u32[]{:S(2)}, u32[]{:S(2)}) %collective-permute-start.1) | collective-permute-done | bytes 544 | tf_op jit(solution)/shard_map/ppermute | solution.py:205
  8.1 2.5 %collective-permute-start.4 = (bf16[4,8,16]{2,1,0:T(8,128)(2,1)S(1)}, bf16[4,8,16]{2,1,0:T(8,128)(2,1)S(1)}, u32[]{:S(2)}, u32[]{:S(2)}) collective-permute-start(bf16[4,8,16]{2,1,0:T(8,128)(2,1)S(1)} %constant_dynamic-update-slice_fusion.2), channel_id=1, source_target_pairs={{0,8},{1,2},{2,10},{3,0},{4,12},{5,6},{6,14},{7,4},{8,11},{9,1},{1... | collective-permute-start | bytes 3080 | tf_op jit(solution)/shard_map/ppermute | solution.py:205
  10.6 0.0 collective-permute-done.2.refs_2_
  10.6 1.3 %shard_map.65 = (f32[8,16]{1,0:T(8,128)S(1)}, bf16[2,8,80000]{2,1,0:T(8,128)(2,1)S(1)}, f32[8,10240]{1,0:T(8,128)S(1)}, f32[8,128]{1,0:T(8,128)S(1)}) custom-call(bf16[8,80000]{1,0:T(8,128)(2,1)} %amps_hbm.1, bf16[8,80000]{1,0:T(8,128)(2,1)} %ints_hbm.1, bf16[2,8,80000]{2,1,0:T(8,128)(2,1)S(1)} %get-tuple-element.17.held_ref, ...), custom_call_target="tpu_custom_call", output_to_operand_aliasing={{1}: (2, {})} | custom-call | flops 20480000 | bytes 2560000 | tf_op jit(solution)/shard_map/pallas_call | solution.py:271
  11.8 0.0 collective-permute-done.3
  11.8 0.1 collective-permute-done.4
  11.9 0.0 collective-permute-done.5.refs_3_
  11.9 2.0 %shard_map.66 = bf16[8,80000]{1,0:T(8,128)(2,1)} custom-call(f32[8,16]{1,0:T(8,128)S(1)} %get-tuple-element.24.chi_ref, f32[8,10240]{1,0:T(8,128)S(1)} %get-tuple-element.25.virtual_ref, f32[8,128]{1,0:T(8,128)S(1)} %get-tuple-element.26.occupied_ref, bf16[16,16]{1,0:T(8,128)(2,1)S(1)} %bitcast.8, bf16[32,16]{1,0:T(8,128)(2,1)S(1)} %bitcast.7, ...), custom_call_target="tpu_custom_call" | custom-call | flops 20480000 | bytes 5120000 | tf_op jit(solution)/shard_map/pallas_call | solution.py:286
  (3 shorter events, 0.0 us)
Async XLA Ops:
  0.0 2.3 %collective-permute-start = (bf16[1,8,16]{2,1,0:T(8,128)(2,1)}, bf16[1,8,16]{2,1,0:T(8,128)(2,1)S(1)}, u32[]{:S(2)}, u32[]{:S(2)}) collective-permute-start(bf16[1,8,16]{2,1,0:T(8,128)(2,1)} %refs_3_.1), channel_id=1, source_target_pairs={{0,1},{1,0},{2,3},{3,2},{4,5},{5,4},{6,7},{7,6},{8,9},{9,8},{10,11... | collective-permute-start | bytes 776 | tf_op jit(solution)/shard_map/ppermute | solution.py:205
  2.3 8.2 %collective-permute-start.2 = (bf16[8,80000]{1,0:T(8,128)(2,1)}, bf16[8,80000]{1,0:T(8,128)(2,1)S(1)}, u32[]{:S(2)}, u32[]{:S(2)}) collective-permute-start(bf16[8,80000]{1,0:T(8,128)(2,1)} %ints_hbm.1), channel_id=1, source_target_pairs={{0,1},{1,0},{2,3},{3,2},{4,5},{5,4},{6,7},{7,6},{8,9},{9,8},{10,11... | collective-permute-start | bytes 3840008 | tf_op jit(solution)/shard_map/ppermute | solution.py:180
  2.4 9.5 %collective-permute-start.5 = (bf16[8,80000]{1,0:T(8,128)(2,1)}, bf16[8,80000]{1,0:T(8,128)(2,1)S(1)}, u32[]{:S(2)}, u32[]{:S(2)}) collective-permute-start(bf16[8,80000]{1,0:T(8,128)(2,1)} %amps_hbm.1), channel_id=1, source_target_pairs={{0,1},{1,0},{2,3},{3,2},{4,5},{5,4},{6,7},{7,6},{8,9},{9,8},{10,11... | collective-permute-start | bytes 3840008 | tf_op jit(solution)/shard_map/ppermute | solution.py:180
  2.9 5.2 %collective-permute-start.1 = (bf16[2,8,16]{2,1,0:T(8,128)(2,1)S(1)}, bf16[2,8,16]{2,1,0:T(8,128)(2,1)S(1)}, u32[]{:S(2)}, u32[]{:S(2)}) collective-permute-start(bf16[2,8,16]{2,1,0:T(8,128)(2,1)S(1)} %get-tuple-element.30), channel_id=1, source_target_pairs={{0,6},{1,12},{2,4},{3,14},{4,2},{5,8},{6,0},{7,10},{8,5},{9,15},{1... | collective-permute-start | bytes 1544 | tf_op jit(solution)/shard_map/ppermute | solution.py:205
  6.5 5.3 %collective-permute-start.3 = (bf16[2,8,16]{2,1,0:T(8,128)(2,1)S(1)}, bf16[2,8,16]{2,1,0:T(8,128)(2,1)S(1)}, u32[]{:S(2)}, u32[]{:S(2)}) collective-permute-start(bf16[2,8,16]{2,1,0:T(8,128)(2,1)S(1)} %get-tuple-element.30), channel_id=1, source_target_pairs={{0,4},{1,10},{2,6},{3,8},{4,0},{5,14},{6,2},{7,12},{8,3},{9,13},{1... | collective-permute-start | bytes 1544 | tf_op jit(solution)/shard_map/ppermute | solution.py:205
  8.1 3.8 %collective-permute-start.4 = (bf16[4,8,16]{2,1,0:T(8,128)(2,1)S(1)}, bf16[4,8,16]{2,1,0:T(8,128)(2,1)S(1)}, u32[]{:S(2)}, u32[]{:S(2)}) collective-permute-start(bf16[4,8,16]{2,1,0:T(8,128)(2,1)S(1)} %constant_dynamic-update-slice_fusion.2), channel_id=1, source_target_pairs={{0,8},{1,2},{2,10},{3,0},{4,12},{5,6},{6,14},{7,4},{8,11},{9,1},{1... | collective-permute-start | bytes 3080 | tf_op jit(solution)/shard_map/ppermute | solution.py:205

commit v8 on v7

--- a/solution.py
+++ b/solution.py
@@ -63,30 +63,38 @@
     return jnp.concatenate(sums, axis=1)
 
 
-def tile_copies(amps_hbm, ints_hbm, tiles_ref, sems):
-    return [
-        pltpu.make_async_copy(source, tiles_ref.at[which], sems.at[which])
-        for which, source in enumerate((amps_hbm, ints_hbm))
-    ]
-
-
-def load_kernel(here, *refs):
-    small, (amps_hbm, ints_hbm), targets = refs[:4], refs[4:6], refs[6:10]
-    tiles_ref, sems, tile_sems = refs[10:]
+def tile_copies(sources, tiles_ref, sems):
+    return [pltpu.make_async_copy(source, tiles_ref.at[which], sems.at[which]) for which, source in enumerate(sources)]
+
+
+def energy_sums(team, me, small, virtual_ref, occupied_ref):
+    vir_ref, occ_ref, orbitals_ref = small
+    virtual_ref[...] = virtual_sums(vir_ref[...].reshape(1, -1), me // team, virtual_ref.shape[1] // 128)
+    occupied_ref[...] = occupied_sums(occ_ref[...].reshape(1, -1), orbitals_ref[...])
+
+
+def load_kernel(team, first, *refs):
+    small, sources, targets = refs[:4], refs[4:6], refs[6:10]
+    tiles_ref, virtual_ref, occupied_ref, sems, tile_sems = refs[10:]
+    me = lax.axis_index("idx")
     copies = [pltpu.make_async_copy(*move, sems.at[slot]) for slot, move in enumerate(zip(small, targets))]
+    tiles = tile_copies(sources, tiles_ref, tile_sems)
     for copy in copies:
         copy.start()
 
-    @pl.when(lax.axis_index("idx") < here)
+    @pl.when(first(me))
     def _():
-        tiles = tile_copies(amps_hbm, ints_hbm, tiles_ref, tile_sems)
         for copy in tiles:
             copy.start()
+
+    for copy in copies:
+        copy.wait()
+
+    @pl.when(first(me))
+    def _():
+        energy_sums(team, me, targets[:3], virtual_ref, occupied_ref)
         for copy in tiles:
             copy.wait()
-
-    for copy in copies:
-        copy.wait()
 
 
 def folded_dot(left, rights):
@@ -128,21 +136,20 @@
     return turned
 
 
-def chi_kernel(team, here, slabs, owners, amps_hbm, ints_hbm, held_ref, vir_ref, occ_ref, orbitals_ref, *refs):
-    bare, ints = refs[:slabs], refs[slabs : slabs + team - 1]
-    chi_ref, tiles_ref, virtual_ref, occupied_ref, sems = refs[slabs + team - 1 :]
+def chi_kernel(team, first, slabs, owners, amps_hbm, ints_hbm, vir_ref, occ_ref, orbitals_ref, *refs):
+    bare, ints = refs[3 : slabs + 3], refs[slabs + 3 : slabs + team + 2]
+    chi_ref, tiles_ref, virtual_ref, occupied_ref, sems = refs[slabs + team + 2 :]
     me = lax.axis_index("idx")
 
-    @pl.when(me >= here)
+    @pl.when(jnp.logical_not(first(me)))
     def _():
-        copies = tile_copies(amps_hbm, ints_hbm, tiles_ref, sems)
+        copies = tile_copies((amps_hbm, ints_hbm), tiles_ref, sems)
         for copy in copies:
             copy.start()
+        energy_sums(team, me, (vir_ref, occ_ref, orbitals_ref), virtual_ref, occupied_ref)
         for copy in copies:
             copy.wait()
 
-    virtual_ref[...] = virtual_sums(vir_ref[...].reshape(1, -1), me // team, virtual_ref.shape[1] // 128)
-    occupied_ref[...] = occupied_sums(occ_ref[...].reshape(1, -1), orbitals_ref[...])
     chi = folded_dot(tiles_ref.at[0], [tiles_ref.at[1], *ints])
     if bare:
         stack = jnp.concatenate([ref[...] for ref in bare], axis=0)
@@ -244,17 +251,21 @@
     cost = functools.partial(pl.CostEstimate, flops=2 * local_pairs * pair_count * width, transcendentals=0)
 
     paired = size == 16 and team == 2
-    here = size // 2 if paired else size
+
+    def first(me):
+        return jnp.logical_and(me < 8, me >> 1 != 1) if paired else me >= 0
 
     small = (vir_energy, occ_energy, pair_orbitals.T, hole_integrals)
-    *energies, near_hole, own = pl.pallas_call(
-        functools.partial(load_kernel, here),
-        out_shape=[
-            *[pltpu.VMEM(array.shape, array.dtype) for array in small],
-            pltpu.VMEM((2, *amplitudes.shape), amplitudes.dtype),
-        ],
+    prepared = [
+        pltpu.VMEM((2, *amplitudes.shape), amplitudes.dtype),
+        pltpu.VMEM((IRREPS, tiles * 128), jnp.float32),
+        pltpu.VMEM((local_pairs, 128), jnp.float32),
+    ]
+    *energies, near_hole, own, virtual, occupied = pl.pallas_call(
+        functools.partial(load_kernel, team, first),
+        out_shape=[*[pltpu.VMEM(array.shape, array.dtype) for array in small], *prepared],
         in_specs=[IN_HBM] * 6,
-        out_specs=[IN_VMEM] * 5,
+        out_specs=[IN_VMEM] * 7,
         scratch_shapes=[pltpu.SemaphoreType.DMA((4,)), pltpu.SemaphoreType.DMA((2,))],
         compiler_params=pltpu.CompilerParams(vmem_limit_bytes=61 * 1024 * 1024),
         cost_estimate=pl.CostEstimate(flops=0, bytes_accessed=0, transcendentals=0),
@@ -269,20 +280,22 @@
     early, late = [[slab.reshape(-1, pair_count) for slab in slabs] for slabs in (early, late)]
 
     chi, own, virtual, occupied = pl.pallas_call(
-        functools.partial(chi_kernel, team, here, len(early), owners),
-        out_shape=[
-            jax.ShapeDtypeStruct((local_pairs, pair_count), jnp.float32),
-            pltpu.VMEM(own.shape, own.dtype),
-            jax.ShapeDtypeStruct((IRREPS, tiles * 128), jnp.float32),
-            jax.ShapeDtypeStruct((local_pairs, 128), jnp.float32),
-        ],
-        in_specs=[IN_HBM] * 2 + [IN_VMEM] * (3 + len(early) + team),
+        functools.partial(chi_kernel, team, first, len(early), owners),
+        out_shape=[jax.ShapeDtypeStruct((local_pairs, pair_count), jnp.float32), *prepared],
+        in_specs=[IN_HBM] * 2 + [IN_VMEM] * (5 + len(early) + team),
         out_specs=[IN_VMEM] * 4,
         scratch_shapes=[pltpu.SemaphoreType.DMA((2,))],
-        input_output_aliases={2: 1},
+        input_output_aliases={5: 1, 6: 2, 7: 3},
         compiler_params=params,
         cost_estimate=cost(bytes_accessed=2 * amplitudes.nbytes),
-    )(in_hbm(amplitudes), in_hbm(integrals), near(own), *energies, *early, *[near(far) for far in far_ints])
+    )(
+        in_hbm(amplitudes),
+        in_hbm(integrals),
+        *energies,
+        *[near(array) for array in (own, virtual, occupied)],
+        *early,
+        *[near(far) for far in far_ints],
+    )
     return pl.pallas_call(
         functools.partial(update_kernel, team, len(late), owners),
         out_shape=jax.ShapeDtypeStruct((local_pairs, width), jnp.bfloat16),

time: 14 us -> 14.1 us (level)
  waiting for transfers between devices: 1.22 us -> 2 us
  starting transfers between devices: 7.55 us -> 7.11 us
  Pallas kernels: 5.06 us -> 4.73 us
    ppermute x4, waiting for transfers between devices: 1.21 us -> 1.99 us  [permute(): return lax.ppermute(block, 'idx', [(d, hop(d)) for d in range(16)])]
    ppermute x4, starting transfers between devices: 6.98 us -> 6.53 us  [permute(): return lax.ppermute(block, 'idx', [(d, hop(d)) for d in range(16)])]
    pallas_call x2, Pallas kernels: 3.08 us -> 2.74 us  [the longest x1 1.81 us: on_device(): pl.pallas_call(functools.partial(load_kernel, team, first), out_shape=[*[...]
  transfers between devices with their start and end apart: 6 -> 6, of which waited for: 2 -> 2; matrix products, arithmetic and copies ran while one was open for 0% -> 0% of each run, Pallas kernels for 22% -> 20%
where the time goes in v8:
time: 14.1 us; the launch traced here: 13.9 us
  starting transfers between devices  7.11 us (50%)
  Pallas kernels  4.73 us (34%)
  waiting for transfers between devices  2 us (14%)
    ppermute x4, starting transfers between devices, permute(): return lax.ppermute(block, 'idx', [(d, hop(d)) for d in range(16)])  6.53 us
    ppermute x4, waiting for transfers between devices, permute(): return lax.ppermute(block, 'idx', [(d, hop(d)) for d in range(16)])  1.99 us
    pallas_call x1, Pallas kernels, on_device(): pl.pallas_call(functools.partial(update_kernel, team, len(late), owners),...  1.99 us
    pallas_call x1, Pallas kernels, on_device(): pl.pallas_call(functools.partial(load_kernel, team, first), out_shape=[*[...  1.81 us
    pallas_call x1, Pallas kernels, on_device(): pl.pallas_call(functools.partial(chi_kernel, team, first, len(early), own...  0.94 us
    ppermute x2, starting transfers between devices, team_exchange(): lax.ppermute(block, 'idx', [(d, d // team * team + (d - step) % team) for...  0.58 us
  transfers between devices with their start and end apart: 6, of which 2 were waited for; matrix products, arithmetic and copies ran while one was open for 0% of the time, Pallas kernels for 20%

profile of v8, /device:TPU:0, one launch (start us, length us, event | category | flops | bytes accessed | tf_op | source)
XLA Modules:
  0.0 13.9 jit_solution(10046648571006522262)
XLA Ops:
  0.0 0.5 %collective-permute-start = (bf16[1,8,16]{2,1,0:T(8,128)(2,1)}, bf16[1,8,16]{2,1,0:T(8,128)(2,1)S(1)}, u32[]{:S(2)}, u32[]{:S(2)}) collective-permute-start(bf16[1,8,16]{2,1,0:T(8,128)(2,1)} %refs_3_.1), channel_id=1, source_target_pairs={{0,1},{1,0},{2,3},{3,2},{4,5},{5,4},{6,7},{7,6},{8,9},{9,8},{10,11... | collective-permute-start | bytes 776 | tf_op jit(solution)/shard_map/ppermute | solution.py:212
  0.5 1.8 %shard_map.64 = (f32[800]{0:T(1024)S(1)}, f32[200]{0:T(256)S(1)}, s32[2,8]{1,0:T(2,128)S(1)}, bf16[1,8,16]{2,1,0:T(8,128)(2,1)S(1)}, bf16[2,8,80000]{2,1,0:T(8,1...) custom-call(f32[800]{0:T(1024)} %refs_0_.1, f32[200]{0:T(256)} %refs_1_.1, s32[2,8]{1,0:T(2,128)} %bitcast.9, ...), custom_call_target="tpu_custom_call" | custom-call | tf_op jit(solution)/shard_map/pallas_call | solution.py:264
  2.3 0.0 collective-permute-done
  2.3 0.1 collective-permute-start.2
  2.4 0.5 %collective-permute-start.5 = (bf16[8,80000]{1,0:T(8,128)(2,1)}, bf16[8,80000]{1,0:T(8,128)(2,1)S(1)}, u32[]{:S(2)}, u32[]{:S(2)}) collective-permute-start(bf16[8,80000]{1,0:T(8,128)(2,1)} %amps_hbm.1), channel_id=1, source_target_pairs={{0,1},{1,0},{2,3},{3,2},{4,5},{5,4},{6,7},{7,6},{8,9},{9,8},{10,11... | collective-permute-start | bytes 3840008 | tf_op jit(solution)/shard_map/ppermute | solution.py:187
  2.9 3.6 %collective-permute-start.1 = (bf16[2,8,16]{2,1,0:T(8,128)(2,1)S(1)}, bf16[2,8,16]{2,1,0:T(8,128)(2,1)S(1)}, u32[]{:S(2)}, u32[]{:S(2)}) collective-permute-start(bf16[2,8,16]{2,1,0:T(8,128)(2,1)S(1)} %get-tuple-element.34), channel_id=1, source_target_pairs={{0,6},{1,12},{2,4},{3,14},{4,2},{5,8},{6,0},{7,10},{8,5},{9,15},{1... | collective-permute-start | bytes 1544 | tf_op jit(solution)/shard_map/ppermute | solution.py:212
  6.5 0.0 collective-permute-start.3
  6.5 1.6 %collective-permute-done.1 = bf16[2,8,16]{2,1,0:T(8,128)(2,1)S(1)} collective-permute-done((bf16[2,8,16]{2,1,0:T(8,128)(2,1)S(1)}, bf16[2,8,16]{2,1,0:T(8,128)(2,1)S(1)}, u32[]{:S(2)}, u32[]{:S(2)}) %collective-permute-start.1) | collective-permute-done | bytes 544 | tf_op jit(solution)/shard_map/ppermute | solution.py:212
  8.1 2.5 %collective-permute-start.4 = (bf16[4,8,16]{2,1,0:T(8,128)(2,1)S(1)}, bf16[4,8,16]{2,1,0:T(8,128)(2,1)S(1)}, u32[]{:S(2)}, u32[]{:S(2)}) collective-permute-start(bf16[4,8,16]{2,1,0:T(8,128)(2,1)S(1)} %constant_dynamic-update-slice_fusion.2), channel_id=1, source_target_pairs={{0,8},{1,2},{2,10},{3,0},{4,12},{5,6},{6,14},{7,4},{8,11},{9,1},{1... | collective-permute-start | bytes 3080 | tf_op jit(solution)/shard_map/ppermute | solution.py:212
  10.6 0.0 collective-permute-done.2.refs_5_
  10.6 0.9 %shard_map.65 = (f32[8,16]{1,0:T(8,128)S(1)}, bf16[2,8,80000]{2,1,0:T(8,128)(2,1)S(1)}, f32[8,10240]{1,0:T(8,128)S(1)}, f32[8,128]{1,0:T(8,128)S(1)}) custom-call(bf16[8,80000]{1,0:T(8,128)(2,1)} %amps_hbm.1, bf16[8,80000]{1,0:T(8,128)(2,1)} %ints_hbm.1, ...), custom_call_target="tpu_custom_call", output_to_operand_aliasing={{1}: (5, {}), {2}: (6, {}), {3}: (7, {})} | custom-call | flops 20480000 | bytes 2560000 | tf_op jit(solution)/shard_map/pallas_call | solution.py:282
  11.5 0.0 collective-permute-done.3
  11.5 0.4 %collective-permute-done.4 = bf16[4,8,16]{2,1,0:T(8,128)(2,1)S(1)} collective-permute-done((bf16[4,8,16]{2,1,0:T(8,128)(2,1)S(1)}, bf16[4,8,16]{2,1,0:T(8,128)(2,1)S(1)}, u32[]{:S(2)}, u32[]{:S(2)}) %collective-permute-start.4) | collective-permute-done | bytes 1056 | tf_op jit(solution)/shard_map/ppermute | solution.py:212
  11.9 0.0 collective-permute-done.5.refs_3_
  11.9 2.0 %shard_map.66 = bf16[8,80000]{1,0:T(8,128)(2,1)} custom-call(f32[8,16]{1,0:T(8,128)S(1)} %get-tuple-element.28.chi_ref, f32[8,10240]{1,0:T(8,128)S(1)} %get-tuple-element.29.virtual_ref, f32[8,128]{1,0:T(8,128)S(1)} %get-tuple-element.30.occupied_ref, bf16[16,16]{1,0:T(8,128)(2,1)S(1)} %bitcast.8, bf16[32,16]{1,0:T(8,128)(2,1)S(1)} %bitcast.7, ...), custom_call_target="tpu_custom_call" | custom-call | flops 20480000 | bytes 5120000 | tf_op jit(solution)/shard_map/pallas_call | solution.py:299
  (3 shorter events, 0.0 us)
Async XLA Ops:
  0.0 2.3 %collective-permute-start = (bf16[1,8,16]{2,1,0:T(8,128)(2,1)}, bf16[1,8,16]{2,1,0:T(8,128)(2,1)S(1)}, u32[]{:S(2)}, u32[]{:S(2)}) collective-permute-start(bf16[1,8,16]{2,1,0:T(8,128)(2,1)} %refs_3_.1), channel_id=1, source_target_pairs={{0,1},{1,0},{2,3},{3,2},{4,5},{5,4},{6,7},{7,6},{8,9},{9,8},{10,11... | collective-permute-start | bytes 776 | tf_op jit(solution)/shard_map/ppermute | solution.py:212
  2.3 8.3 %collective-permute-start.2 = (bf16[8,80000]{1,0:T(8,128)(2,1)}, bf16[8,80000]{1,0:T(8,128)(2,1)S(1)}, u32[]{:S(2)}, u32[]{:S(2)}) collective-permute-start(bf16[8,80000]{1,0:T(8,128)(2,1)} %ints_hbm.1), channel_id=1, source_target_pairs={{0,1},{1,0},{2,3},{3,2},{4,5},{5,4},{6,7},{7,6},{8,9},{9,8},{10,11... | collective-permute-start | bytes 3840008 | tf_op jit(solution)/shard_map/ppermute | solution.py:187
  2.4 9.5 %collective-permute-start.5 = (bf16[8,80000]{1,0:T(8,128)(2,1)}, bf16[8,80000]{1,0:T(8,128)(2,1)S(1)}, u32[]{:S(2)}, u32[]{:S(2)}) collective-permute-start(bf16[8,80000]{1,0:T(8,128)(2,1)} %amps_hbm.1), channel_id=1, source_target_pairs={{0,1},{1,0},{2,3},{3,2},{4,5},{5,4},{6,7},{7,6},{8,9},{9,8},{10,11... | collective-permute-start | bytes 3840008 | tf_op jit(solution)/shard_map/ppermute | solution.py:187
  2.9 5.2 %collective-permute-start.1 = (bf16[2,8,16]{2,1,0:T(8,128)(2,1)S(1)}, bf16[2,8,16]{2,1,0:T(8,128)(2,1)S(1)}, u32[]{:S(2)}, u32[]{:S(2)}) collective-permute-start(bf16[2,8,16]{2,1,0:T(8,128)(2,1)S(1)} %get-tuple-element.34), channel_id=1, source_target_pairs={{0,6},{1,12},{2,4},{3,14},{4,2},{5,8},{6,0},{7,10},{8,5},{9,15},{1... | collective-permute-start | bytes 1544 | tf_op jit(solution)/shard_map/ppermute | solution.py:212
  6.5 5.0 %collective-permute-start.3 = (bf16[2,8,16]{2,1,0:T(8,128)(2,1)S(1)}, bf16[2,8,16]{2,1,0:T(8,128)(2,1)S(1)}, u32[]{:S(2)}, u32[]{:S(2)}) collective-permute-start(bf16[2,8,16]{2,1,0:T(8,128)(2,1)S(1)} %get-tuple-element.34), channel_id=1, source_target_pairs={{0,4},{1,10},{2,6},{3,8},{4,0},{5,14},{6,2},{7,12},{8,3},{9,13},{1... | collective-permute-start | bytes 1544 | tf_op jit(solution)/shard_map/ppermute | solution.py:212
  8.1 3.8 %collective-permute-start.4 = (bf16[4,8,16]{2,1,0:T(8,128)(2,1)S(1)}, bf16[4,8,16]{2,1,0:T(8,128)(2,1)S(1)}, u32[]{:S(2)}, u32[]{:S(2)}) collective-permute-start(bf16[4,8,16]{2,1,0:T(8,128)(2,1)S(1)} %constant_dynamic-update-slice_fusion.2), channel_id=1, source_target_pairs={{0,8},{1,2},{2,10},{3,0},{4,12},{5,6},{6,14},{7,4},{8,11},{9,1},{1... | collective-permute-start | bytes 3080 | tf_op jit(solution)/shard_map/ppermute | solution.py:212

commit v9 on v8

--- a/solution.py
+++ b/solution.py
@@ -171,8 +171,8 @@
     for g, (start, end) in enumerate(itertools.pairwise(irrep_tiles(math.isqrt(width // IRREPS)))):
         cut = pl.ds(start * 128, (end - start) * 128)
         block = jnp.concatenate([ref[:, cut] for ref in amps], axis=0)
-        ladder = jnp.dot(chi_half, block, preferred_element_type=jnp.float32).astype(jnp.bfloat16)
-        total = ints_ref[:, cut].astype(jnp.float32) + ladder.astype(jnp.float32)
+        ladder = jnp.dot(chi_half, block, preferred_element_type=jnp.float32)
+        total = ints_ref[:, cut].astype(jnp.float32) + ladder
         denominator = virtual_ref[g : g + 1, : (end - start) * 128] - occupied
         buffer[:, cut] = (total / denominator).astype(jnp.bfloat16)
         copy = pltpu.make_async_copy(buffer.at[:, cut], out_ref.at[:, cut], sems.at[g])

time: 14.1 us -> 14 us (level)
  no operation moved by 1% of the time
where the time goes in v9:
time: 14 us; the launch traced here: 13.8 us
  starting transfers between devices  7.11 us (51%)
  Pallas kernels  4.6 us (33%)
  waiting for transfers between devices  2 us (14%)
    ppermute x4, starting transfers between devices, permute(): return lax.ppermute(block, 'idx', [(d, hop(d)) for d in range(16)])  6.53 us
    ppermute x4, waiting for transfers between devices, permute(): return lax.ppermute(block, 'idx', [(d, hop(d)) for d in range(16)])  1.99 us
    pallas_call x1, Pallas kernels, on_device(): pl.pallas_call(functools.partial(update_kernel, team, len(late), owners),...  1.86 us
    pallas_call x1, Pallas kernels, on_device(): pl.pallas_call(functools.partial(load_kernel, team, first), out_shape=[*[...  1.81 us
    pallas_call x1, Pallas kernels, on_device(): pl.pallas_call(functools.partial(chi_kernel, team, first, len(early), own...  0.94 us
    ppermute x2, starting transfers between devices, team_exchange(): lax.ppermute(block, 'idx', [(d, d // team * team + (d - step) % team) for...  0.58 us
  transfers between devices with their start and end apart: 6, of which 2 were waited for; matrix products, arithmetic and copies ran while one was open for 0% of the time, Pallas kernels for 20%

profile of v9, /device:TPU:0, one launch (start us, length us, event | category | flops | bytes accessed | tf_op | source)
XLA Modules:
  0.0 13.8 jit_solution(2074056415500120312)
XLA Ops:
  0.0 0.5 %collective-permute-start = (bf16[1,8,16]{2,1,0:T(8,128)(2,1)}, bf16[1,8,16]{2,1,0:T(8,128)(2,1)S(1)}, u32[]{:S(2)}, u32[]{:S(2)}) collective-permute-start(bf16[1,8,16]{2,1,0:T(8,128)(2,1)} %refs_3_.1), channel_id=1, source_target_pairs={{0,1},{1,0},{2,3},{3,2},{4,5},{5,4},{6,7},{7,6},{8,9},{9,8},{10,11... | collective-permute-start | bytes 776 | tf_op jit(solution)/shard_map/ppermute | solution.py:212
  0.5 1.8 %shard_map.64 = (f32[800]{0:T(1024)S(1)}, f32[200]{0:T(256)S(1)}, s32[2,8]{1,0:T(2,128)S(1)}, bf16[1,8,16]{2,1,0:T(8,128)(2,1)S(1)}, bf16[2,8,80000]{2,1,0:T(8,1...) custom-call(f32[800]{0:T(1024)} %refs_0_.1, f32[200]{0:T(256)} %refs_1_.1, s32[2,8]{1,0:T(2,128)} %bitcast.9, ...), custom_call_target="tpu_custom_call" | custom-call | tf_op jit(solution)/shard_map/pallas_call | solution.py:264
  2.3 0.0 collective-permute-done
  2.3 0.1 collective-permute-start.2
  2.4 0.5 %collective-permute-start.5 = (bf16[8,80000]{1,0:T(8,128)(2,1)}, bf16[8,80000]{1,0:T(8,128)(2,1)S(1)}, u32[]{:S(2)}, u32[]{:S(2)}) collective-permute-start(bf16[8,80000]{1,0:T(8,128)(2,1)} %amps_hbm.1), channel_id=1, source_target_pairs={{0,1},{1,0},{2,3},{3,2},{4,5},{5,4},{6,7},{7,6},{8,9},{9,8},{10,11... | collective-permute-start | bytes 3840008 | tf_op jit(solution)/shard_map/ppermute | solution.py:187
  2.9 3.6 %collective-permute-start.1 = (bf16[2,8,16]{2,1,0:T(8,128)(2,1)S(1)}, bf16[2,8,16]{2,1,0:T(8,128)(2,1)S(1)}, u32[]{:S(2)}, u32[]{:S(2)}) collective-permute-start(bf16[2,8,16]{2,1,0:T(8,128)(2,1)S(1)} %get-tuple-element.34), channel_id=1, source_target_pairs={{0,6},{1,12},{2,4},{3,14},{4,2},{5,8},{6,0},{7,10},{8,5},{9,15},{1... | collective-permute-start | bytes 1544 | tf_op jit(solution)/shard_map/ppermute | solution.py:212
  6.5 0.0 collective-permute-start.3
  6.5 1.6 %collective-permute-done.1 = bf16[2,8,16]{2,1,0:T(8,128)(2,1)S(1)} collective-permute-done((bf16[2,8,16]{2,1,0:T(8,128)(2,1)S(1)}, bf16[2,8,16]{2,1,0:T(8,128)(2,1)S(1)}, u32[]{:S(2)}, u32[]{:S(2)}) %collective-permute-start.1) | collective-permute-done | bytes 544 | tf_op jit(solution)/shard_map/ppermute | solution.py:212
  8.1 2.5 %collective-permute-start.4 = (bf16[4,8,16]{2,1,0:T(8,128)(2,1)S(1)}, bf16[4,8,16]{2,1,0:T(8,128)(2,1)S(1)}, u32[]{:S(2)}, u32[]{:S(2)}) collective-permute-start(bf16[4,8,16]{2,1,0:T(8,128)(2,1)S(1)} %constant_dynamic-update-slice_fusion.2), channel_id=1, source_target_pairs={{0,8},{1,2},{2,10},{3,0},{4,12},{5,6},{6,14},{7,4},{8,11},{9,1},{1... | collective-permute-start | bytes 3080 | tf_op jit(solution)/shard_map/ppermute | solution.py:212
  10.6 0.0 collective-permute-done.2.refs_5_
  10.6 0.9 %shard_map.65 = (f32[8,16]{1,0:T(8,128)S(1)}, bf16[2,8,80000]{2,1,0:T(8,128)(2,1)S(1)}, f32[8,10240]{1,0:T(8,128)S(1)}, f32[8,128]{1,0:T(8,128)S(1)}) custom-call(bf16[8,80000]{1,0:T(8,128)(2,1)} %amps_hbm.1, bf16[8,80000]{1,0:T(8,128)(2,1)} %ints_hbm.1, ...), custom_call_target="tpu_custom_call", output_to_operand_aliasing={{1}: (5, {}), {2}: (6, {}), {3}: (7, {})} | custom-call | flops 20480000 | bytes 2560000 | tf_op jit(solution)/shard_map/pallas_call | solution.py:282
  11.5 0.0 collective-permute-done.3
  11.5 0.4 %collective-permute-done.4 = bf16[4,8,16]{2,1,0:T(8,128)(2,1)S(1)} collective-permute-done((bf16[4,8,16]{2,1,0:T(8,128)(2,1)S(1)}, bf16[4,8,16]{2,1,0:T(8,128)(2,1)S(1)}, u32[]{:S(2)}, u32[]{:S(2)}) %collective-permute-start.4) | collective-permute-done | bytes 1056 | tf_op jit(solution)/shard_map/ppermute | solution.py:212
  11.9 0.0 collective-permute-done.5.refs_3_
  11.9 1.9 %shard_map.66 = bf16[8,80000]{1,0:T(8,128)(2,1)} custom-call(f32[8,16]{1,0:T(8,128)S(1)} %get-tuple-element.28.chi_ref, f32[8,10240]{1,0:T(8,128)S(1)} %get-tuple-element.29.virtual_ref, f32[8,128]{1,0:T(8,128)S(1)} %get-tuple-element.30.occupied_ref, bf16[16,16]{1,0:T(8,128)(2,1)S(1)} %bitcast.8, bf16[32,16]{1,0:T(8,128)(2,1)S(1)} %bitcast.7, ...), custom_call_target="tpu_custom_call" | custom-call | flops 20480000 | bytes 5120000 | tf_op jit(solution)/shard_map/pallas_call | solution.py:299
  (3 shorter events, 0.0 us)
Async XLA Ops:
  0.0 2.3 %collective-permute-start = (bf16[1,8,16]{2,1,0:T(8,128)(2,1)}, bf16[1,8,16]{2,1,0:T(8,128)(2,1)S(1)}, u32[]{:S(2)}, u32[]{:S(2)}) collective-permute-start(bf16[1,8,16]{2,1,0:T(8,128)(2,1)} %refs_3_.1), channel_id=1, source_target_pairs={{0,1},{1,0},{2,3},{3,2},{4,5},{5,4},{6,7},{7,6},{8,9},{9,8},{10,11... | collective-permute-start | bytes 776 | tf_op jit(solution)/shard_map/ppermute | solution.py:212
  2.3 8.3 %collective-permute-start.2 = (bf16[8,80000]{1,0:T(8,128)(2,1)}, bf16[8,80000]{1,0:T(8,128)(2,1)S(1)}, u32[]{:S(2)}, u32[]{:S(2)}) collective-permute-start(bf16[8,80000]{1,0:T(8,128)(2,1)} %ints_hbm.1), channel_id=1, source_target_pairs={{0,1},{1,0},{2,3},{3,2},{4,5},{5,4},{6,7},{7,6},{8,9},{9,8},{10,11... | collective-permute-start | bytes 3840008 | tf_op jit(solution)/shard_map/ppermute | solution.py:187
  2.4 9.5 %collective-permute-start.5 = (bf16[8,80000]{1,0:T(8,128)(2,1)}, bf16[8,80000]{1,0:T(8,128)(2,1)S(1)}, u32[]{:S(2)}, u32[]{:S(2)}) collective-permute-start(bf16[8,80000]{1,0:T(8,128)(2,1)} %amps_hbm.1), channel_id=1, source_target_pairs={{0,1},{1,0},{2,3},{3,2},{4,5},{5,4},{6,7},{7,6},{8,9},{9,8},{10,11... | collective-permute-start | bytes 3840008 | tf_op jit(solution)/shard_map/ppermute | solution.py:187
  2.9 5.2 %collective-permute-start.1 = (bf16[2,8,16]{2,1,0:T(8,128)(2,1)S(1)}, bf16[2,8,16]{2,1,0:T(8,128)(2,1)S(1)}, u32[]{:S(2)}, u32[]{:S(2)}) collective-permute-start(bf16[2,8,16]{2,1,0:T(8,128)(2,1)S(1)} %get-tuple-element.34), channel_id=1, source_target_pairs={{0,6},{1,12},{2,4},{3,14},{4,2},{5,8},{6,0},{7,10},{8,5},{9,15},{1... | collective-permute-start | bytes 1544 | tf_op jit(solution)/shard_map/ppermute | solution.py:212
  6.5 5.0 %collective-permute-start.3 = (bf16[2,8,16]{2,1,0:T(8,128)(2,1)S(1)}, bf16[2,8,16]{2,1,0:T(8,128)(2,1)S(1)}, u32[]{:S(2)}, u32[]{:S(2)}) collective-permute-start(bf16[2,8,16]{2,1,0:T(8,128)(2,1)S(1)} %get-tuple-element.34), channel_id=1, source_target_pairs={{0,4},{1,10},{2,6},{3,8},{4,0},{5,14},{6,2},{7,12},{8,3},{9,13},{1... | collective-permute-start | bytes 1544 | tf_op jit(solution)/shard_map/ppermute | solution.py:212
  8.1 3.8 %collective-permute-start.4 = (bf16[4,8,16]{2,1,0:T(8,128)(2,1)S(1)}, bf16[4,8,16]{2,1,0:T(8,128)(2,1)S(1)}, u32[]{:S(2)}, u32[]{:S(2)}) collective-permute-start(bf16[4,8,16]{2,1,0:T(8,128)(2,1)S(1)} %constant_dynamic-update-slice_fusion.2), channel_id=1, source_target_pairs={{0,8},{1,2},{2,10},{3,0},{4,12},{5,6},{6,14},{7,4},{8,11},{9,1},{1... | collective-permute-start | bytes 3080 | tf_op jit(solution)/shard_map/ppermute | solution.py:212

commit v10 on v9

--- a/solution.py
+++ b/solution.py
@@ -118,17 +118,19 @@
 
 def bare_rows(team, pairs, stack, held, me):
     symmetry, rank = me // team, me % team
-    lane = lax.broadcasted_iota(jnp.int32, (pairs, stack.shape[0]), 1)
-    owner = lane
-    if held is not None:
-        wide = stack.shape[0] // len(held)
-        owner = jnp.full(lane.shape, -1, jnp.int32)
-        for slot, row in enumerate(held):
-            owner = jnp.where(lane == slot * wide + symmetry, row, owner)
-    pick = owner == rank * pairs + lax.broadcasted_iota(jnp.int32, lane.shape, 0)
-    rows = jnp.dot(pick.astype(jnp.bfloat16), stack, preferred_element_type=jnp.float32)
     if held is None:
-        return rows
+        lane = lax.broadcasted_iota(jnp.int32, (pairs, stack.shape[0]), 1)
+        pick = lane == rank * pairs + lax.broadcasted_iota(jnp.int32, lane.shape, 0)
+        return jnp.dot(pick.astype(jnp.bfloat16), stack, preferred_element_type=jnp.float32)
+    wide = stack.shape[0] // len(held)
+    values = stack.astype(jnp.float32)
+    place = lax.broadcasted_iota(jnp.int32, (wide, stack.shape[1]), 0)
+    target = lax.broadcasted_iota(jnp.int32, (pairs, stack.shape[1]), 0) + rank * pairs
+    rows = jnp.zeros(target.shape, jnp.float32)
+    for slot, row in enumerate(held):
+        here = values[slot * wide : (slot + 1) * wide]
+        here = jnp.sum(jnp.where(place == symmetry, here, 0.0), axis=0, keepdims=True)
+        rows = jnp.where(target == row, here, rows)
     turned = rows
     for other in range(1, team):
         cut = other * pairs

time: 14 us -> 13.8 us (0.986)
  no operation moved by 1% of the time
where the time goes in v10:
time: 13.8 us; the launch traced here: 13.7 us
  starting transfers between devices  7.11 us (52%)
  Pallas kernels  4.48 us (32%)
  waiting for transfers between devices  2 us (14%)
    ppermute x4, starting transfers between devices, permute(): return lax.ppermute(block, 'idx', [(d, hop(d)) for d in range(16)])  6.53 us
    ppermute x4, waiting for transfers between devices, permute(): return lax.ppermute(block, 'idx', [(d, hop(d)) for d in range(16)])  1.99 us
    pallas_call x1, Pallas kernels, on_device(): pl.pallas_call(functools.partial(load_kernel, team, first), out_shape=[*[...  1.81 us
    pallas_call x1, Pallas kernels, on_device(): pl.pallas_call(functools.partial(update_kernel, team, len(late), owners),...  1.74 us
    pallas_call x1, Pallas kernels, on_device(): pl.pallas_call(functools.partial(chi_kernel, team, first, len(early), own...  0.94 us
    ppermute x2, starting transfers between devices, team_exchange(): lax.ppermute(block, 'idx', [(d, d // team * team + (d - step) % team) for...  0.58 us
  transfers between devices with their start and end apart: 6, of which 2 were waited for; matrix products, arithmetic and copies ran while one was open for 0% of the time, Pallas kernels for 20%

profile of v10, /device:TPU:0, one launch (start us, length us, event | category | flops | bytes accessed | tf_op | source)
XLA Modules:
  0.0 13.7 jit_solution(1289307457566682250)
XLA Ops:
  0.0 0.5 %collective-permute-start = (bf16[1,8,16]{2,1,0:T(8,128)(2,1)}, bf16[1,8,16]{2,1,0:T(8,128)(2,1)S(1)}, u32[]{:S(2)}, u32[]{:S(2)}) collective-permute-start(bf16[1,8,16]{2,1,0:T(8,128)(2,1)} %refs_3_.1), channel_id=1, source_target_pairs={{0,1},{1,0},{2,3},{3,2},{4,5},{5,4},{6,7},{7,6},{8,9},{9,8},{10,11... | collective-permute-start | bytes 776 | tf_op jit(solution)/shard_map/ppermute | solution.py:214
  0.5 1.8 %shard_map.64 = (f32[800]{0:T(1024)S(1)}, f32[200]{0:T(256)S(1)}, s32[2,8]{1,0:T(2,128)S(1)}, bf16[1,8,16]{2,1,0:T(8,128)(2,1)S(1)}, bf16[2,8,80000]{2,1,0:T(8,1...) custom-call(f32[800]{0:T(1024)} %refs_0_.1, f32[200]{0:T(256)} %refs_1_.1, s32[2,8]{1,0:T(2,128)} %bitcast.9, ...), custom_call_target="tpu_custom_call" | custom-call | tf_op jit(solution)/shard_map/pallas_call | solution.py:266
  2.3 0.0 collective-permute-done
  2.3 0.1 collective-permute-start.2
  2.4 0.5 %collective-permute-start.5 = (bf16[8,80000]{1,0:T(8,128)(2,1)}, bf16[8,80000]{1,0:T(8,128)(2,1)S(1)}, u32[]{:S(2)}, u32[]{:S(2)}) collective-permute-start(bf16[8,80000]{1,0:T(8,128)(2,1)} %amps_hbm.1), channel_id=1, source_target_pairs={{0,1},{1,0},{2,3},{3,2},{4,5},{5,4},{6,7},{7,6},{8,9},{9,8},{10,11... | collective-permute-start | bytes 3840008 | tf_op jit(solution)/shard_map/ppermute | solution.py:189
  2.9 3.6 %collective-permute-start.1 = (bf16[2,8,16]{2,1,0:T(8,128)(2,1)S(1)}, bf16[2,8,16]{2,1,0:T(8,128)(2,1)S(1)}, u32[]{:S(2)}, u32[]{:S(2)}) collective-permute-start(bf16[2,8,16]{2,1,0:T(8,128)(2,1)S(1)} %get-tuple-element.34), channel_id=1, source_target_pairs={{0,6},{1,12},{2,4},{3,14},{4,2},{5,8},{6,0},{7,10},{8,5},{9,15},{1... | collective-permute-start | bytes 1544 | tf_op jit(solution)/shard_map/ppermute | solution.py:214
  6.5 0.0 collective-permute-start.3
  6.5 1.6 %collective-permute-done.1 = bf16[2,8,16]{2,1,0:T(8,128)(2,1)S(1)} collective-permute-done((bf16[2,8,16]{2,1,0:T(8,128)(2,1)S(1)}, bf16[2,8,16]{2,1,0:T(8,128)(2,1)S(1)}, u32[]{:S(2)}, u32[]{:S(2)}) %collective-permute-start.1) | collective-permute-done | bytes 544 | tf_op jit(solution)/shard_map/ppermute | solution.py:214
  8.1 2.5 %collective-permute-start.4 = (bf16[4,8,16]{2,1,0:T(8,128)(2,1)S(1)}, bf16[4,8,16]{2,1,0:T(8,128)(2,1)S(1)}, u32[]{:S(2)}, u32[]{:S(2)}) collective-permute-start(bf16[4,8,16]{2,1,0:T(8,128)(2,1)S(1)} %constant_dynamic-update-slice_fusion.2), channel_id=1, source_target_pairs={{0,8},{1,2},{2,10},{3,0},{4,12},{5,6},{6,14},{7,4},{8,11},{9,1},{1... | collective-permute-start | bytes 3080 | tf_op jit(solution)/shard_map/ppermute | solution.py:214
  10.6 0.0 collective-permute-done.2.refs_5_
  10.6 0.9 %shard_map.65 = (f32[8,16]{1,0:T(8,128)S(1)}, bf16[2,8,80000]{2,1,0:T(8,128)(2,1)S(1)}, f32[8,10240]{1,0:T(8,128)S(1)}, f32[8,128]{1,0:T(8,128)S(1)}) custom-call(bf16[8,80000]{1,0:T(8,128)(2,1)} %amps_hbm.1, bf16[8,80000]{1,0:T(8,128)(2,1)} %ints_hbm.1, ...), custom_call_target="tpu_custom_call", output_to_operand_aliasing={{1}: (5, {}), {2}: (6, {}), {3}: (7, {})} | custom-call | flops 20480000 | bytes 2560000 | tf_op jit(solution)/shard_map/pallas_call | solution.py:284
  11.5 0.0 collective-permute-done.3
  11.5 0.4 %collective-permute-done.4 = bf16[4,8,16]{2,1,0:T(8,128)(2,1)S(1)} collective-permute-done((bf16[4,8,16]{2,1,0:T(8,128)(2,1)S(1)}, bf16[4,8,16]{2,1,0:T(8,128)(2,1)S(1)}, u32[]{:S(2)}, u32[]{:S(2)}) %collective-permute-start.4) | collective-permute-done | bytes 1056 | tf_op jit(solution)/shard_map/ppermute | solution.py:214
  11.9 0.0 collective-permute-done.5.refs_3_
  11.9 1.7 %shard_map.66 = bf16[8,80000]{1,0:T(8,128)(2,1)} custom-call(f32[8,16]{1,0:T(8,128)S(1)} %get-tuple-element.28.chi_ref, f32[8,10240]{1,0:T(8,128)S(1)} %get-tuple-element.29.virtual_ref, f32[8,128]{1,0:T(8,128)S(1)} %get-tuple-element.30.occupied_ref, bf16[16,16]{1,0:T(8,128)(2,1)S(1)} %bitcast.8, bf16[32,16]{1,0:T(8,128)(2,1)S(1)} %bitcast.7, ...), custom_call_target="tpu_custom_call" | custom-call | flops 20480000 | bytes 5120000 | tf_op jit(solution)/shard_map/pallas_call | solution.py:301
  (3 shorter events, 0.0 us)
Async XLA Ops:
  0.0 2.3 %collective-permute-start = (bf16[1,8,16]{2,1,0:T(8,128)(2,1)}, bf16[1,8,16]{2,1,0:T(8,128)(2,1)S(1)}, u32[]{:S(2)}, u32[]{:S(2)}) collective-permute-start(bf16[1,8,16]{2,1,0:T(8,128)(2,1)} %refs_3_.1), channel_id=1, source_target_pairs={{0,1},{1,0},{2,3},{3,2},{4,5},{5,4},{6,7},{7,6},{8,9},{9,8},{10,11... | collective-permute-start | bytes 776 | tf_op jit(solution)/shard_map/ppermute | solution.py:214
  2.3 8.3 %collective-permute-start.2 = (bf16[8,80000]{1,0:T(8,128)(2,1)}, bf16[8,80000]{1,0:T(8,128)(2,1)S(1)}, u32[]{:S(2)}, u32[]{:S(2)}) collective-permute-start(bf16[8,80000]{1,0:T(8,128)(2,1)} %ints_hbm.1), channel_id=1, source_target_pairs={{0,1},{1,0},{2,3},{3,2},{4,5},{5,4},{6,7},{7,6},{8,9},{9,8},{10,11... | collective-permute-start | bytes 3840008 | tf_op jit(solution)/shard_map/ppermute | solution.py:189
  2.4 9.5 %collective-permute-start.5 = (bf16[8,80000]{1,0:T(8,128)(2,1)}, bf16[8,80000]{1,0:T(8,128)(2,1)S(1)}, u32[]{:S(2)}, u32[]{:S(2)}) collective-permute-start(bf16[8,80000]{1,0:T(8,128)(2,1)} %amps_hbm.1), channel_id=1, source_target_pairs={{0,1},{1,0},{2,3},{3,2},{4,5},{5,4},{6,7},{7,6},{8,9},{9,8},{10,11... | collective-permute-start | bytes 3840008 | tf_op jit(solution)/shard_map/ppermute | solution.py:189
  2.9 5.2 %collective-permute-start.1 = (bf16[2,8,16]{2,1,0:T(8,128)(2,1)S(1)}, bf16[2,8,16]{2,1,0:T(8,128)(2,1)S(1)}, u32[]{:S(2)}, u32[]{:S(2)}) collective-permute-start(bf16[2,8,16]{2,1,0:T(8,128)(2,1)S(1)} %get-tuple-element.34), channel_id=1, source_target_pairs={{0,6},{1,12},{2,4},{3,14},{4,2},{5,8},{6,0},{7,10},{8,5},{9,15},{1... | collective-permute-start | bytes 1544 | tf_op jit(solution)/shard_map/ppermute | solution.py:214
  6.5 5.0 %collective-permute-start.3 = (bf16[2,8,16]{2,1,0:T(8,128)(2,1)S(1)}, bf16[2,8,16]{2,1,0:T(8,128)(2,1)S(1)}, u32[]{:S(2)}, u32[]{:S(2)}) collective-permute-start(bf16[2,8,16]{2,1,0:T(8,128)(2,1)S(1)} %get-tuple-element.34), channel_id=1, source_target_pairs={{0,4},{1,10},{2,6},{3,8},{4,0},{5,14},{6,2},{7,12},{8,3},{9,13},{1... | collective-permute-start | bytes 1544 | tf_op jit(solution)/shard_map/ppermute | solution.py:214
  8.1 3.8 %collective-permute-start.4 = (bf16[4,8,16]{2,1,0:T(8,128)(2,1)S(1)}, bf16[4,8,16]{2,1,0:T(8,128)(2,1)S(1)}, u32[]{:S(2)}, u32[]{:S(2)}) collective-permute-start(bf16[4,8,16]{2,1,0:T(8,128)(2,1)S(1)} %constant_dynamic-update-slice_fusion.2), channel_id=1, source_target_pairs={{0,8},{1,2},{2,10},{3,0},{4,12},{5,6},{6,14},{7,4},{8,11},{9,1},{1... | collective-permute-start | bytes 3080 | tf_op jit(solution)/shard_map/ppermute | solution.py:214

commit v11 on v10

--- a/solution.py
+++ b/solution.py
@@ -124,13 +124,11 @@
         return jnp.dot(pick.astype(jnp.bfloat16), stack, preferred_element_type=jnp.float32)
     wide = stack.shape[0] // len(held)
     values = stack.astype(jnp.float32)
-    place = lax.broadcasted_iota(jnp.int32, (wide, stack.shape[1]), 0)
     target = lax.broadcasted_iota(jnp.int32, (pairs, stack.shape[1]), 0) + rank * pairs
     rows = jnp.zeros(target.shape, jnp.float32)
     for slot, row in enumerate(held):
         here = values[slot * wide : (slot + 1) * wide]
-        here = jnp.sum(jnp.where(place == symmetry, here, 0.0), axis=0, keepdims=True)
-        rows = jnp.where(target == row, here, rows)
+        rows = jnp.where(target == row, pltpu.roll(here, (row - symmetry) & (wide - 1), 0), rows)
     turned = rows
     for other in range(1, team):
         cut = other * pairs
@@ -171,15 +169,17 @@
     width = ints_ref.shape[1]
     copies = []
     for g, (start, end) in enumerate(itertools.pairwise(irrep_tiles(math.isqrt(width // IRREPS)))):
-        cut = pl.ds(start * 128, (end - start) * 128)
-        block = jnp.concatenate([ref[:, cut] for ref in amps], axis=0)
-        ladder = jnp.dot(chi_half, block, preferred_element_type=jnp.float32)
-        total = ints_ref[:, cut].astype(jnp.float32) + ladder
-        denominator = virtual_ref[g : g + 1, : (end - start) * 128] - occupied
-        buffer[:, cut] = (total / denominator).astype(jnp.bfloat16)
-        copy = pltpu.make_async_copy(buffer.at[:, cut], out_ref.at[:, cut], sems.at[g])
-        copy.start()
-        copies.append(copy)
+        parts = [(start, end)] if g < IRREPS - 1 else [(start, (start + 2 * end) // 3), ((start + 2 * end) // 3, end)]
+        for part, (low, high) in enumerate(parts):
+            cut = pl.ds(low * 128, (high - low) * 128)
+            block = jnp.concatenate([ref[:, cut] for ref in amps], axis=0)
+            ladder = jnp.dot(chi_half, block, preferred_element_type=jnp.float32)
+            total = ints_ref[:, cut].astype(jnp.float32) + ladder
+            denominator = virtual_ref[g : g + 1, (low - start) * 128 : (high - start) * 128] - occupied
+            buffer[:, cut] = (total / denominator).astype(jnp.bfloat16)
+            copy = pltpu.make_async_copy(buffer.at[:, cut], out_ref.at[:, cut], sems.at[g + part])
+            copy.start()
+            copies.append(copy)
     for copy in copies:
         copy.wait()
 
@@ -305,7 +305,7 @@
         out_specs=IN_HBM,
         scratch_shapes=[
             pltpu.VMEM((local_pairs, width), jnp.bfloat16),
-            pltpu.SemaphoreType.DMA((IRREPS,)),
+            pltpu.SemaphoreType.DMA((IRREPS + 1,)),
         ],
         compiler_params=params,
         cost_estimate=cost(bytes_accessed=4 * local_pairs * width * 2),

time: 13.8 us -> 13.8 us (level)
  no operation moved by 1% of the time
where the time goes in v11:
time: 13.8 us; the launch traced here: 13.6 us
  starting transfers between devices  7.11 us (52%)
  Pallas kernels  4.46 us (32%)
  waiting for transfers between devices  2 us (14%)
    ppermute x4, starting transfers between devices, permute(): return lax.ppermute(block, 'idx', [(d, hop(d)) for d in range(16)])  6.53 us
    ppermute x4, waiting for transfers between devices, permute(): return lax.ppermute(block, 'idx', [(d, hop(d)) for d in range(16)])  1.99 us
    pallas_call x1, Pallas kernels, on_device(): pl.pallas_call(functools.partial(load_kernel, team, first), out_shape=[*[...  1.81 us
    pallas_call x1, Pallas kernels, on_device(): pl.pallas_call(functools.partial(update_kernel, team, len(late), owners),...  1.72 us
    pallas_call x1, Pallas kernels, on_device(): pl.pallas_call(functools.partial(chi_kernel, team, first, len(early), own...  0.94 us
    ppermute x2, starting transfers between devices, team_exchange(): lax.ppermute(block, 'idx', [(d, d // team * team + (d - step) % team) for...  0.58 us
  transfers between devices with their start and end apart: 6, of which 2 were waited for; matrix products, arithmetic and copies ran while one was open for 0% of the time, Pallas kernels for 20%

profile of v11, /device:TPU:0, one launch (start us, length us, event | category | flops | bytes accessed | tf_op | source)
XLA Modules:
  0.0 13.6 jit_solution(17191379182266863298)
XLA Ops:
  0.0 0.5 %collective-permute-start = (bf16[1,8,16]{2,1,0:T(8,128)(2,1)}, bf16[1,8,16]{2,1,0:T(8,128)(2,1)S(1)}, u32[]{:S(2)}, u32[]{:S(2)}) collective-permute-start(bf16[1,8,16]{2,1,0:T(8,128)(2,1)} %refs_3_.1), channel_id=1, source_target_pairs={{0,1},{1,0},{2,3},{3,2},{4,5},{5,4},{6,7},{7,6},{8,9},{9,8},{10,11... | collective-permute-start | bytes 776 | tf_op jit(solution)/shard_map/ppermute | solution.py:214
  0.5 1.8 %shard_map.64 = (f32[800]{0:T(1024)S(1)}, f32[200]{0:T(256)S(1)}, s32[2,8]{1,0:T(2,128)S(1)}, bf16[1,8,16]{2,1,0:T(8,128)(2,1)S(1)}, bf16[2,8,80000]{2,1,0:T(8,1...) custom-call(f32[800]{0:T(1024)} %refs_0_.1, f32[200]{0:T(256)} %refs_1_.1, s32[2,8]{1,0:T(2,128)} %bitcast.9, ...), custom_call_target="tpu_custom_call" | custom-call | tf_op jit(solution)/shard_map/pallas_call | solution.py:266
  2.3 0.0 collective-permute-done
  2.3 0.1 collective-permute-start.2
  2.4 0.5 %collective-permute-start.5 = (bf16[8,80000]{1,0:T(8,128)(2,1)}, bf16[8,80000]{1,0:T(8,128)(2,1)S(1)}, u32[]{:S(2)}, u32[]{:S(2)}) collective-permute-start(bf16[8,80000]{1,0:T(8,128)(2,1)} %amps_hbm.1), channel_id=1, source_target_pairs={{0,1},{1,0},{2,3},{3,2},{4,5},{5,4},{6,7},{7,6},{8,9},{9,8},{10,11... | collective-permute-start | bytes 3840008 | tf_op jit(solution)/shard_map/ppermute | solution.py:189
  2.9 3.6 %collective-permute-start.1 = (bf16[2,8,16]{2,1,0:T(8,128)(2,1)S(1)}, bf16[2,8,16]{2,1,0:T(8,128)(2,1)S(1)}, u32[]{:S(2)}, u32[]{:S(2)}) collective-permute-start(bf16[2,8,16]{2,1,0:T(8,128)(2,1)S(1)} %get-tuple-element.34), channel_id=1, source_target_pairs={{0,6},{1,12},{2,4},{3,14},{4,2},{5,8},{6,0},{7,10},{8,5},{9,15},{1... | collective-permute-start | bytes 1544 | tf_op jit(solution)/shard_map/ppermute | solution.py:214
  6.5 0.0 collective-permute-start.3
  6.5 1.6 %collective-permute-done.1 = bf16[2,8,16]{2,1,0:T(8,128)(2,1)S(1)} collective-permute-done((bf16[2,8,16]{2,1,0:T(8,128)(2,1)S(1)}, bf16[2,8,16]{2,1,0:T(8,128)(2,1)S(1)}, u32[]{:S(2)}, u32[]{:S(2)}) %collective-permute-start.1) | collective-permute-done | bytes 544 | tf_op jit(solution)/shard_map/ppermute | solution.py:214
  8.1 2.5 %collective-permute-start.4 = (bf16[4,8,16]{2,1,0:T(8,128)(2,1)S(1)}, bf16[4,8,16]{2,1,0:T(8,128)(2,1)S(1)}, u32[]{:S(2)}, u32[]{:S(2)}) collective-permute-start(bf16[4,8,16]{2,1,0:T(8,128)(2,1)S(1)} %constant_dynamic-update-slice_fusion.2), channel_id=1, source_target_pairs={{0,8},{1,2},{2,10},{3,0},{4,12},{5,6},{6,14},{7,4},{8,11},{9,1},{1... | collective-permute-start | bytes 3080 | tf_op jit(solution)/shard_map/ppermute | solution.py:214
  10.6 0.0 collective-permute-done.2.refs_5_
  10.6 0.9 %shard_map.65 = (f32[8,16]{1,0:T(8,128)S(1)}, bf16[2,8,80000]{2,1,0:T(8,128)(2,1)S(1)}, f32[8,10240]{1,0:T(8,128)S(1)}, f32[8,128]{1,0:T(8,128)S(1)}) custom-call(bf16[8,80000]{1,0:T(8,128)(2,1)} %amps_hbm.1, bf16[8,80000]{1,0:T(8,128)(2,1)} %ints_hbm.1, ...), custom_call_target="tpu_custom_call", output_to_operand_aliasing={{1}: (5, {}), {2}: (6, {}), {3}: (7, {})} | custom-call | flops 20480000 | bytes 2560000 | tf_op jit(solution)/shard_map/pallas_call | solution.py:284
  11.5 0.0 collective-permute-done.3
  11.5 0.4 %collective-permute-done.4 = bf16[4,8,16]{2,1,0:T(8,128)(2,1)S(1)} collective-permute-done((bf16[4,8,16]{2,1,0:T(8,128)(2,1)S(1)}, bf16[4,8,16]{2,1,0:T(8,128)(2,1)S(1)}, u32[]{:S(2)}, u32[]{:S(2)}) %collective-permute-start.4) | collective-permute-done | bytes 1056 | tf_op jit(solution)/shard_map/ppermute | solution.py:214
  11.9 0.0 collective-permute-done.5.refs_3_
  11.9 1.7 %shard_map.66 = bf16[8,80000]{1,0:T(8,128)(2,1)} custom-call(f32[8,16]{1,0:T(8,128)S(1)} %get-tuple-element.28.chi_ref, f32[8,10240]{1,0:T(8,128)S(1)} %get-tuple-element.29.virtual_ref, f32[8,128]{1,0:T(8,128)S(1)} %get-tuple-element.30.occupied_ref, bf16[16,16]{1,0:T(8,128)(2,1)S(1)} %bitcast.8, bf16[32,16]{1,0:T(8,128)(2,1)S(1)} %bitcast.7, ...), custom_call_target="tpu_custom_call" | custom-call | flops 20480000 | bytes 5120000 | tf_op jit(solution)/shard_map/pallas_call | solution.py:301
  (3 shorter events, 0.0 us)
Async XLA Ops:
  0.0 2.3 %collective-permute-start = (bf16[1,8,16]{2,1,0:T(8,128)(2,1)}, bf16[1,8,16]{2,1,0:T(8,128)(2,1)S(1)}, u32[]{:S(2)}, u32[]{:S(2)}) collective-permute-start(bf16[1,8,16]{2,1,0:T(8,128)(2,1)} %refs_3_.1), channel_id=1, source_target_pairs={{0,1},{1,0},{2,3},{3,2},{4,5},{5,4},{6,7},{7,6},{8,9},{9,8},{10,11... | collective-permute-start | bytes 776 | tf_op jit(solution)/shard_map/ppermute | solution.py:214
  2.3 8.3 %collective-permute-start.2 = (bf16[8,80000]{1,0:T(8,128)(2,1)}, bf16[8,80000]{1,0:T(8,128)(2,1)S(1)}, u32[]{:S(2)}, u32[]{:S(2)}) collective-permute-start(bf16[8,80000]{1,0:T(8,128)(2,1)} %ints_hbm.1), channel_id=1, source_target_pairs={{0,1},{1,0},{2,3},{3,2},{4,5},{5,4},{6,7},{7,6},{8,9},{9,8},{10,11... | collective-permute-start | bytes 3840008 | tf_op jit(solution)/shard_map/ppermute | solution.py:189
  2.4 9.5 %collective-permute-start.5 = (bf16[8,80000]{1,0:T(8,128)(2,1)}, bf16[8,80000]{1,0:T(8,128)(2,1)S(1)}, u32[]{:S(2)}, u32[]{:S(2)}) collective-permute-start(bf16[8,80000]{1,0:T(8,128)(2,1)} %amps_hbm.1), channel_id=1, source_target_pairs={{0,1},{1,0},{2,3},{3,2},{4,5},{5,4},{6,7},{7,6},{8,9},{9,8},{10,11... | collective-permute-start | bytes 3840008 | tf_op jit(solution)/shard_map/ppermute | solution.py:189
  2.9 5.2 %collective-permute-start.1 = (bf16[2,8,16]{2,1,0:T(8,128)(2,1)S(1)}, bf16[2,8,16]{2,1,0:T(8,128)(2,1)S(1)}, u32[]{:S(2)}, u32[]{:S(2)}) collective-permute-start(bf16[2,8,16]{2,1,0:T(8,128)(2,1)S(1)} %get-tuple-element.34), channel_id=1, source_target_pairs={{0,6},{1,12},{2,4},{3,14},{4,2},{5,8},{6,0},{7,10},{8,5},{9,15},{1... | collective-permute-start | bytes 1544 | tf_op jit(solution)/shard_map/ppermute | solution.py:214
  6.5 5.0 %collective-permute-start.3 = (bf16[2,8,16]{2,1,0:T(8,128)(2,1)S(1)}, bf16[2,8,16]{2,1,0:T(8,128)(2,1)S(1)}, u32[]{:S(2)}, u32[]{:S(2)}) collective-permute-start(bf16[2,8,16]{2,1,0:T(8,128)(2,1)S(1)} %get-tuple-element.34), channel_id=1, source_target_pairs={{0,4},{1,10},{2,6},{3,8},{4,0},{5,14},{6,2},{7,12},{8,3},{9,13},{1... | collective-permute-start | bytes 1544 | tf_op jit(solution)/shard_map/ppermute | solution.py:214
  8.1 3.8 %collective-permute-start.4 = (bf16[4,8,16]{2,1,0:T(8,128)(2,1)S(1)}, bf16[4,8,16]{2,1,0:T(8,128)(2,1)S(1)}, u32[]{:S(2)}, u32[]{:S(2)}) collective-permute-start(bf16[4,8,16]{2,1,0:T(8,128)(2,1)S(1)} %constant_dynamic-update-slice_fusion.2), channel_id=1, source_target_pairs={{0,8},{1,2},{2,10},{3,0},{4,12},{5,6},{6,14},{7,4},{8,11},{9,1},{1... | collective-permute-start | bytes 3080 | tf_op jit(solution)/shard_map/ppermute | solution.py:214
